TPU v7x, 32 devices: a whole 2x2x4 slice. The times are simulated.
32 devices in a mesh: grp: 2 (over y), gr: 4 (over x, core), gc: 4 (over z).
Axes of the slice: x: 2, y: 2, z: 4, core: 2. Of those that a mesh axis runs over, the one named last changes fastest.
Arguments:
- activations: bfloat16 [256, 32, 4096], P(('grp', 'gr', 'gc')), parts along dimension 0, may hold values from -6 to 6
- out_grads: bfloat16 [256, 32, 4096], P(('grp', 'gr', 'gc')), parts along dimension 0, may hold values from -6 to 6
- proj_in: bfloat16 [4096, 64], replicated, may hold values from -0.09375 to 0.09375
- proj_out: bfloat16 [4096, 64], replicated, may hold values from -0.09375 to 0.09375
- inv_gram: bfloat16 [4096, 4096], P('gr', 'gc'), may hold values from -1 to 2, as said below
Outputs:
- kernel: float32 [256, 128], P(('grp', 'gr'), 'gc'), parts along dimension 0
There are 2 independent parts, one for each index of `grp`. A program takes and returns all parts, laid end to end along the dimension named above; an argument that names none is the same for every part. Nothing has to cross between parts.
Inputs may be any that keep to these rules, and one draw needn't show every extreme that they name: inv_gram is symmetric and positive definite.
All inputs are finite; a program needn't handle non-finite values.
Results may differ from a plain program's by a relative error of at most 0.0016.
Values may be sent and summed in bfloat16 or wider, within the bound.
No kernel may reach another device: no remote copies, remote signals or barrier semaphores. Data moves between devices by JAX's collectives and lax.ppermute only.
A program may use at most 64 MiB of HBM per device.

v0:
```python
import math

import jax
import jax.numpy as jnp
from jax import lax
from jax.sharding import Mesh, PartitionSpec as P

PLANE = ("chip", "gc")


def other_core(value):
    return lax.ppermute(value, "core", [(0, 1), (1, 0)])


def per_device(chips, cols, activations, out_grads, proj_in, proj_out, inv_gram):
    seqs, length, width = activations.shape
    rank = proj_in.shape[1]
    feat = rank * rank
    row_block, col_block = inv_gram.shape
    plane = chips * cols
    half = seqs * plane
    tall = half // chips
    core = lax.axis_index("core")

    inv_other = other_core(inv_gram)

    proj_act = jnp.dot(
        activations.reshape(seqs * length, width), proj_in, preferred_element_type=jnp.float32
    ).astype(jnp.bfloat16)
    proj_grad = jnp.dot(
        out_grads.reshape(seqs * length, width), proj_out, preferred_element_type=jnp.float32
    ).astype(jnp.bfloat16)
    proj_act = proj_act.reshape(seqs, length, rank)
    proj_grad = proj_grad.reshape(seqs, length, rank)
    summed = jnp.einsum(
        "sto,sti->soi", proj_grad, proj_act, preferred_element_type=jnp.float32
    ).reshape(seqs, feat)
    own_rows = (summed * (1.0 / math.sqrt(length))).astype(jnp.bfloat16)

    pieces = []
    for chip in range(chips):
        low = own_rows[:, 2 * chip * row_block : (2 * chip + 1) * row_block]
        high = own_rows[:, (2 * chip + 1) * row_block : (2 * chip + 2) * row_block]
        own, other = jnp.where(core == 0, low, high), jnp.where(core == 0, high, low)
        for col in range(cols):
            pieces.append(
                jnp.concatenate([own, other, own_rows[:, col * col_block : (col + 1) * col_block]], axis=1)
            )
    got = lax.all_to_all(jnp.stack(pieces), PLANE, 0, 0, tiled=True)
    got = got.reshape(half, 2 * row_block + col_block)

    mine = got[:, 2 * row_block :]
    theirs = other_core(mine)
    precond = jnp.dot(got[:, :row_block], inv_gram, preferred_element_type=jnp.float32)
    precond += jnp.dot(
        got[:, row_block : 2 * row_block], inv_other, preferred_element_type=jnp.float32
    )
    precond = precond.astype(jnp.bfloat16)
    mine = mine.reshape(chips, 1, tall, col_block)
    theirs = theirs.reshape(chips, 1, tall, col_block)
    right = jnp.where(
        core == 0,
        jnp.concatenate([mine, theirs], axis=1),
        jnp.concatenate([theirs, mine], axis=1),
    ).reshape(2 * half, col_block)
    terms = lax.dot_general(
        precond, right, (((1,), (1,)), ((), ())), preferred_element_type=jnp.float32
    ) * (8.0 / feat)

    wide = 2 * half // cols
    fold = max(1, 128 // wide)
    terms = terms.reshape(chips, fold, tall // fold, cols, wide).transpose(0, 3, 2, 1, 4)
    terms = terms.reshape(plane, tall // fold, fold * wide)
    total = jnp.sum(lax.all_to_all(terms, PLANE, 0, 0, tiled=True), axis=0)
    return jnp.concatenate([total[:, i * wide : (i + 1) * wide] for i in range(fold)])


def solution(mesh):
    grp, gr, gc = (mesh.shape[name] for name in ("grp", "gr", "gc"))
    split = Mesh(mesh.devices.reshape(grp, gr // 2, 2, gc), ("grp", "chip", "core", "gc"))
    rows = ("grp", "chip", "core", "gc")
    in_specs = (P(rows, None, None), P(rows, None, None), P(), P(), P(("chip", "core"), "gc"))
    out_specs = P(("grp", "chip", "core"), "gc")

    def fn(*args):
        return per_device(gr // 2, gc, *args)

    return jax.shard_map(fn, mesh=split, in_specs=in_specs, out_specs=out_specs, check_vma=False)
```

profile of v0, /device:TPU:0, one launch (start us, length us, event | category | flops | bytes accessed | tf_op | source)
XLA Modules:
  0.0 40.8 jit_solution(12651660831471376759)
XLA Ops:
  0.0 0.0 copy-start
  0.0 0.0 copy-start.1
  0.0 0.5 %collective-permute-start = (bf16[1024,1024]{1,0:T(8,128)(2,1)}, bf16[1024,1024]{1,0:T(8,128)(2,1)}, u32[]{:S(2)}, u32[]{:S(2)}) collective-permute-start(bf16[1024,1024]{1,0:T(8,128)(2,1)} %param.9), channel_id=1, source_target_pairs={{0,4},{4,0},{1,5},{5,1},{2,6},{6,2},{3,7},{7,3},{8,12},{12,8},{9,1... | collective-permute-start | bytes 6291464 | tf_op jit(solution)/shard_map/ppermute | solution.py:12
  0.5 1.1 %copy-done = bf16[8,32,4096]{2,1,0:T(8,128)(2,1)S(1)} copy-done((bf16[8,32,4096]{2,1,0:T(8,128)(2,1)S(1)}, bf16[8,32,4096]{2,1,0:T(8,128)(2,1)}, u32[]{:S(2)}) %copy-start) | copy-done | bytes 2097176
  1.6 1.8 %convolution_convert_fusion = bf16[256,64]{0,1:T(8,128)(2,1)S(1)} fusion(bf16[256,4096]{1,0:T(8,128)(2,1)S(1)} %bitcast.52, bf16[4096,64]{0,1:T(8,128)(2,1)} %param.7), kind=kOutput, calls=%fused_computation.5 | convolution fusion | flops 134234112 | bytes 2654208 | tf_op jit(solution)/shard_map/dot_general | solution.py:27
  3.4 0.1 copy.9
  3.5 0.0 copy-done.1
  3.5 2.4 %convolution_convert_fusion.1 = bf16[256,64]{0,1:T(8,128)(2,1)S(1)} fusion(bf16[256,4096]{1,0:T(8,128)(2,1)} %bitcast.53, bf16[4096,64]{0,1:T(8,128)(2,1)S(1)} %copy-done.1), kind=kOutput, calls=%fused_computation.6 | convolution fusion | flops 134234112 | bytes 2654208 | tf_op jit(solution)/shard_map/dot_general | solution.py:30
  5.9 0.1 copy.8
  6.0 0.2 fusion
  6.3 0.2 convert_element_type.18
  6.6 19.6 %all_to_all.10 = bf16[8,8,3072]{2,1,0:T(8,128)(2,1)S(1)} all-to-all(bf16[8,8,3072]{2,1,0:T(8,128)(2,1)S(1)} %fusion.11), channel_id=1, replica_groups=mesh['grp'=2,'chip'=2,'core'=2,'gc'=4] {'chip','gc'}, dimensions={0} | all-to-all | bytes 786432 | tf_op jit(solution)/shard_map/all_to_all | solution.py:49
  26.2 0.1 collective-permute-start.1
  26.3 2.1 %fusion.6 = f32[64,1024]{1,0:T(8,128)S(1)} fusion(bf16[1024,1024]{1,0:T(8,128)(2,1)} %param.9, bf16[64,3072]{1,0:T(8,128)(2,1)S(1)} %bitcast.55), kind=kOutput, calls=%fused_computation.10 | convolution fusion | flops 134217728 | bytes 2490368 | tf_op jit(solution)/shard_map/dot_general | solution.py:54
  28.4 0.0 collective-permute-done.1
  28.4 0.0 collective-permute-done
  28.4 2.3 %fusion.3 = f32[64,128]{1,0:T(8,128)S(1)} fusion(bf16[128,1024]{1,0:T(8,128)(2,1)S(1)} %bitcast.57, f32[64,1024]{1,0:T(8,128)S(1)} %fusion.6, bf16[1024,1024]{1,0:T(8,128)(2,1)} %collective-permute-done, bf16[64,3072]{1,0:T(8,128)(2,1)S(1)} %bitcast.56), kind=kOutput, calls=%fused_computation.7 | convolution fusion | flops 151134208 | bytes 2785280 | tf_op jit(solution)/shard_map/dot_general | solution.py:66
  30.7 0.1 reshape.43
  30.8 0.1 copy.12
  30.9 0.1 reshape.44
  31.0 9.1 %all_to_all.11 = f32[8,8,128]{2,1,0:T(8,128)S(1)} all-to-all(f32[8,8,128]{2,1,0:T(8,128)S(1)} %reshape.44), channel_id=1, replica_groups=mesh['grp'=2,'chip'=2,'core'=2,'gc'=4] {'chip','gc'}, dimensions={0} | all-to-all | bytes 65536 | tf_op jit(solution)/shard_map/all_to_all | solution.py:74
  40.1 0.1 fusion.24
  40.2 0.6 %pad_maximum_fusion.10 = f32[32,32]{1,0:T(8,128)} fusion(f32[8,32]{1,0:T(8,128)S(1)} %get-tuple-element.14, f32[8,32]{1,0:T(8,128)S(1)} %get-tuple-element.15, f32[8,32]{1,0:T(8,128)S(1)} %get-tuple-element.16, f32[8,32]{1,0:T(8,128)S(1)} %get-tuple-element.13), kind=kLoop, calls=%fused_computation.39 | loop fusion | flops 3072 | bytes 8192 | tf_op jit(solution)/shard_map/concatenate | solution.py:75
  (12 shorter events, 0.1 us)
Async XLA Ops:
  0.0 1.6 %copy-start = (bf16[8,32,4096]{2,1,0:T(8,128)(2,1)S(1)}, bf16[8,32,4096]{2,1,0:T(8,128)(2,1)}, u32[]{:S(2)}) copy-start(bf16[8,32,4096]{2,1,0:T(8,128)(2,1)} %param.5) | copy-start | bytes 6291460
  0.0 3.5 %copy-start.1 = (bf16[4096,64]{0,1:T(8,128)(2,1)S(1)}, bf16[4096,64]{0,1:T(8,128)(2,1)}, u32[]{:S(2)}) copy-start(bf16[4096,64]{0,1:T(8,128)(2,1)} %param.8) | copy-start | bytes 1572868
  0.0 28.4 %collective-permute-start = (bf16[1024,1024]{1,0:T(8,128)(2,1)}, bf16[1024,1024]{1,0:T(8,128)(2,1)}, u32[]{:S(2)}, u32[]{:S(2)}) collective-permute-start(bf16[1024,1024]{1,0:T(8,128)(2,1)} %param.9), channel_id=1, source_target_pairs={{0,4},{4,0},{1,5},{5,1},{2,6},{6,2},{3,7},{7,3},{8,12},{12,8},{9,1... | collective-permute-start | bytes 6291464 | tf_op jit(solution)/shard_map/ppermute | solution.py:12
  26.2 2.2 %collective-permute-start.1 = (bf16[64,1024]{1,0:T(8,128)(2,1)S(1)}, bf16[64,1024]{1,0:T(8,128)(2,1)S(1)}, u32[]{:S(2)}, u32[]{:S(2)}) collective-permute-start(bf16[64,1024]{1,0:T(8,128)(2,1)S(1)} %slice.58), channel_id=1, source_target_pairs={{0,4},{4,0},{1,5},{5,1},{2,6},{6,2},{3,7},{7,3},{8,12},{12,8},{9,1... | collective-permute-start | bytes 393224 | tf_op jit(solution)/shard_map/ppermute | solution.py:12
where the time goes:
time: 41.2 us; the launch traced here: 40.8 us
  blocking collectives  28.7 us (70%)
  matrix products  8.72 us (21%)
  local copies, waits for them, and re-layouts  1.96 us (5%)
  other arithmetic  0.71 us (2%)
  starting transfers between devices  0.52 us (1%)
    all_to_all x1, blocking collectives, per_device(): got = lax.all_to_all(jnp.stack(pieces), PLANE, 0, 0, tiled=True)  19.6 us
    all_to_all x1, blocking collectives, per_device(): total = jnp.sum(lax.all_to_all(terms, PLANE, 0, 0, tiled=True), axis=0)  9.11 us
    dot_general x1, matrix products, per_device(): jnp.dot(out_grads.reshape(seqs * length, width), proj_out, preferred_elem...  2.35 us
    dot_general x1, matrix products, per_device(): lax.dot_general(precond, right, (((1,), (1,)), ((), ())), preferred_eleme...  2.26 us
    dot_general x1, matrix products, per_device(): jnp.dot(got[:, :row_block], inv_gram, preferred_element_type=jnp.float32)  2.07 us
    dot_general x1, matrix products, per_device(): jnp.dot(activations.reshape(seqs * length, width), proj_in, preferred_ele...  1.8 us
    unnamed x4, local copies, waits for them, and re-layouts  1.14 us
  transfers between devices with their start and end apart: 2, of which 0 were waited for; matrix products, arithmetic and copies ran while one was open for 17% of the time, Pallas kernels for 0%

commit v1 on v0

--- a/solution.py
+++ b/solution.py
@@ -41,20 +41,25 @@
     for chip in range(chips):
         low = own_rows[:, 2 * chip * row_block : (2 * chip + 1) * row_block]
         high = own_rows[:, (2 * chip + 1) * row_block : (2 * chip + 2) * row_block]
-        own, other = jnp.where(core == 0, low, high), jnp.where(core == 0, high, low)
-        for col in range(cols):
-            pieces.append(
-                jnp.concatenate([own, other, own_rows[:, col * col_block : (col + 1) * col_block]], axis=1)
-            )
-    got = lax.all_to_all(jnp.stack(pieces), PLANE, 0, 0, tiled=True)
-    got = got.reshape(half, 2 * row_block + col_block)
+        piece = jnp.where(
+            core == 0, jnp.concatenate([low, high], axis=1), jnp.concatenate([high, low], axis=1)
+        )
+        pieces.extend([piece] * cols)
+    got = lax.all_to_all(jnp.stack(pieces), PLANE, 0, 0, tiled=True).reshape(half, 2 * row_block)
+    own, other = got[:, :row_block], got[:, row_block:]
 
-    mine = got[:, 2 * row_block :]
+    col = lax.axis_index("gc")
+    held = jnp.where(col % 2 == core, own, other)
+    own_terms = jnp.dot(own, inv_gram, preferred_element_type=jnp.float32)
+    mine = held
+    for step in range(1, chips):
+        pairs = [
+            (z // 2 * cols + z, (z // 2 + step) % chips * cols + z) for z in range(cols)
+        ]
+        moved, own_terms = lax.optimization_barrier((lax.ppermute(held, PLANE, pairs), own_terms))
+        mine = jnp.where(lax.axis_index("chip") == (col // 2 + step) % chips, moved, mine)
     theirs = other_core(mine)
-    precond = jnp.dot(got[:, :row_block], inv_gram, preferred_element_type=jnp.float32)
-    precond += jnp.dot(
-        got[:, row_block : 2 * row_block], inv_other, preferred_element_type=jnp.float32
-    )
+    precond = own_terms + jnp.dot(other, inv_other, preferred_element_type=jnp.float32)
     precond = precond.astype(jnp.bfloat16)
     mine = mine.reshape(chips, 1, tall, col_block)
     theirs = theirs.reshape(chips, 1, tall, col_block)

time: 41.2 us -> 48.9 us (1.19)
  blocking collectives: 28.7 us -> 10.2 us
  waiting for transfers between devices: 0.01 us -> 11.5 us
  starting transfers between devices: 0.52 us -> 10.2 us
  local copies, waits for them, and re-layouts: 1.96 us -> 5.64 us
  other arithmetic: 0.71 us -> 1.93 us
    all_to_all x1 -> x0, blocking collectives: 19.6 us -> none  [per_device(): got = lax.all_to_all(jnp.stack(pieces), PLANE, 0, 0, tiled=True)]
    all_to_all x0 -> x1, waiting for transfers between devices: none -> 9.78 us  [per_device(): lax.all_to_all(jnp.stack(pieces), PLANE, 0, 0, tiled=True)]
    all_to_all x0 -> x1, starting transfers between devices: none -> 7.25 us  [per_device(): lax.all_to_all(jnp.stack(pieces), PLANE, 0, 0, tiled=True)]
    unnamed x4 -> x9, local copies, waits for them, and re-layouts: 1.14 us -> 4.21 us
    ppermute x0 -> x1, starting transfers between devices: none -> 2.47 us  [per_device(): lax.ppermute(held, PLANE, pairs)]
    ppermute x2, waiting for transfers between devices: 0.01 us -> 1.34 us  [other_core(): return lax.ppermute(value, 'core', [(0, 1), (1, 0)])]
    unnamed x7 -> x2, other arithmetic: 0.04 us -> 1.24 us
    all_to_all x1, blocking collectives: 9.11 us -> 10.2 us  [per_device(): total = jnp.sum(lax.all_to_all(terms, PLANE, 0, 0, tiled=True), axis=0)]
  transfers between devices with their start and end apart: 2 -> 4, of which waited for: 0 -> 3; matrix products, arithmetic and copies ran while one was open for 17% -> 25% of each run, Pallas kernels for 0% -> 0%
where the time goes in v1:
time: 48.9 us; the launch traced here: 48.4 us
  waiting for transfers between devices  11.5 us (24%)
  starting transfers between devices  10.2 us (21%)
  blocking collectives  10.2 us (21%)
  matrix products  8.72 us (18%)
  local copies, waits for them, and re-layouts  5.64 us (12%)
  other arithmetic  1.93 us (4%)
    all_to_all x1, blocking collectives, per_device(): total = jnp.sum(lax.all_to_all(terms, PLANE, 0, 0, tiled=True), axis=0)  10.2 us
    all_to_all x1, waiting for transfers between devices, per_device(): lax.all_to_all(jnp.stack(pieces), PLANE, 0, 0, tiled=True)  9.78 us
    all_to_all x1, starting transfers between devices, per_device(): lax.all_to_all(jnp.stack(pieces), PLANE, 0, 0, tiled=True)  7.25 us
    unnamed x9, local copies, waits for them, and re-layouts  4.21 us
    ppermute x1, starting transfers between devices, per_device(): lax.ppermute(held, PLANE, pairs)  2.47 us
    dot_general x1, matrix products, per_device(): jnp.dot(out_grads.reshape(seqs * length, width), proj_out, preferred_elem...  2.35 us
    dot_general x1, matrix products, per_device(): lax.dot_general(precond, right, (((1,), (1,)), ((), ())), preferred_eleme...  2.26 us
    dot_general x1, matrix products, per_device(): own_terms = jnp.dot(own, inv_gram, preferred_element_type=jnp.float32)  2.07 us
  transfers between devices with their start and end apart: 4, of which 3 were waited for; matrix products, arithmetic and copies ran while one was open for 25% of the time, Pallas kernels for 0%

profile of v1, /device:TPU:0, one launch (start us, length us, event | category | flops | bytes accessed | tf_op | source)
XLA Modules:
  0.0 48.4 jit_solution(13695330094920647790)
XLA Ops:
  0.0 0.0 copy-start
  0.0 0.0 copy-start.1
  0.0 0.5 collective-permute-start.1
  0.5 1.1 %copy-done = bf16[8,32,4096]{2,1,0:T(8,128)(2,1)S(1)} copy-done((bf16[8,32,4096]{2,1,0:T(8,128)(2,1)S(1)}, bf16[8,32,4096]{2,1,0:T(8,128)(2,1)}, u32[]{:S(2)}) %copy-start) | copy-done | bytes 2097176
  1.6 1.8 %convolution_convert_fusion = bf16[256,64]{0,1:T(8,128)(2,1)S(1)} fusion(bf16[256,4096]{1,0:T(8,128)(2,1)S(1)} %bitcast.26, bf16[4096,64]{0,1:T(8,128)(2,1)} %param.7), kind=kOutput, calls=%fused_computation.2 | convolution fusion | flops 134234112 | bytes 2654208 | tf_op jit(solution)/shard_map/dot_general | solution.py:27
  3.4 0.1 copy.9
  3.5 0.0 copy-done.1
  3.5 2.4 %convolution_convert_fusion.1 = bf16[256,64]{0,1:T(8,128)(2,1)S(1)} fusion(bf16[256,4096]{1,0:T(8,128)(2,1)} %bitcast.31, bf16[4096,64]{0,1:T(8,128)(2,1)S(1)} %copy-done.1), kind=kOutput, calls=%fused_computation.3 | convolution fusion | flops 134234112 | bytes 2654208 | tf_op jit(solution)/shard_map/dot_general | solution.py:30
  5.9 0.1 copy.8
  6.0 0.2 fusion
  6.3 0.2 convert_element_type.18
  6.5 0.6 %constant_dynamic-update-slice_fusion.7 = (bf16[8,8,2048]{2,1,0:T(8,128)(2,1)}, bf16[1,8,2048]{2,1,0:T(8,128)(2,1)S(1)}) fusion(bf16[8,1024]{1,0:T(8,128)(2,1)S(1)} %get-tuple-element.15, bf16[8,1024]{1,0:T(8,128)(2,1)S(1)} %get-tuple-element.16, bf16[8,4096]{1,0:T(8,128)(2,1)S(1)} %convert_element_type.18, pred[]{:T(512)S(6)} %eq.15), kind=kLoop, calls=%fused_computation.25 | loop fusion | flops 81919 | bytes 131073
  7.1 0.6 %constant_dynamic-update-slice_fusion.6 = bf16[8,8,2048]{2,1,0:T(8,128)(2,1)} fusion(bf16[8,8,2048]{2,1,0:T(8,128)(2,1)} %get-tuple-element.11, bf16[1,8,2048]{2,1,0:T(8,128)(2,1)S(1)} %get-tuple-element.12), kind=kLoop, calls=%fused_computation.24 | loop fusion | bytes 65536
  7.7 0.6 %constant_dynamic-update-slice_fusion.5 = bf16[8,8,2048]{2,1,0:T(8,128)(2,1)} fusion(bf16[8,8,2048]{2,1,0:T(8,128)(2,1)} %constant_dynamic-update-slice_fusion.6, bf16[1,8,2048]{2,1,0:T(8,128)(2,1)S(1)} %get-tuple-element.12), kind=kLoop, calls=%fused_computation.23 | loop fusion | bytes 65536
  8.3 0.6 %constant_dynamic-update-slice_fusion.4 = bf16[8,8,2048]{2,1,0:T(8,128)(2,1)} fusion(bf16[8,8,2048]{2,1,0:T(8,128)(2,1)} %constant_dynamic-update-slice_fusion.5, bf16[1,8,2048]{2,1,0:T(8,128)(2,1)S(1)} %get-tuple-element.12), kind=kLoop, calls=%fused_computation.22 | loop fusion | bytes 65536
  8.9 0.6 %constant_dynamic-update-slice_fusion.3 = (bf16[8,8,2048]{2,1,0:T(8,128)(2,1)}, bf16[1,8,2048]{2,1,0:T(8,128)(2,1)S(1)}) fusion(bf16[8,8,2048]{2,1,0:T(8,128)(2,1)} %constant_dynamic-update-slice_fusion.4, bf16[8,1024]{1,0:T(8,128)(2,1)S(1)} %get-tuple-element.14, bf16[8,1024]{1,0:T(8,128)(2,1)S(1)} %get-tuple-element.13, ...), kind=kLoop, calls=%fused_computation.21 | loop fusion | flops 81920 | bytes 131073
  9.5 0.6 %constant_dynamic-update-slice_fusion.2 = bf16[8,8,2048]{2,1,0:T(8,128)(2,1)} fusion(bf16[8,8,2048]{2,1,0:T(8,128)(2,1)} %get-tuple-element.9, bf16[1,8,2048]{2,1,0:T(8,128)(2,1)S(1)} %get-tuple-element.10), kind=kLoop, calls=%fused_computation.20 | loop fusion | bytes 65536
  10.1 0.6 %constant_dynamic-update-slice_fusion.1 = bf16[8,8,2048]{2,1,0:T(8,128)(2,1)} fusion(bf16[8,8,2048]{2,1,0:T(8,128)(2,1)} %constant_dynamic-update-slice_fusion.2, bf16[1,8,2048]{2,1,0:T(8,128)(2,1)S(1)} %get-tuple-element.10), kind=kLoop, calls=%fused_computation.19 | loop fusion | bytes 65536
  10.8 0.6 %constant_dynamic-update-slice_fusion = bf16[8,8,2048]{2,1,0:T(8,128)(2,1)} fusion(bf16[8,8,2048]{2,1,0:T(8,128)(2,1)} %constant_dynamic-update-slice_fusion.1, bf16[1,8,2048]{2,1,0:T(8,128)(2,1)S(1)} %get-tuple-element.10), kind=kLoop, calls=%fused_computation.18 | loop fusion | bytes 65536 | tf_op jit(solution)/shard_map/stack | solution.py:48
  11.4 7.3 %all-to-all-start = ((bf16[8,8,2048]{2,1,0:T(8,128)(2,1)}), bf16[8,8,2048]{2,1,0:T(8,128)(2,1)S(1)}, u32[]{:S(2)}, u32[]{:S(2)}) async-start(bf16[8,8,2048]{2,1,0:T(8,128)(2,1)} %constant_dynamic-update-slice_fusion), calls=%async_computation | async-start | bytes 524288 | tf_op jit(solution)/shard_map/all_to_all | solution.py:48
  18.6 9.8 %all-to-all-done = bf16[8,8,2048]{2,1,0:T(8,128)(2,1)S(1)} async-done(((bf16[8,8,2048]{2,1,0:T(8,128)(2,1)}), bf16[8,8,2048]{2,1,0:T(8,128)(2,1)S(1)}, u32[]{:S(2)}, u32[]{:S(2)}) %all-to-all-start) | async-done | bytes 262176 | tf_op jit(solution)/shard_map/all_to_all | solution.py:48
  28.4 2.5 %collective-permute-start = (bf16[64,1024]{1,0:T(8,128)(2,1)S(1)}, bf16[64,1024]{1,0:T(8,128)(2,1)S(1)}, u32[]{:S(2)}, u32[]{:S(2)}) collective-permute-start(bf16[64,1024]{1,0:T(8,128)(2,1)S(1)} %broadcast_select_fusion.1), channel_id=1, source_target_pairs={{0,8},{1,9},{10,2},{11,3},{4,12},{5,13},{14,6},{15,7},{16,24},{17,... | collective-permute-start | bytes 393224 | tf_op jit(solution)/shard_map/ppermute | solution.py:59
  30.9 2.1 %fusion.7 = f32[64,1024]{1,0:T(8,128)S(1)} fusion(bf16[1024,1024]{1,0:T(8,128)(2,1)} %param.9, bf16[64,2048]{1,0:T(8,128)(2,1)S(1)} %bitcast.28), kind=kOutput, calls=%fused_computation.12 | convolution fusion | flops 134217728 | bytes 2490368 | tf_op jit(solution)/shard_map/dot_general | solution.py:53
  33.0 0.4 collective-permute-done
  33.4 0.1 collective-permute-start.2
  33.5 1.3 %collective-permute-done.2 = bf16[64,1024]{1,0:T(8,128)(2,1)S(1)} collective-permute-done((bf16[64,1024]{1,0:T(8,128)(2,1)S(1)}, bf16[64,1024]{1,0:T(8,128)(2,1)S(1)}, u32[]{:S(2)}, u32[]{:S(2)}) %collective-permute-start.2) | collective-permute-done | bytes 131104 | tf_op jit(solution)/shard_map/ppermute | solution.py:12
  34.9 0.0 collective-permute-done.1
  34.9 2.3 %convolution_multiply_fusion.1 = f32[64,128]{1,0:T(8,128)S(1)} fusion(bf16[128,1024]{1,0:T(8,128)(2,1)S(1)} %bitcast.32, f32[64,1024]{1,0:T(8,128)S(1)} %fusion.7, bf16[1024,1024]{1,0:T(8,128)(2,1)} %collective-permute-done.1, bf16[64,2048]{1,0:T(8,128)(2,1)S(1)} %bitcast.30), kind=kOutput, calls=%fused_computation.4 | convolution fusion | flops 151134208 | bytes 2785280 | tf_op jit(solution)/shard_map/dot_general | solution.py:71
  37.2 0.1 reshape.43
  37.3 0.1 copy.12
  37.4 0.1 reshape.44
  37.5 10.2 %all_to_all.10 = f32[8,8,128]{2,1,0:T(8,128)S(1)} all-to-all(f32[8,8,128]{2,1,0:T(8,128)S(1)} %reshape.44), channel_id=1, replica_groups=mesh['grp'=2,'chip'=2,'core'=2,'gc'=4] {'chip','gc'}, dimensions={0} | all-to-all | bytes 65536 | tf_op jit(solution)/shard_map/all_to_all | solution.py:79
  47.8 0.1 fusion.14
  47.8 0.6 %pad_maximum_fusion = f32[32,32]{1,0:T(8,128)} fusion(f32[8,32]{1,0:T(8,128)S(1)} %get-tuple-element.18, f32[8,32]{1,0:T(8,128)S(1)} %get-tuple-element.19, f32[8,32]{1,0:T(8,128)S(1)} %get-tuple-element.20, f32[8,32]{1,0:T(8,128)S(1)} %get-tuple-element.17), kind=kLoop, calls=%fused_computation.26 | loop fusion | flops 3072 | bytes 8192 | tf_op jit(solution)/shard_map/concatenate | solution.py:80
  (5 shorter events, 0.1 us)
Async XLA Ops:
  0.0 1.6 %copy-start = (bf16[8,32,4096]{2,1,0:T(8,128)(2,1)S(1)}, bf16[8,32,4096]{2,1,0:T(8,128)(2,1)}, u32[]{:S(2)}) copy-start(bf16[8,32,4096]{2,1,0:T(8,128)(2,1)} %param.5) | copy-start | bytes 6291460
  0.0 3.5 %copy-start.1 = (bf16[4096,64]{0,1:T(8,128)(2,1)S(1)}, bf16[4096,64]{0,1:T(8,128)(2,1)}, u32[]{:S(2)}) copy-start(bf16[4096,64]{0,1:T(8,128)(2,1)} %param.8) | copy-start | bytes 1572868
  0.0 34.9 %collective-permute-start.1 = (bf16[1024,1024]{1,0:T(8,128)(2,1)}, bf16[1024,1024]{1,0:T(8,128)(2,1)}, u32[]{:S(2)}, u32[]{:S(2)}) collective-permute-start(bf16[1024,1024]{1,0:T(8,128)(2,1)} %param.9), channel_id=1, source_target_pairs={{0,4},{4,0},{1,5},{5,1},{2,6},{6,2},{3,7},{7,3},{8,12},{12,8},{9,1... | collective-permute-start | bytes 6291464 | tf_op jit(solution)/shard_map/ppermute | solution.py:12
  11.4 17.0 %all-to-all-start = ((bf16[8,8,2048]{2,1,0:T(8,128)(2,1)}), bf16[8,8,2048]{2,1,0:T(8,128)(2,1)S(1)}, u32[]{:S(2)}, u32[]{:S(2)}) async-start(bf16[8,8,2048]{2,1,0:T(8,128)(2,1)} %constant_dynamic-update-slice_fusion), calls=%async_computation | async-start | bytes 524288 | tf_op jit(solution)/shard_map/all_to_all | solution.py:48
  28.4 5.0 %collective-permute-start = (bf16[64,1024]{1,0:T(8,128)(2,1)S(1)}, bf16[64,1024]{1,0:T(8,128)(2,1)S(1)}, u32[]{:S(2)}, u32[]{:S(2)}) collective-permute-start(bf16[64,1024]{1,0:T(8,128)(2,1)S(1)} %broadcast_select_fusion.1), channel_id=1, source_target_pairs={{0,8},{1,9},{10,2},{11,3},{4,12},{5,13},{14,6},{15,7},{16,24},{17,... | collective-permute-start | bytes 393224 | tf_op jit(solution)/shard_map/ppermute | solution.py:59
  33.4 1.4 %collective-permute-start.2 = (bf16[64,1024]{1,0:T(8,128)(2,1)S(1)}, bf16[64,1024]{1,0:T(8,128)(2,1)S(1)}, u32[]{:S(2)}, u32[]{:S(2)}) collective-permute-start(bf16[64,1024]{1,0:T(8,128)(2,1)S(1)} %broadcast_select_fusion), channel_id=1, source_target_pairs={{0,4},{4,0},{1,5},{5,1},{2,6},{6,2},{3,7},{7,3},{8,12},{12,8},{9,1... | collective-permute-start | bytes 393224 | tf_op jit(solution)/shard_map/ppermute | solution.py:12

commit v2 on v0

--- a/solution.py
+++ b/solution.py
@@ -1,15 +1,124 @@
+import functools
 import math
 
 import jax
 import jax.numpy as jnp
 from jax import lax
+from jax.experimental import pallas as pl
+from jax.experimental.pallas import tpu as pltpu
 from jax.sharding import Mesh, PartitionSpec as P
 
 PLANE = ("chip", "gc")
+CHUNK = 64
+VMEM = pl.BlockSpec(memory_space=pltpu.VMEM)
+HBM = pl.BlockSpec(memory_space=pl.ANY)
+NT = (((1,), (1,)), ((), ()))
 
 
 def other_core(value):
     return lax.ppermute(value, "core", [(0, 1), (1, 0)])
+
+
+def project_kernel(act, grad, w_in, w_out, pa, pg, act_v, grad_v, in_v, out_v, w_sem, x_sem):
+    rows = act.shape[0]
+    steps = rows // CHUNK
+    weights = [
+        pltpu.make_async_copy(w_in, in_v, w_sem.at[0]),
+        pltpu.make_async_copy(w_out, out_v, w_sem.at[1]),
+    ]
+    copies = []
+    for side, (src, dst) in enumerate(((act, act_v), (grad, grad_v))):
+        weights[side].start()
+        for step in range(steps):
+            part = pl.ds(step * CHUNK, CHUNK)
+            copies.append(
+                pltpu.make_async_copy(src.at[part], dst.at[part], x_sem.at[side * steps + step])
+            )
+            copies[-1].start()
+    for side, (held, weight, out) in enumerate(((act_v, in_v, pa), (grad_v, out_v, pg))):
+        weights[side].wait()
+        for step in range(steps):
+            part = pl.ds(step * CHUNK, CHUNK)
+            copies[side * steps + step].wait()
+            out[part, :] = lax.dot_general(
+                held[part, :], weight[...], NT, preferred_element_type=jnp.float32
+            ).astype(out.dtype)
+
+
+def project(act, grad, w_in, w_out):
+    rows, width = act.shape
+    rank = w_in.shape[0]
+    kind = act.dtype
+    return pl.pallas_call(
+        project_kernel,
+        out_shape=[jax.ShapeDtypeStruct((rows, rank), kind)] * 2,
+        in_specs=[HBM] * 4,
+        out_specs=[VMEM] * 2,
+        scratch_shapes=[
+            pltpu.VMEM((rows, width), kind),
+            pltpu.VMEM((rows, width), kind),
+            pltpu.VMEM((rank, width), kind),
+            pltpu.VMEM((rank, width), kind),
+            pltpu.SemaphoreType.DMA((2,)),
+            pltpu.SemaphoreType.DMA((2 * rows // CHUNK,)),
+        ],
+        compiler_params=pltpu.CompilerParams(vmem_limit_bytes=58 * 2**20),
+        cost_estimate=pl.CostEstimate(
+            flops=4 * rows * width * rank, bytes_accessed=4 * (rows + rank) * width, transcendentals=0
+        ),
+        name="project",
+    )(act, grad, w_in, w_out)
+
+
+def precond_kernel(block, got, own, other, out):
+    total = jnp.dot(got[:, :block], own[...], preferred_element_type=jnp.float32)
+    total += jnp.dot(got[:, block : 2 * block], other[...], preferred_element_type=jnp.float32)
+    out[...] = total.astype(out.dtype)
+
+
+def precondition(got, own, other):
+    rows = got.shape[0]
+    block, width = own.shape
+    return pl.pallas_call(
+        functools.partial(precond_kernel, block),
+        out_shape=jax.ShapeDtypeStruct((rows, width), got.dtype),
+        in_specs=[VMEM] * 3,
+        out_specs=VMEM,
+        compiler_params=pltpu.CompilerParams(vmem_limit_bytes=16 * 2**20),
+        cost_estimate=pl.CostEstimate(
+            flops=4 * rows * block * width, bytes_accessed=4 * block * width, transcendentals=0
+        ),
+        name="precondition",
+    )(got, own, other)
+
+
+def terms_kernel(chips, cols, fold, scale, precond, right, out):
+    terms = lax.dot_general(precond[...], right[...], NT, preferred_element_type=jnp.float32) * scale
+    tall, wide = terms.shape[0] // chips, terms.shape[1] // cols
+    step = tall // fold
+    for chip in range(chips):
+        for col in range(cols):
+            lanes = terms[chip * tall : (chip + 1) * tall, col * wide : (col + 1) * wide]
+            out[chip * cols + col] = jnp.concatenate(
+                [lanes[i * step : (i + 1) * step] for i in range(fold)], axis=1
+            )
+
+
+def kernel_terms(chips, cols, fold, scale, precond, right):
+    rows, width = precond.shape
+    other = right.shape[0]
+    tall, wide = rows // chips, other // cols
+    return pl.pallas_call(
+        functools.partial(terms_kernel, chips, cols, fold, scale),
+        out_shape=jax.ShapeDtypeStruct((chips * cols, tall // fold, fold * wide), jnp.float32),
+        in_specs=[VMEM] * 2,
+        out_specs=VMEM,
+        compiler_params=pltpu.CompilerParams(vmem_limit_bytes=32 * 2**20),
+        cost_estimate=pl.CostEstimate(
+            flops=2 * rows * other * width, bytes_accessed=4 * rows * other, transcendentals=0
+        ),
+        name="kernel_terms",
+    )(precond, right)
 
 
 def per_device(chips, cols, activations, out_grads, proj_in, proj_out, inv_gram):
@@ -24,12 +133,12 @@
 
     inv_other = other_core(inv_gram)
 
-    proj_act = jnp.dot(
-        activations.reshape(seqs * length, width), proj_in, preferred_element_type=jnp.float32
-    ).astype(jnp.bfloat16)
-    proj_grad = jnp.dot(
-        out_grads.reshape(seqs * length, width), proj_out, preferred_element_type=jnp.float32
-    ).astype(jnp.bfloat16)
+    proj_act, proj_grad = project(
+        activations.reshape(seqs * length, width),
+        out_grads.reshape(seqs * length, width),
+        proj_in.T,
+        proj_out.T,
+    )
     proj_act = proj_act.reshape(seqs, length, rank)
     proj_grad = proj_grad.reshape(seqs, length, rank)
     summed = jnp.einsum(
@@ -51,11 +160,7 @@
 
     mine = got[:, 2 * row_block :]
     theirs = other_core(mine)
-    precond = jnp.dot(got[:, :row_block], inv_gram, preferred_element_type=jnp.float32)
-    precond += jnp.dot(
-        got[:, row_block : 2 * row_block], inv_other, preferred_element_type=jnp.float32
-    )
-    precond = precond.astype(jnp.bfloat16)
+    theirs, precond = lax.optimization_barrier((theirs, precondition(got, inv_gram, inv_other)))
     mine = mine.reshape(chips, 1, tall, col_block)
     theirs = theirs.reshape(chips, 1, tall, col_block)
     right = jnp.where(
@@ -63,14 +168,10 @@
         jnp.concatenate([mine, theirs], axis=1),
         jnp.concatenate([theirs, mine], axis=1),
     ).reshape(2 * half, col_block)
-    terms = lax.dot_general(
-        precond, right, (((1,), (1,)), ((), ())), preferred_element_type=jnp.float32
-    ) * (8.0 / feat)
 
     wide = 2 * half // cols
     fold = max(1, 128 // wide)
-    terms = terms.reshape(chips, fold, tall // fold, cols, wide).transpose(0, 3, 2, 1, 4)
-    terms = terms.reshape(plane, tall // fold, fold * wide)
+    terms = kernel_terms(chips, cols, fold, 8.0 / feat, precond, right)
     total = jnp.sum(lax.all_to_all(terms, PLANE, 0, 0, tiled=True), axis=0)
     return jnp.concatenate([total[:, i * wide : (i + 1) * wide] for i in range(fold)])
 

time: 41.2 us -> 40.8 us (level)
  Pallas kernels: 0 us -> 8.63 us
  matrix products: 8.72 us -> 1.25 us
  local copies, waits for them, and re-layouts: 1.96 us -> 0.27 us
    pallas_call x0 -> x3, Pallas kernels: none -> 8.63 us  [the longest x1 5.92 us: project(): pl.pallas_call(project_kernel, out_shape=[jax.ShapeDtypeStruct((rows, ran...]
    dot_general x4 -> x0, matrix products: 8.48 us -> none  [the longest x1 2.35 us: per_device(): jnp.dot(out_grads.reshape(seqs * length, width), proj_out, preferred_elem...]
    unnamed x4 -> x2, local copies, waits for them, and re-layouts: 1.14 us -> 0.01 us
    dot_general x1, matrix products: 0.24 us -> 1.25 us  [per_device(): jnp.einsum('sto,sti->soi', proj_grad, proj_act, preferred_element_type=jn...]
  transfers between devices with their start and end apart: 2 -> 2, of which waited for: 0 -> 0; matrix products, arithmetic and copies ran while one was open for 17% -> 4% of each run, Pallas kernels for 0% -> 21%
where the time goes in v2:
time: 40.8 us; the launch traced here: 40.5 us
  blocking collectives  29 us (71%)
  Pallas kernels  8.63 us (21%)
  matrix products  1.25 us (3%)
  other arithmetic  0.72 us (2%)
  starting transfers between devices  0.52 us (1%)
    all_to_all x1, blocking collectives, per_device(): got = lax.all_to_all(jnp.stack(pieces), PLANE, 0, 0, tiled=True)  19.9 us
    all_to_all x1, blocking collectives, per_device(): total = jnp.sum(lax.all_to_all(terms, PLANE, 0, 0, tiled=True), axis=0)  9.11 us
    pallas_call x1, Pallas kernels, project(): pl.pallas_call(project_kernel, out_shape=[jax.ShapeDtypeStruct((rows, ran...  5.92 us
    pallas_call x1, Pallas kernels, precondition(): pl.pallas_call(functools.partial(precond_kernel, block), out_shape=jax.Sh...  2.43 us
    dot_general x1, matrix products, per_device(): jnp.einsum('sto,sti->soi', proj_grad, proj_act, preferred_element_type=jn...  1.25 us
  transfers between devices with their start and end apart: 2, of which 0 were waited for; matrix products, arithmetic and copies ran while one was open for 4% of the time, Pallas kernels for 21%

profile of v2, /device:TPU:0, one launch (start us, length us, event | category | flops | bytes accessed | tf_op | source)
XLA Modules:
  0.0 40.5 jit_solution(7004751905424037153)
XLA Ops:
  0.0 0.5 %collective-permute-start.1 = (bf16[1024,1024]{1,0:T(8,128)(2,1)}, bf16[1024,1024]{1,0:T(8,128)(2,1)}, u32[]{:S(2)}, u32[]{:S(2)}) collective-permute-start(bf16[1024,1024]{1,0:T(8,128)(2,1)} %own.1), channel_id=1, source_target_pairs={{0,4},{4,0},{1,5},{5,1},{2,6},{6,2},{3,7},{7,3},{8,12},{12,8},{9,1... | collective-permute-start | bytes 6291464 | tf_op jit(solution)/shard_map/ppermute | solution.py:19
  0.5 5.9 %project.1 = (bf16[256,64]{1,0:T(8,128)(2,1)}, bf16[256,64]{1,0:T(8,128)(2,1)}) custom-call(bf16[256,4096]{1,0:T(8,128)(2,1)} %bitcast.53, bf16[256,4096]{1,0:T(8,128)(2,1)} %bitcast.54, bf16[64,4096]{1,0:T(8,128)(2,1)} %bitcast.55, bf16[64,4096]{1,0:T(8,128)(2,1)} %bitcast.56), custom_call_target="tpu_custom_call" | custom-call | flops 268435456 | bytes 5242880 | tf_op jit(solution)/shard_map/project/pallas_call | solution.py:52
  6.4 0.0 copy-start
  6.4 1.3 %fusion = bf16[8,64,64]{2,1,0:T(8,128)(2,1)S(1)} fusion(bf16[8,32,64]{2,1,0:T(8,128)(2,1)} %bitcast.60, bf16[8,32,64]{2,1,0:T(8,128)(2,1)} %bitcast.59), kind=kOutput, calls=%fused_computation.1 | convolution fusion | flops 2162688 | bytes 131072 | tf_op jit(solution)/shard_map/sto,sti->soi/dot_general | solution.py:144
  7.7 0.2 convert_element_type.7
  8.0 19.9 %all_to_all.10 = bf16[8,8,3072]{2,1,0:T(8,128)(2,1)S(1)} all-to-all(bf16[8,8,3072]{2,1,0:T(8,128)(2,1)S(1)} %fusion.4), channel_id=1, replica_groups=mesh['grp'=2,'chip'=2,'core'=2,'gc'=4] {'chip','gc'}, dimensions={0} | all-to-all | bytes 786432 | tf_op jit(solution)/shard_map/all_to_all | solution.py:158
  27.8 0.1 collective-permute-start
  27.9 0.0 collective-permute-done.1.other
  27.9 0.0 copy-done
  27.9 2.4 %precondition.1.precond = bf16[64,1024]{1,0:T(8,128)(2,1)S(1)} custom-call(bf16[64,3072]{1,0:T(8,128)(2,1)S(1)} %bitcast.51, bf16[1024,1024]{1,0:T(8,128)(2,1)S(1)} %copy-done, bf16[1024,1024]{1,0:T(8,128)(2,1)} %collective-permute-done.1.other), custom_call_target="tpu_custom_call" | custom-call | flops 268435456 | bytes 4194304 | tf_op jit(solution)/shard_map/precondition/pallas_call | solution.py:82
  30.4 0.0 collective-permute-done
  30.4 0.3 kernel_terms.1
  30.7 9.1 %all_to_all.11 = f32[8,8,128]{2,1,0:T(8,128)S(1)} all-to-all(f32[8,8,128]{2,1,0:T(8,128)S(1)} %kernel_terms.1), channel_id=1, replica_groups=mesh['grp'=2,'chip'=2,'core'=2,'gc'=4] {'chip','gc'}, dimensions={0} | all-to-all | bytes 65536 | tf_op jit(solution)/shard_map/all_to_all | solution.py:175
  39.8 0.1 fusion.17
  39.9 0.6 %pad_maximum_fusion.10 = f32[32,32]{1,0:T(8,128)} fusion(f32[8,32]{1,0:T(8,128)S(1)} %get-tuple-element.22, f32[8,32]{1,0:T(8,128)S(1)} %get-tuple-element.23, f32[8,32]{1,0:T(8,128)S(1)} %get-tuple-element.24, f32[8,32]{1,0:T(8,128)S(1)} %get-tuple-element.21), kind=kLoop, calls=%fused_computation.29 | loop fusion | flops 3072 | bytes 8192 | tf_op jit(solution)/shard_map/concatenate | solution.py:176
  (12 shorter events, 0.1 us)
Async XLA Ops:
  0.0 27.9 %collective-permute-start.1 = (bf16[1024,1024]{1,0:T(8,128)(2,1)}, bf16[1024,1024]{1,0:T(8,128)(2,1)}, u32[]{:S(2)}, u32[]{:S(2)}) collective-permute-start(bf16[1024,1024]{1,0:T(8,128)(2,1)} %own.1), channel_id=1, source_target_pairs={{0,4},{4,0},{1,5},{5,1},{2,6},{6,2},{3,7},{7,3},{8,12},{12,8},{9,1... | collective-permute-start | bytes 6291464 | tf_op jit(solution)/shard_map/ppermute | solution.py:19
  6.4 21.5 %copy-start = (bf16[1024,1024]{1,0:T(8,128)(2,1)S(1)}, bf16[1024,1024]{1,0:T(8,128)(2,1)}, u32[]{:S(2)}) copy-start(bf16[1024,1024]{1,0:T(8,128)(2,1)} %own.1) | copy-start | bytes 6291460
  27.8 2.5 %collective-permute-start = (bf16[64,1024]{1,0:T(8,128)(2,1)S(1)}, bf16[64,1024]{1,0:T(8,128)(2,1)S(1)}, u32[]{:S(2)}, u32[]{:S(2)}) collective-permute-start(bf16[64,1024]{1,0:T(8,128)(2,1)S(1)} %slice.48), channel_id=1, source_target_pairs={{0,4},{4,0},{1,5},{5,1},{2,6},{6,2},{3,7},{7,3},{8,12},{12,8},{9,1... | collective-permute-start | bytes 393224 | tf_op jit(solution)/shard_map/ppermute | solution.py:19

commit v3 on v2

--- a/solution.py
+++ b/solution.py
@@ -9,7 +9,8 @@
 from jax.sharding import Mesh, PartitionSpec as P
 
 PLANE = ("chip", "gc")
-CHUNK = 64
+CHUNK = 1024
+LIMIT = 57 * 2**20
 VMEM = pl.BlockSpec(memory_space=pltpu.VMEM)
 HBM = pl.BlockSpec(memory_space=pl.ANY)
 NT = (((1,), (1,)), ((), ()))
@@ -19,55 +20,73 @@
     return lax.ppermute(value, "core", [(0, 1), (1, 0)])
 
 
-def project_kernel(act, grad, w_in, w_out, pa, pg, act_v, grad_v, in_v, out_v, w_sem, x_sem):
-    rows = act.shape[0]
-    steps = rows // CHUNK
-    weights = [
-        pltpu.make_async_copy(w_in, in_v, w_sem.at[0]),
-        pltpu.make_async_copy(w_out, out_v, w_sem.at[1]),
-    ]
+def rows_kernel(length, act, grad, w_in, w_out, out, act_v, grad_v, in_v, out_v, w_sem, x_sem):
+    seqs, rank = out.shape[:2]
+    rows, width = act.shape
+    steps = width // CHUNK
+    sides = ((act, w_in, act_v, in_v), (grad, w_out, grad_v, out_v))
     copies = []
-    for side, (src, dst) in enumerate(((act, act_v), (grad, grad_v))):
-        weights[side].start()
+    for side, (x, w, x_v, w_v) in enumerate(sides):
         for step in range(steps):
             part = pl.ds(step * CHUNK, CHUNK)
-            copies.append(
-                pltpu.make_async_copy(src.at[part], dst.at[part], x_sem.at[side * steps + step])
+            slot = side * steps + step
+            pair = (
+                pltpu.make_async_copy(w.at[:, part], w_v.at[:, part], w_sem.at[slot]),
+                pltpu.make_async_copy(x.at[:, part], x_v.at[:, part], x_sem.at[slot]),
             )
-            copies[-1].start()
-    for side, (held, weight, out) in enumerate(((act_v, in_v, pa), (grad_v, out_v, pg))):
-        weights[side].wait()
+            for copy in pair:
+                copy.start()
+            copies.append(pair)
+    projected = []
+    for side, (x, w, x_v, w_v) in enumerate(sides):
+        total = jnp.zeros((rank, rows), jnp.float32)
         for step in range(steps):
+            for copy in copies[side * steps + step]:
+                copy.wait()
             part = pl.ds(step * CHUNK, CHUNK)
-            copies[side * steps + step].wait()
-            out[part, :] = lax.dot_general(
-                held[part, :], weight[...], NT, preferred_element_type=jnp.float32
-            ).astype(out.dtype)
+            total += lax.dot_general(
+                w_v[:, part], x_v[:, part], NT, preferred_element_type=jnp.float32
+            )
+        projected.append(total.astype(out.dtype))
+    proj_act, proj_grad = projected
+    group = 128 // length
+    place = lax.broadcasted_iota(jnp.int32, (rank, 128), 1) // length
+    for first in range(0, seqs, group):
+        tokens = slice(first * length, (first + group) * length)
+        grads = proj_grad[:, tokens]
+        left = jnp.concatenate(
+            [jnp.where(place == i, grads, jnp.zeros_like(grads)) for i in range(group)]
+        )
+        summed = lax.dot_general(left, proj_act[:, tokens], NT, preferred_element_type=jnp.float32)
+        summed = (summed * (1.0 / math.sqrt(length))).astype(out.dtype)
+        out[first : first + group] = summed.reshape(group, rank, rank)
 
 
-def project(act, grad, w_in, w_out):
-    rows, width = act.shape
+def gradient_rows(activations, out_grads, w_in, w_out):
+    seqs, length, width = activations.shape
     rank = w_in.shape[0]
-    kind = act.dtype
+    rows = seqs * length
+    kind = activations.dtype
+    steps = 2 * width // CHUNK
     return pl.pallas_call(
-        project_kernel,
-        out_shape=[jax.ShapeDtypeStruct((rows, rank), kind)] * 2,
+        functools.partial(rows_kernel, length),
+        out_shape=jax.ShapeDtypeStruct((seqs, rank, rank), kind),
         in_specs=[HBM] * 4,
-        out_specs=[VMEM] * 2,
+        out_specs=VMEM,
         scratch_shapes=[
             pltpu.VMEM((rows, width), kind),
             pltpu.VMEM((rows, width), kind),
             pltpu.VMEM((rank, width), kind),
             pltpu.VMEM((rank, width), kind),
-            pltpu.SemaphoreType.DMA((2,)),
-            pltpu.SemaphoreType.DMA((2 * rows // CHUNK,)),
+            pltpu.SemaphoreType.DMA((steps,)),
+            pltpu.SemaphoreType.DMA((steps,)),
         ],
-        compiler_params=pltpu.CompilerParams(vmem_limit_bytes=58 * 2**20),
+        compiler_params=pltpu.CompilerParams(vmem_limit_bytes=LIMIT),
         cost_estimate=pl.CostEstimate(
             flops=4 * rows * width * rank, bytes_accessed=4 * (rows + rank) * width, transcendentals=0
         ),
-        name="project",
-    )(act, grad, w_in, w_out)
+        name="gradient_rows",
+    )(activations.reshape(rows, width), out_grads.reshape(rows, width), w_in, w_out)
 
 
 def precond_kernel(block, got, own, other, out):
@@ -133,18 +152,7 @@
 
     inv_other = other_core(inv_gram)
 
-    proj_act, proj_grad = project(
-        activations.reshape(seqs * length, width),
-        out_grads.reshape(seqs * length, width),
-        proj_in.T,
-        proj_out.T,
-    )
-    proj_act = proj_act.reshape(seqs, length, rank)
-    proj_grad = proj_grad.reshape(seqs, length, rank)
-    summed = jnp.einsum(
-        "sto,sti->soi", proj_grad, proj_act, preferred_element_type=jnp.float32
-    ).reshape(seqs, feat)
-    own_rows = (summed * (1.0 / math.sqrt(length))).astype(jnp.bfloat16)
+    own_rows = gradient_rows(activations, out_grads, proj_in.T, proj_out.T).reshape(seqs, feat)
 
     pieces = []
     for chip in range(chips):

time: 40.8 us -> 39.5 us (0.968)
  matrix products: 1.25 us -> 0 us
  Pallas kernels: 8.63 us -> 7.56 us
  local copies, waits for them, and re-layouts: 0.27 us -> 1.32 us
    dot_general x1 -> x0, matrix products: 1.25 us -> none  [per_device(): jnp.einsum('sto,sti->soi', proj_grad, proj_act, preferred_element_type=jn...]
    reshape x0 -> x1, local copies, waits for them, and re-layouts: none -> 1.23 us  [per_device(): gradient_rows(activations, out_grads, proj_in.T, proj_out.T)]
    pallas_call x1, Pallas kernels: 5.92 us -> 4.84 us  [gradient_rows(): pl.pallas_call(functools.partial(rows_kernel, length), out_shape=jax.Shap...]
  transfers between devices with their start and end apart: 2 -> 2, of which waited for: 0 -> 0; matrix products, arithmetic and copies ran while one was open for 4% -> 3% of each run, Pallas kernels for 21% -> 19%
where the time goes in v3:
time: 39.5 us; the launch traced here: 39.2 us
  blocking collectives  29 us (73%)
  Pallas kernels  7.56 us (19%)
  local copies, waits for them, and re-layouts  1.32 us (3%)
  other arithmetic  0.71 us (2%)
  starting transfers between devices  0.52 us (1%)
    all_to_all x1, blocking collectives, per_device(): got = lax.all_to_all(jnp.stack(pieces), PLANE, 0, 0, tiled=True)  19.9 us
    all_to_all x1, blocking collectives, per_device(): total = jnp.sum(lax.all_to_all(terms, PLANE, 0, 0, tiled=True), axis=0)  9.11 us
    pallas_call x1, Pallas kernels, gradient_rows(): pl.pallas_call(functools.partial(rows_kernel, length), out_shape=jax.Shap...  4.84 us
    pallas_call x1, Pallas kernels, precondition(): pl.pallas_call(functools.partial(precond_kernel, block), out_shape=jax.Sh...  2.43 us
    reshape x1, local copies, waits for them, and re-layouts, per_device(): gradient_rows(activations, out_grads, proj_in.T, proj_out.T)  1.23 us
  transfers between devices with their start and end apart: 2, of which 0 were waited for; matrix products, arithmetic and copies ran while one was open for 3% of the time, Pallas kernels for 19%

profile of v3, /device:TPU:0, one launch (start us, length us, event | category | flops | bytes accessed | tf_op | source)
XLA Modules:
  0.0 39.2 jit_solution(3757106079292523853)
XLA Ops:
  0.0 0.5 %collective-permute-start.1 = (bf16[1024,1024]{1,0:T(8,128)(2,1)}, bf16[1024,1024]{1,0:T(8,128)(2,1)}, u32[]{:S(2)}, u32[]{:S(2)}) collective-permute-start(bf16[1024,1024]{1,0:T(8,128)(2,1)} %own.1), channel_id=1, source_target_pairs={{0,4},{4,0},{1,5},{5,1},{2,6},{6,2},{3,7},{7,3},{8,12},{12,8},{9,1... | collective-permute-start | bytes 6291464 | tf_op jit(solution)/shard_map/ppermute | solution.py:20
  0.5 4.8 %gradient_rows.1 = bf16[8,64,64]{2,1,0:T(8,128)(2,1)} custom-call(bf16[256,4096]{1,0:T(8,128)(2,1)} %bitcast.47, bf16[256,4096]{1,0:T(8,128)(2,1)} %bitcast.48, bf16[64,4096]{1,0:T(8,128)(2,1)} %bitcast.50, bf16[64,4096]{1,0:T(8,128)(2,1)} %bitcast.51), custom_call_target="tpu_custom_call" | custom-call | flops 268435456 | bytes 5242880 | tf_op jit(solution)/shard_map/gradient_rows/pallas_call | solution.py:71
  5.3 0.0 copy-start
  5.3 1.2 %reshape.25 = bf16[8,4096]{1,0:T(8,128)(2,1)S(1)} reshape(bf16[8,64,64]{2,1,0:T(8,128)(2,1)} %gradient_rows.1) | data formatting | bytes 131072 | tf_op jit(solution)/shard_map/reshape | solution.py:155
  6.7 19.9 %all_to_all.10 = bf16[8,8,3072]{2,1,0:T(8,128)(2,1)S(1)} all-to-all(bf16[8,8,3072]{2,1,0:T(8,128)(2,1)S(1)} %fusion.3), channel_id=1, replica_groups=mesh['grp'=2,'chip'=2,'core'=2,'gc'=4] {'chip','gc'}, dimensions={0} | all-to-all | bytes 786432 | tf_op jit(solution)/shard_map/all_to_all | solution.py:166
  26.5 0.1 collective-permute-start
  26.6 0.0 collective-permute-done.1.other
  26.6 0.0 copy-done
  26.6 2.4 %precondition.1.precond = bf16[64,1024]{1,0:T(8,128)(2,1)S(1)} custom-call(bf16[64,3072]{1,0:T(8,128)(2,1)S(1)} %bitcast.45, bf16[1024,1024]{1,0:T(8,128)(2,1)S(1)} %copy-done, bf16[1024,1024]{1,0:T(8,128)(2,1)} %collective-permute-done.1.other), custom_call_target="tpu_custom_call" | custom-call | flops 268435456 | bytes 4194304 | tf_op jit(solution)/shard_map/precondition/pallas_call | solution.py:101
  29.1 0.0 collective-permute-done
  29.1 0.3 kernel_terms.1
  29.4 9.1 %all_to_all.11 = f32[8,8,128]{2,1,0:T(8,128)S(1)} all-to-all(f32[8,8,128]{2,1,0:T(8,128)S(1)} %kernel_terms.1), channel_id=1, replica_groups=mesh['grp'=2,'chip'=2,'core'=2,'gc'=4] {'chip','gc'}, dimensions={0} | all-to-all | bytes 65536 | tf_op jit(solution)/shard_map/all_to_all | solution.py:183
  38.5 0.1 fusion.16
  38.6 0.6 %pad_maximum_fusion.10 = f32[32,32]{1,0:T(8,128)} fusion(f32[8,32]{1,0:T(8,128)S(1)} %get-tuple-element.18, f32[8,32]{1,0:T(8,128)S(1)} %get-tuple-element.19, f32[8,32]{1,0:T(8,128)S(1)} %get-tuple-element.20, f32[8,32]{1,0:T(8,128)S(1)} %get-tuple-element.17), kind=kLoop, calls=%fused_computation.27 | loop fusion | flops 3072 | bytes 8192 | tf_op jit(solution)/shard_map/concatenate | solution.py:184
  (12 shorter events, 0.1 us)
Async XLA Ops:
  0.0 26.6 %collective-permute-start.1 = (bf16[1024,1024]{1,0:T(8,128)(2,1)}, bf16[1024,1024]{1,0:T(8,128)(2,1)}, u32[]{:S(2)}, u32[]{:S(2)}) collective-permute-start(bf16[1024,1024]{1,0:T(8,128)(2,1)} %own.1), channel_id=1, source_target_pairs={{0,4},{4,0},{1,5},{5,1},{2,6},{6,2},{3,7},{7,3},{8,12},{12,8},{9,1... | collective-permute-start | bytes 6291464 | tf_op jit(solution)/shard_map/ppermute | solution.py:20
  5.3 21.3 %copy-start = (bf16[1024,1024]{1,0:T(8,128)(2,1)S(1)}, bf16[1024,1024]{1,0:T(8,128)(2,1)}, u32[]{:S(2)}) copy-start(bf16[1024,1024]{1,0:T(8,128)(2,1)} %own.1) | copy-start | bytes 6291460
  26.5 2.5 %collective-permute-start = (bf16[64,1024]{1,0:T(8,128)(2,1)S(1)}, bf16[64,1024]{1,0:T(8,128)(2,1)S(1)}, u32[]{:S(2)}, u32[]{:S(2)}) collective-permute-start(bf16[64,1024]{1,0:T(8,128)(2,1)S(1)} %slice.48), channel_id=1, source_target_pairs={{0,4},{4,0},{1,5},{5,1},{2,6},{6,2},{3,7},{7,3},{8,12},{12,8},{9,1... | collective-permute-start | bytes 393224 | tf_op jit(solution)/shard_map/ppermute | solution.py:20

commit v4 on v3

--- a/solution.py
+++ b/solution.py
@@ -10,7 +10,7 @@
 
 PLANE = ("chip", "gc")
 CHUNK = 1024
-LIMIT = 57 * 2**20
+LIMIT = 107 * 2**19
 VMEM = pl.BlockSpec(memory_space=pltpu.VMEM)
 HBM = pl.BlockSpec(memory_space=pl.ANY)
 NT = (((1,), (1,)), ((), ()))
@@ -39,16 +39,17 @@
             copies.append(pair)
     projected = []
     for side, (x, w, x_v, w_v) in enumerate(sides):
-        total = jnp.zeros((rank, rows), jnp.float32)
+        total = jnp.zeros((rows, rank), jnp.float32)
         for step in range(steps):
             for copy in copies[side * steps + step]:
                 copy.wait()
             part = pl.ds(step * CHUNK, CHUNK)
             total += lax.dot_general(
-                w_v[:, part], x_v[:, part], NT, preferred_element_type=jnp.float32
+                x_v[:, part], w_v[:, part], NT, preferred_element_type=jnp.float32
             )
-        projected.append(total.astype(out.dtype))
-    proj_act, proj_grad = projected
+        projected.append(total)
+    both = jnp.concatenate(projected, axis=1).T.astype(out.dtype)
+    proj_act, proj_grad = both[:rank], both[rank:]
     group = 128 // length
     place = lax.broadcasted_iota(jnp.int32, (rank, 128), 1) // length
     for first in range(0, seqs, group):

time: 39.5 us -> 38 us (0.962)
  local copies, waits for them, and re-layouts: 1.32 us -> 0.27 us
  Pallas kernels: 7.56 us -> 7 us
    reshape x1, local copies, waits for them, and re-layouts: 1.23 us -> 0.18 us  [per_device(): gradient_rows(activations, out_grads, proj_in.T, proj_out.T)]
    pallas_call x1, Pallas kernels: 4.84 us -> 4.29 us  [gradient_rows(): pl.pallas_call(functools.partial(rows_kernel, length), out_shape=jax.Shap...]
  transfers between devices with their start and end apart: 2 -> 2, of which waited for: 0 -> 0; matrix products, arithmetic and copies ran while one was open for 3% -> 1% of each run, Pallas kernels for 19% -> 18%
where the time goes in v4:
time: 38 us; the launch traced here: 37.8 us
  blocking collectives  29.1 us (77%)
  Pallas kernels  7 us (18%)
  other arithmetic  0.72 us (2%)
  starting transfers between devices  0.52 us (1%)
    all_to_all x1, blocking collectives, per_device(): got = lax.all_to_all(jnp.stack(pieces), PLANE, 0, 0, tiled=True)  20 us
    all_to_all x1, blocking collectives, per_device(): total = jnp.sum(lax.all_to_all(terms, PLANE, 0, 0, tiled=True), axis=0)  9.11 us
    pallas_call x1, Pallas kernels, gradient_rows(): pl.pallas_call(functools.partial(rows_kernel, length), out_shape=jax.Shap...  4.29 us
    pallas_call x1, Pallas kernels, precondition(): pl.pallas_call(functools.partial(precond_kernel, block), out_shape=jax.Sh...  2.43 us
  transfers between devices with their start and end apart: 2, of which 0 were waited for; matrix products, arithmetic and copies ran while one was open for 1% of the time, Pallas kernels for 18%

profile of v4, /device:TPU:0, one launch (start us, length us, event | category | flops | bytes accessed | tf_op | source)
XLA Modules:
  0.0 37.8 jit_solution(10554328093378088971)
XLA Ops:
  0.0 0.5 %collective-permute-start.1 = (bf16[1024,1024]{1,0:T(8,128)(2,1)}, bf16[1024,1024]{1,0:T(8,128)(2,1)}, u32[]{:S(2)}, u32[]{:S(2)}) collective-permute-start(bf16[1024,1024]{1,0:T(8,128)(2,1)} %own.1), channel_id=1, source_target_pairs={{0,4},{4,0},{1,5},{5,1},{2,6},{6,2},{3,7},{7,3},{8,12},{12,8},{9,1... | collective-permute-start | bytes 6291464 | tf_op jit(solution)/shard_map/ppermute | solution.py:20
  0.5 4.3 %gradient_rows.1 = bf16[8,64,64]{2,1,0:T(8,128)(2,1)S(1)} custom-call(bf16[256,4096]{1,0:T(8,128)(2,1)} %bitcast.47, bf16[256,4096]{1,0:T(8,128)(2,1)} %bitcast.48, bf16[64,4096]{1,0:T(8,128)(2,1)} %bitcast.50, bf16[64,4096]{1,0:T(8,128)(2,1)} %bitcast.51), custom_call_target="tpu_custom_call" | custom-call | flops 268435456 | bytes 5242880 | tf_op jit(solution)/shard_map/gradient_rows/pallas_call | solution.py:72
  4.8 0.0 copy-start
  4.8 0.2 reshape.25
  5.1 20.0 %all_to_all.10 = bf16[8,8,3072]{2,1,0:T(8,128)(2,1)S(1)} all-to-all(bf16[8,8,3072]{2,1,0:T(8,128)(2,1)S(1)} %fusion.3), channel_id=1, replica_groups=mesh['grp'=2,'chip'=2,'core'=2,'gc'=4] {'chip','gc'}, dimensions={0} | all-to-all | bytes 786432 | tf_op jit(solution)/shard_map/all_to_all | solution.py:167
  25.1 0.1 collective-permute-start
  25.2 0.0 collective-permute-done.1.other
  25.2 0.0 copy-done
  25.2 2.4 %precondition.1.precond = bf16[64,1024]{1,0:T(8,128)(2,1)S(1)} custom-call(bf16[64,3072]{1,0:T(8,128)(2,1)S(1)} %bitcast.45, bf16[1024,1024]{1,0:T(8,128)(2,1)S(1)} %copy-done, bf16[1024,1024]{1,0:T(8,128)(2,1)} %collective-permute-done.1.other), custom_call_target="tpu_custom_call" | custom-call | flops 268435456 | bytes 4194304 | tf_op jit(solution)/shard_map/precondition/pallas_call | solution.py:102
  27.6 0.0 collective-permute-done
  27.7 0.3 kernel_terms.1
  28.0 9.1 %all_to_all.11 = f32[8,8,128]{2,1,0:T(8,128)S(1)} all-to-all(f32[8,8,128]{2,1,0:T(8,128)S(1)} %kernel_terms.1), channel_id=1, replica_groups=mesh['grp'=2,'chip'=2,'core'=2,'gc'=4] {'chip','gc'}, dimensions={0} | all-to-all | bytes 65536 | tf_op jit(solution)/shard_map/all_to_all | solution.py:184
  37.1 0.1 fusion.16
  37.1 0.6 %pad_maximum_fusion.10 = f32[32,32]{1,0:T(8,128)} fusion(f32[8,32]{1,0:T(8,128)S(1)} %get-tuple-element.18, f32[8,32]{1,0:T(8,128)S(1)} %get-tuple-element.19, f32[8,32]{1,0:T(8,128)S(1)} %get-tuple-element.20, f32[8,32]{1,0:T(8,128)S(1)} %get-tuple-element.17), kind=kLoop, calls=%fused_computation.27 | loop fusion | flops 3072 | bytes 8192 | tf_op jit(solution)/shard_map/concatenate | solution.py:185
  (12 shorter events, 0.1 us)
Async XLA Ops:
  0.0 25.2 %collective-permute-start.1 = (bf16[1024,1024]{1,0:T(8,128)(2,1)}, bf16[1024,1024]{1,0:T(8,128)(2,1)}, u32[]{:S(2)}, u32[]{:S(2)}) collective-permute-start(bf16[1024,1024]{1,0:T(8,128)(2,1)} %own.1), channel_id=1, source_target_pairs={{0,4},{4,0},{1,5},{5,1},{2,6},{6,2},{3,7},{7,3},{8,12},{12,8},{9,1... | collective-permute-start | bytes 6291464 | tf_op jit(solution)/shard_map/ppermute | solution.py:20
  4.8 20.4 %copy-start = (bf16[1024,1024]{1,0:T(8,128)(2,1)S(1)}, bf16[1024,1024]{1,0:T(8,128)(2,1)}, u32[]{:S(2)}) copy-start(bf16[1024,1024]{1,0:T(8,128)(2,1)} %own.1) | copy-start | bytes 6291460
  25.1 2.5 %collective-permute-start = (bf16[64,1024]{1,0:T(8,128)(2,1)S(1)}, bf16[64,1024]{1,0:T(8,128)(2,1)S(1)}, u32[]{:S(2)}, u32[]{:S(2)}) collective-permute-start(bf16[64,1024]{1,0:T(8,128)(2,1)S(1)} %slice.48), channel_id=1, source_target_pairs={{0,4},{4,0},{1,5},{5,1},{2,6},{6,2},{3,7},{7,3},{8,12},{12,8},{9,1... | collective-permute-start | bytes 393224 | tf_op jit(solution)/shard_map/ppermute | solution.py:20

commit v5 on v4

v5 whole, which is shorter than its diff:
```python
import functools
import math

import jax
import jax.numpy as jnp
from jax import lax
from jax.experimental import pallas as pl
from jax.experimental.pallas import tpu as pltpu
from jax.sharding import Mesh, PartitionSpec as P

PLANE = ("chip", "gc")
CHUNK = 1024
LIMIT = 107 * 2**19
VMEM = pl.BlockSpec(memory_space=pltpu.VMEM)
HBM = pl.BlockSpec(memory_space=pl.ANY)
NT = (((1,), (1,)), ((), ()))


def other_core(value):
    return lax.ppermute(value, "core", [(0, 1), (1, 0)])


def left_parity(chip, col):
    home = col // 2
    return jnp.where(chip < home, col % 2, 1 - col % 2)


def rows_kernel(length, block, cols, act, grad, w_in, w_out, out, act_v, grad_v, in_v, out_v, w_sem, x_sem):
    seqs = out.shape[1]
    rank = w_in.shape[0]
    rows, width = act.shape
    steps = width // CHUNK
    sides = ((act, w_in, act_v, in_v), (grad, w_out, grad_v, out_v))
    copies = []
    for side, (x, w, x_v, w_v) in enumerate(sides):
        for step in range(steps):
            part = pl.ds(step * CHUNK, CHUNK)
            slot = side * steps + step
            pair = (
                pltpu.make_async_copy(w.at[:, part], w_v.at[:, part], w_sem.at[slot]),
                pltpu.make_async_copy(x.at[:, part], x_v.at[:, part], x_sem.at[slot]),
            )
            for copy in pair:
                copy.start()
            copies.append(pair)
    projected = []
    for side, (x, w, x_v, w_v) in enumerate(sides):
        total = jnp.zeros((rows, rank), jnp.float32)
        for step in range(steps):
            for copy in copies[side * steps + step]:
                copy.wait()
            part = pl.ds(step * CHUNK, CHUNK)
            total += lax.dot_general(
                x_v[:, part], w_v[:, part], NT, preferred_element_type=jnp.float32
            )
        projected.append(total)
    both = jnp.concatenate(projected, axis=1).T.astype(out.dtype)
    proj_act, proj_grad = both[:rank], both[rank:]
    many = rank // 2 * seqs
    row = lax.broadcasted_iota(jnp.int32, (many, rank), 0)
    column = lax.broadcasted_iota(jnp.int32, (many, rank), 1)
    token = lax.broadcasted_iota(jnp.int32, (many, rows), 1)
    sequence = lax.broadcasted_iota(jnp.int32, (many, rows), 0) % seqs
    left = []
    for odd in range(2):
        pick = (column == row // seqs * 2 + odd).astype(jnp.float32).astype(out.dtype)
        spread = jnp.dot(pick, proj_grad, preferred_element_type=jnp.float32)
        left.append(jnp.where(token // length == sequence, spread, 0.0).astype(out.dtype))
    nothing = jnp.zeros_like(proj_act)
    right = jnp.concatenate(
        [
            jnp.concatenate([proj_act, nothing], axis=1),
            jnp.concatenate([nothing, proj_act], axis=1),
        ]
    )
    summed = lax.dot_general(
        jnp.concatenate(left, axis=1), right, NT, preferred_element_type=jnp.float32
    )
    summed = summed * (1.0 / math.sqrt(length))
    lanes = 2 * rank
    tiles = block // lanes
    grad_rows = [
        summed[i * seqs : (i + 1) * seqs].astype(out.dtype) for i in range(many // seqs)
    ]
    for place in range(out.shape[0]):
        chip, col = place // cols, place % cols
        odd = col % 2 if chip < col // 2 else 1 - col % 2
        for slot, source in enumerate((2 * chip + odd, col)):
            for i in range(tiles):
                start = slot * block + i * lanes
                out[place, :, start : start + lanes] = grad_rows[source * tiles + i]


def gradient_pieces(plane, cols, block, activations, out_grads, w_in, w_out):
    seqs, length, width = activations.shape
    rank = w_in.shape[0]
    rows = seqs * length
    kind = activations.dtype
    steps = 2 * width // CHUNK
    return pl.pallas_call(
        functools.partial(rows_kernel, length, block, cols),
        out_shape=jax.ShapeDtypeStruct((plane, seqs, 2 * block), kind),
        in_specs=[HBM] * 4,
        out_specs=VMEM,
        scratch_shapes=[
            pltpu.VMEM((rows, width), kind),
            pltpu.VMEM((rows, width), kind),
            pltpu.VMEM((rank, width), kind),
            pltpu.VMEM((rank, width), kind),
            pltpu.SemaphoreType.DMA((steps,)),
            pltpu.SemaphoreType.DMA((steps,)),
        ],
        compiler_params=pltpu.CompilerParams(vmem_limit_bytes=LIMIT),
        cost_estimate=pl.CostEstimate(
            flops=4 * rows * width * rank, bytes_accessed=4 * (rows + rank) * width, transcendentals=0
        ),
        name="gradient_pieces",
    )(activations.reshape(rows, width), out_grads.reshape(rows, width), w_in, w_out)


def precond_kernel(block, weights, got, own, other, out):
    left = got[:, :block].astype(jnp.float32)
    right = got[:, block:].astype(jnp.float32)
    for_own = (left * weights[0] + right * weights[1]).astype(got.dtype)
    for_other = (left * weights[2] + right * weights[3]).astype(got.dtype)
    total = jnp.dot(for_own, own[...], preferred_element_type=jnp.float32)
    total += jnp.dot(for_other, other[...], preferred_element_type=jnp.float32)
    out[...] = total.astype(out.dtype)


def precondition(weights, got, own, other):
    rows = got.shape[0]
    block, width = own.shape
    return pl.pallas_call(
        functools.partial(precond_kernel, block),
        out_shape=jax.ShapeDtypeStruct((rows, width), got.dtype),
        in_specs=[pl.BlockSpec(memory_space=pltpu.SMEM)] + [VMEM] * 3,
        out_specs=VMEM,
        compiler_params=pltpu.CompilerParams(vmem_limit_bytes=16 * 2**20),
        cost_estimate=pl.CostEstimate(
            flops=4 * rows * block * width, bytes_accessed=4 * block * width, transcendentals=0
        ),
        name="precondition",
    )(weights, got, own, other)


def terms_kernel(n, fold, scale, core, precond, right, out):
    chips = n // 2
    size = right.shape[0] // n
    step = size // fold

    def packed(terms, row, col):
        lanes = terms[row * size : (row + 1) * size, col * size : (col + 1) * size]
        return jnp.concatenate([lanes[i * step : (i + 1) * step] for i in range(fold)], axis=1)

    def add(first, count):
        held = precond[pl.ds(first * size, count * size), :]
        once = lax.dot_general(held, right[...], NT, preferred_element_type=jnp.float32) * scale
        turned = lax.dot_general(right[...], held, NT, preferred_element_type=jnp.float32) * scale
        for chip in range(count):
            mine = 2 * (first + chip) + core[0]
            for place in range(n):
                out[mine * n + place] += packed(once, chip, place)
                out[place * n + mine] += packed(turned, place, chip)

    out[...] = jnp.zeros_like(out)
    if chips <= 2:
        add(0, chips)
    else:
        pl.loop(0, chips)(functools.partial(add, count=1))


def kernel_terms(n, fold, scale, core, precond, right):
    rows, width = precond.shape
    other = right.shape[0]
    size = other // n
    return pl.pallas_call(
        functools.partial(terms_kernel, n, fold, scale),
        out_shape=jax.ShapeDtypeStruct((n * n, size // fold, fold * size), jnp.float32),
        in_specs=[pl.BlockSpec(memory_space=pltpu.SMEM)] + [VMEM] * 2,
        out_specs=VMEM,
        compiler_params=pltpu.CompilerParams(
            vmem_limit_bytes=max(16 * 2**20, 12 * other * other)
        ),
        cost_estimate=pl.CostEstimate(
            flops=4 * rows * other * width, bytes_accessed=4 * other * other, transcendentals=0
        ),
        name="kernel_terms",
    )(core, precond, right)


def per_device(chips, cols, activations, out_grads, proj_in, proj_out, inv_gram):
    seqs, length, width = activations.shape
    rank = proj_in.shape[1]
    feat = rank * rank
    block = inv_gram.shape[0]
    plane = chips * cols
    half = seqs * plane
    tall = half // chips
    chip, core, col = (lax.axis_index(name) for name in ("chip", "core", "gc"))

    inv_other = other_core(inv_gram)

    pieces = gradient_pieces(plane, cols, block, activations, out_grads, proj_in.T, proj_out.T)
    got = lax.all_to_all(pieces, PLANE, 0, 0, tiled=True).reshape(half, 2 * block)

    mine = got[:, block:]
    theirs = other_core(mine)
    home = col // 2 == chip
    once = jnp.where(home & (col % 2 == 1), 0.0, 1.0)
    again = jnp.where(home, 0.5, 0.0)
    own_left = left_parity(chip, col) == core
    weights = jnp.stack(
        [
            jnp.where(own_left, once, 0.0),
            jnp.where(own_left, 0.0, again),
            jnp.where(own_left, 0.0, once),
            jnp.where(own_left, again, 0.0),
        ]
    ).astype(jnp.float32)
    theirs, precond = lax.optimization_barrier(
        (theirs, precondition(weights, got, inv_gram, inv_other))
    )
    mine = mine.reshape(chips, 1, tall, block)
    theirs = theirs.reshape(chips, 1, tall, block)
    right = jnp.where(
        core == 0,
        jnp.concatenate([mine, theirs], axis=1),
        jnp.concatenate([theirs, mine], axis=1),
    ).reshape(2 * half, block)

    fold = max(1, 128 // tall)
    terms = kernel_terms(cols, fold, 8.0 / feat, core.reshape(1).astype(jnp.int32), precond, right)
    total = jnp.sum(lax.all_to_all(terms, ("chip", "core", "gc"), 0, 0, tiled=True), axis=0)
    return jnp.concatenate([total[:, i * tall : (i + 1) * tall] for i in range(fold)])


def solution(mesh):
    grp, gr, gc = (mesh.shape[name] for name in ("grp", "gr", "gc"))
    split = Mesh(mesh.devices.reshape(grp, gr // 2, 2, gc), ("grp", "chip", "core", "gc"))
    rows = ("grp", "chip", "core", "gc")
    in_specs = (P(rows, None, None), P(rows, None, None), P(), P(), P(("chip", "core"), "gc"))
    out_specs = P(("grp", "chip", "core"), "gc")

    def fn(*args):
        return per_device(gr // 2, gc, *args)

    return jax.shard_map(fn, mesh=split, in_specs=in_specs, out_specs=out_specs, check_vma=False)
```

time: 38 us -> 36.3 us (0.955)
  blocking collectives: 29.1 us -> 9.19 us
  waiting for transfers between devices: 0.01 us -> 10.4 us
  starting transfers between devices: 0.52 us -> 7.34 us
  Pallas kernels: 7 us -> 8.17 us
    all_to_all x2 -> x1, blocking collectives: 29.1 us -> 9.19 us  [per_device(): lax.all_to_all(terms, ('chip', 'core', 'gc'), 0, 0, tiled=True)]
    all_to_all x0 -> x1, waiting for transfers between devices: none -> 10.4 us  [per_device(): lax.all_to_all(pieces, PLANE, 0, 0, tiled=True).reshape(half, 2 * block)]
    all_to_all x0 -> x1, starting transfers between devices: none -> 6.82 us  [per_device(): lax.all_to_all(pieces, PLANE, 0, 0, tiled=True).reshape(half, 2 * block)]
    pallas_call x2, Pallas kernels: 4.57 us -> 5.73 us  [the longest x1 5.32 us: gradient_pieces(): pl.pallas_call(functools.partial(rows_kernel, length, block, cols), out_s...]
  transfers between devices with their start and end apart: 2 -> 3, of which waited for: 0 -> 1; matrix products, arithmetic and copies ran while one was open for 1% -> 0% of each run, Pallas kernels for 18% -> 22%
where the time goes in v5:
time: 36.3 us; the launch traced here: 36 us
  waiting for transfers between devices  10.4 us (29%)
  blocking collectives  9.19 us (25%)
  Pallas kernels  8.17 us (23%)
  starting transfers between devices  7.34 us (20%)
  other arithmetic  0.74 us (2%)
    all_to_all x1, waiting for transfers between devices, per_device(): lax.all_to_all(pieces, PLANE, 0, 0, tiled=True).reshape(half, 2 * block)  10.4 us
    all_to_all x1, blocking collectives, per_device(): lax.all_to_all(terms, ('chip', 'core', 'gc'), 0, 0, tiled=True)  9.19 us
    all_to_all x1, starting transfers between devices, per_device(): lax.all_to_all(pieces, PLANE, 0, 0, tiled=True).reshape(half, 2 * block)  6.82 us
    pallas_call x1, Pallas kernels, gradient_pieces(): pl.pallas_call(functools.partial(rows_kernel, length, block, cols), out_s...  5.32 us
    pallas_call x1, Pallas kernels, precondition(): pl.pallas_call(functools.partial(precond_kernel, block), out_shape=jax.Sh...  2.44 us
  transfers between devices with their start and end apart: 3, of which 1 were waited for; matrix products, arithmetic and copies ran while one was open for 0% of the time, Pallas kernels for 22%

profile of v5, /device:TPU:0, one launch (start us, length us, event | category | flops | bytes accessed | tf_op | source)
XLA Modules:
  0.0 36.0 jit_solution(15385002057172265440)
XLA Ops:
  0.0 0.5 %collective-permute-start.1 = (bf16[1024,1024]{1,0:T(8,128)(2,1)}, bf16[1024,1024]{1,0:T(8,128)(2,1)}, u32[]{:S(2)}, u32[]{:S(2)}) collective-permute-start(bf16[1024,1024]{1,0:T(8,128)(2,1)} %own.1), channel_id=1, source_target_pairs={{0,4},{4,0},{1,5},{5,1},{2,6},{6,2},{3,7},{7,3},{8,12},{12,8},{9,1... | collective-permute-start | bytes 6291464 | tf_op jit(solution)/shard_map/ppermute | solution.py:20
  0.5 0.0 copy-start
  0.5 5.3 %gradient_pieces.1 = bf16[8,8,2048]{2,1,0:T(8,128)(2,1)} custom-call(bf16[256,4096]{1,0:T(8,128)(2,1)} %bitcast.20, bf16[256,4096]{1,0:T(8,128)(2,1)} %bitcast.21, bf16[64,4096]{1,0:T(8,128)(2,1)} %bitcast.23, bf16[64,4096]{1,0:T(8,128)(2,1)} %bitcast.24), custom_call_target="tpu_custom_call" | custom-call | flops 268435456 | bytes 5242880 | tf_op jit(solution)/shard_map/gradient_pieces/pallas_call | solution.py:100
  5.8 6.8 %all-to-all-start = ((bf16[8,8,2048]{2,1,0:T(8,128)(2,1)}), bf16[8,8,2048]{2,1,0:T(8,128)(2,1)S(1)}, u32[]{:S(2)}, u32[]{:S(2)}) async-start(bf16[8,8,2048]{2,1,0:T(8,128)(2,1)} %gradient_pieces.1), calls=%async_computation | async-start | bytes 524288 | tf_op jit(solution)/shard_map/all_to_all | solution.py:205
  12.6 10.4 %all-to-all-done = bf16[8,8,2048]{2,1,0:T(8,128)(2,1)S(1)} async-done(((bf16[8,8,2048]{2,1,0:T(8,128)(2,1)}), bf16[8,8,2048]{2,1,0:T(8,128)(2,1)S(1)}, u32[]{:S(2)}, u32[]{:S(2)}) %all-to-all-start) | async-done | bytes 262176 | tf_op jit(solution)/shard_map/all_to_all | solution.py:205
  23.1 0.1 collective-permute-start
  23.1 0.1 pad_maximum_fusion.1.weights
  23.2 0.0 collective-permute-done.1.other
  23.2 0.0 copy-done
  23.2 2.4 %precondition.1.precond = bf16[64,1024]{1,0:T(8,128)(2,1)S(1)} custom-call(f32[4]{0:T(128)S(1)} %pad_maximum_fusion.1.weights, bf16[64,2048]{1,0:T(8,128)(2,1)S(1)} %bitcast.18, bf16[1024,1024]{1,0:T(8,128)(2,1)S(1)} %copy-done, bf16[1024,1024]{1,0:T(8,128)(2,1)} %collective-permute-done.1.other), custom_call_target="tpu_custom_call" | custom-call | flops 268435456 | bytes 4194304 | tf_op jit(solution)/shard_map/precondition/pallas_call | solution.py:134
  25.7 0.0 collective-permute-done
  25.7 0.4 %kernel_terms.1 = f32[16,8,128]{2,1,0:T(8,128)S(1)} custom-call(s32[1]{0:T(128)} %bitcast.core, bf16[64,1024]{1,0:T(8,128)(2,1)S(1)} %precondition.1.precond, bf16[128,1024]{1,0:T(8,128)(2,1)S(1)} %bitcast.19), custom_call_target="tpu_custom_call" | custom-call | flops 33554432 | bytes 65536 | tf_op jit(solution)/shard_map/kernel_terms/pallas_call | solution.py:177
  26.1 9.2 %all_to_all.10 = f32[16,8,128]{2,1,0:T(8,128)S(1)} all-to-all(f32[16,8,128]{2,1,0:T(8,128)S(1)} %kernel_terms.1), channel_id=1, replica_groups=mesh['grp'=2,'chip'=2,'core'=2,'gc'=4] {'chip','core','gc'}, dimensions={0} | all-to-all | bytes 131072 | tf_op jit(solution)/shard_map/all_to_all | solution.py:234
  35.3 0.1 fusion
  35.4 0.6 %pad_maximum_fusion = f32[32,32]{1,0:T(8,128)} fusion(f32[8,32]{1,0:T(8,128)S(1)} %get-tuple-element.10, f32[8,32]{1,0:T(8,128)S(1)} %get-tuple-element.11, f32[8,32]{1,0:T(8,128)S(1)} %get-tuple-element.12, f32[8,32]{1,0:T(8,128)S(1)} %get-tuple-element.9), kind=kLoop, calls=%fused_computation.1 | loop fusion | flops 3072 | bytes 8192 | tf_op jit(solution)/shard_map/concatenate | solution.py:235
  (3 shorter events, 0.1 us)
Async XLA Ops:
  0.0 23.2 %collective-permute-start.1 = (bf16[1024,1024]{1,0:T(8,128)(2,1)}, bf16[1024,1024]{1,0:T(8,128)(2,1)}, u32[]{:S(2)}, u32[]{:S(2)}) collective-permute-start(bf16[1024,1024]{1,0:T(8,128)(2,1)} %own.1), channel_id=1, source_target_pairs={{0,4},{4,0},{1,5},{5,1},{2,6},{6,2},{3,7},{7,3},{8,12},{12,8},{9,1... | collective-permute-start | bytes 6291464 | tf_op jit(solution)/shard_map/ppermute | solution.py:20
  0.5 22.8 %copy-start = (bf16[1024,1024]{1,0:T(8,128)(2,1)S(1)}, bf16[1024,1024]{1,0:T(8,128)(2,1)}, u32[]{:S(2)}) copy-start(bf16[1024,1024]{1,0:T(8,128)(2,1)} %own.1) | copy-start | bytes 6291460
  5.8 17.3 %all-to-all-start = ((bf16[8,8,2048]{2,1,0:T(8,128)(2,1)}), bf16[8,8,2048]{2,1,0:T(8,128)(2,1)S(1)}, u32[]{:S(2)}, u32[]{:S(2)}) async-start(bf16[8,8,2048]{2,1,0:T(8,128)(2,1)} %gradient_pieces.1), calls=%async_computation | async-start | bytes 524288 | tf_op jit(solution)/shard_map/all_to_all | solution.py:205
  23.1 2.6 %collective-permute-start = (bf16[64,1024]{1,0:T(8,128)(2,1)S(1)}, bf16[64,1024]{1,0:T(8,128)(2,1)S(1)}, u32[]{:S(2)}, u32[]{:S(2)}) collective-permute-start(bf16[64,1024]{1,0:T(8,128)(2,1)S(1)} %slice.20), channel_id=1, source_target_pairs={{0,4},{4,0},{1,5},{5,1},{2,6},{6,2},{3,7},{7,3},{8,12},{12,8},{9,1... | collective-permute-start | bytes 393224 | tf_op jit(solution)/shard_map/ppermute | solution.py:20

commit v6 on v5

--- a/solution.py
+++ b/solution.py
@@ -199,9 +199,9 @@
     tall = half // chips
     chip, core, col = (lax.axis_index(name) for name in ("chip", "core", "gc"))
 
+    pieces = gradient_pieces(plane, cols, block, activations, out_grads, proj_in.T, proj_out.T)
+    pieces, inv_gram = lax.optimization_barrier((pieces, inv_gram))
     inv_other = other_core(inv_gram)
-
-    pieces = gradient_pieces(plane, cols, block, activations, out_grads, proj_in.T, proj_out.T)
     got = lax.all_to_all(pieces, PLANE, 0, 0, tiled=True).reshape(half, 2 * block)
 
     mine = got[:, block:]

time: 36.3 us -> 36.4 us (level)
  transfers between devices with their start and end apart: 3 -> 3, of which waited for: 1 -> 1; matrix products, arithmetic and copies ran while one was open for 0% -> 0% of each run, Pallas kernels for 22% -> 7%
where the time goes in v6:
time: 36.4 us; the launch traced here: 36.1 us
  waiting for transfers between devices  10.4 us (29%)
  blocking collectives  9.19 us (25%)
  Pallas kernels  8.17 us (22%)
  starting transfers between devices  7.41 us (20%)
  other arithmetic  0.74 us (2%)
    all_to_all x1, waiting for transfers between devices, per_device(): lax.all_to_all(pieces, PLANE, 0, 0, tiled=True).reshape(half, 2 * block)  10.4 us
    all_to_all x1, blocking collectives, per_device(): lax.all_to_all(terms, ('chip', 'core', 'gc'), 0, 0, tiled=True)  9.19 us
    all_to_all x1, starting transfers between devices, per_device(): lax.all_to_all(pieces, PLANE, 0, 0, tiled=True).reshape(half, 2 * block)  6.83 us
    pallas_call x1, Pallas kernels, gradient_pieces(): pl.pallas_call(functools.partial(rows_kernel, length, block, cols), out_s...  5.33 us
    pallas_call x1, Pallas kernels, precondition(): pl.pallas_call(functools.partial(precond_kernel, block), out_shape=jax.Sh...  2.44 us
  transfers between devices with their start and end apart: 3, of which 1 were waited for; matrix products, arithmetic and copies ran while one was open for 0% of the time, Pallas kernels for 7%

profile of v6, /device:TPU:0, one launch (start us, length us, event | category | flops | bytes accessed | tf_op | source)
XLA Modules:
  0.0 36.1 jit_solution(8664655769169523013)
XLA Ops:
  0.0 0.0 copy-start
  0.0 5.3 %gradient_pieces.1 = bf16[8,8,2048]{2,1,0:T(8,128)(2,1)} custom-call(bf16[256,4096]{1,0:T(8,128)(2,1)} %bitcast.20, bf16[256,4096]{1,0:T(8,128)(2,1)} %bitcast.21, bf16[64,4096]{1,0:T(8,128)(2,1)} %bitcast.23, bf16[64,4096]{1,0:T(8,128)(2,1)} %bitcast.24), custom_call_target="tpu_custom_call" | custom-call | flops 268435456 | bytes 5242880 | tf_op jit(solution)/shard_map/gradient_pieces/pallas_call | solution.py:100
  5.3 0.0 copy-done
  5.3 0.5 %collective-permute-start.1 = (bf16[1024,1024]{1,0:T(8,128)(2,1)S(1)}, bf16[1024,1024]{1,0:T(8,128)(2,1)}, u32[]{:S(2)}, u32[]{:S(2)}) collective-permute-start(bf16[1024,1024]{1,0:T(8,128)(2,1)S(1)} %copy-done), channel_id=1, source_target_pairs={{0,4},{4,0},{1,5},{5,1},{2,6},{6,2},{3,7},{7,3},{8,12},{12,8},{9,1... | collective-permute-start | bytes 6291464 | tf_op jit(solution)/shard_map/ppermute | solution.py:20
  5.9 6.8 %all-to-all-start = ((bf16[8,8,2048]{2,1,0:T(8,128)(2,1)}), bf16[8,8,2048]{2,1,0:T(8,128)(2,1)S(1)}, u32[]{:S(2)}, u32[]{:S(2)}) async-start(bf16[8,8,2048]{2,1,0:T(8,128)(2,1)} %gradient_pieces.1), calls=%async_computation | async-start | bytes 524288 | tf_op jit(solution)/shard_map/all_to_all | solution.py:205
  12.7 10.4 %all-to-all-done = bf16[8,8,2048]{2,1,0:T(8,128)(2,1)S(1)} async-done(((bf16[8,8,2048]{2,1,0:T(8,128)(2,1)}), bf16[8,8,2048]{2,1,0:T(8,128)(2,1)S(1)}, u32[]{:S(2)}, u32[]{:S(2)}) %all-to-all-start) | async-done | bytes 262176 | tf_op jit(solution)/shard_map/all_to_all | solution.py:205
  23.1 0.1 collective-permute-start
  23.2 0.1 pad_maximum_fusion.1.weights
  23.3 0.0 collective-permute-done.1.other
  23.3 2.4 %precondition.1.precond = bf16[64,1024]{1,0:T(8,128)(2,1)S(1)} custom-call(f32[4]{0:T(128)S(1)} %pad_maximum_fusion.1.weights, bf16[64,2048]{1,0:T(8,128)(2,1)S(1)} %bitcast.18, bf16[1024,1024]{1,0:T(8,128)(2,1)S(1)} %copy-done, bf16[1024,1024]{1,0:T(8,128)(2,1)} %collective-permute-done.1.other), custom_call_target="tpu_custom_call" | custom-call | flops 268435456 | bytes 4194304 | tf_op jit(solution)/shard_map/precondition/pallas_call | solution.py:134
  25.7 0.0 collective-permute-done
  25.8 0.4 %kernel_terms.1 = f32[16,8,128]{2,1,0:T(8,128)S(1)} custom-call(s32[1]{0:T(128)} %bitcast.core, bf16[64,1024]{1,0:T(8,128)(2,1)S(1)} %precondition.1.precond, bf16[128,1024]{1,0:T(8,128)(2,1)S(1)} %bitcast.19), custom_call_target="tpu_custom_call" | custom-call | flops 33554432 | bytes 65536 | tf_op jit(solution)/shard_map/kernel_terms/pallas_call | solution.py:177
  26.2 9.2 %all_to_all.10 = f32[16,8,128]{2,1,0:T(8,128)S(1)} all-to-all(f32[16,8,128]{2,1,0:T(8,128)S(1)} %kernel_terms.1), channel_id=1, replica_groups=mesh['grp'=2,'chip'=2,'core'=2,'gc'=4] {'chip','core','gc'}, dimensions={0} | all-to-all | bytes 131072 | tf_op jit(solution)/shard_map/all_to_all | solution.py:234
  35.4 0.1 fusion
  35.5 0.6 %pad_maximum_fusion = f32[32,32]{1,0:T(8,128)} fusion(f32[8,32]{1,0:T(8,128)S(1)} %get-tuple-element.14, f32[8,32]{1,0:T(8,128)S(1)} %get-tuple-element.15, f32[8,32]{1,0:T(8,128)S(1)} %get-tuple-element.16, f32[8,32]{1,0:T(8,128)S(1)} %get-tuple-element.13), kind=kLoop, calls=%fused_computation.1 | loop fusion | flops 3072 | bytes 8192 | tf_op jit(solution)/shard_map/concatenate | solution.py:235
  (3 shorter events, 0.1 us)
Async XLA Ops:
  0.0 5.3 %copy-start = (bf16[1024,1024]{1,0:T(8,128)(2,1)S(1)}, bf16[1024,1024]{1,0:T(8,128)(2,1)}, u32[]{:S(2)}) copy-start(bf16[1024,1024]{1,0:T(8,128)(2,1)} %own) | copy-start | bytes 6291460
  5.3 17.9 %collective-permute-start.1 = (bf16[1024,1024]{1,0:T(8,128)(2,1)S(1)}, bf16[1024,1024]{1,0:T(8,128)(2,1)}, u32[]{:S(2)}, u32[]{:S(2)}) collective-permute-start(bf16[1024,1024]{1,0:T(8,128)(2,1)S(1)} %copy-done), channel_id=1, source_target_pairs={{0,4},{4,0},{1,5},{5,1},{2,6},{6,2},{3,7},{7,3},{8,12},{12,8},{9,1... | collective-permute-start | bytes 6291464 | tf_op jit(solution)/shard_map/ppermute | solution.py:20
  5.9 17.2 %all-to-all-start = ((bf16[8,8,2048]{2,1,0:T(8,128)(2,1)}), bf16[8,8,2048]{2,1,0:T(8,128)(2,1)S(1)}, u32[]{:S(2)}, u32[]{:S(2)}) async-start(bf16[8,8,2048]{2,1,0:T(8,128)(2,1)} %gradient_pieces.1), calls=%async_computation | async-start | bytes 524288 | tf_op jit(solution)/shard_map/all_to_all | solution.py:205
  23.1 2.6 %collective-permute-start = (bf16[64,1024]{1,0:T(8,128)(2,1)S(1)}, bf16[64,1024]{1,0:T(8,128)(2,1)S(1)}, u32[]{:S(2)}, u32[]{:S(2)}) collective-permute-start(bf16[64,1024]{1,0:T(8,128)(2,1)S(1)} %slice.20), channel_id=1, source_target_pairs={{0,4},{4,0},{1,5},{5,1},{2,6},{6,2},{3,7},{7,3},{8,12},{12,8},{9,1... | collective-permute-start | bytes 393224 | tf_op jit(solution)/shard_map/ppermute | solution.py:20

commit v7 on v5

--- a/solution.py
+++ b/solution.py
@@ -10,6 +10,7 @@
 
 PLANE = ("chip", "gc")
 CHUNK = 1024
+PARTS = 2
 LIMIT = 107 * 2**19
 VMEM = pl.BlockSpec(memory_space=pltpu.VMEM)
 HBM = pl.BlockSpec(memory_space=pl.ANY)
@@ -30,7 +31,7 @@
     rank = w_in.shape[0]
     rows, width = act.shape
     steps = width // CHUNK
-    sides = ((act, w_in, act_v, in_v), (grad, w_out, grad_v, out_v))
+    sides = ((grad, w_out, grad_v, out_v), (act, w_in, act_v, in_v))
     copies = []
     for side, (x, w, x_v, w_v) in enumerate(sides):
         for step in range(steps):
@@ -43,8 +44,9 @@
             for copy in pair:
                 copy.start()
             copies.append(pair)
-    projected = []
-    for side, (x, w, x_v, w_v) in enumerate(sides):
+
+    def projected(side):
+        _, _, x_v, w_v = sides[side]
         total = jnp.zeros((rows, rank), jnp.float32)
         for step in range(steps):
             for copy in copies[side * steps + step]:
@@ -53,9 +55,9 @@
             total += lax.dot_general(
                 x_v[:, part], w_v[:, part], NT, preferred_element_type=jnp.float32
             )
-        projected.append(total)
-    both = jnp.concatenate(projected, axis=1).T.astype(out.dtype)
-    proj_act, proj_grad = both[:rank], both[rank:]
+        return total.astype(out.dtype)
+
+    proj_grad = projected(0)
     many = rank // 2 * seqs
     row = lax.broadcasted_iota(jnp.int32, (many, rank), 0)
     column = lax.broadcasted_iota(jnp.int32, (many, rank), 1)
@@ -64,8 +66,10 @@
     left = []
     for odd in range(2):
         pick = (column == row // seqs * 2 + odd).astype(jnp.float32).astype(out.dtype)
-        spread = jnp.dot(pick, proj_grad, preferred_element_type=jnp.float32)
+        spread = lax.dot_general(pick, proj_grad, NT, preferred_element_type=jnp.float32)
         left.append(jnp.where(token // length == sequence, spread, 0.0).astype(out.dtype))
+    left = jnp.concatenate(left, axis=1)
+    proj_act = projected(1)
     nothing = jnp.zeros_like(proj_act)
     right = jnp.concatenate(
         [
@@ -73,9 +77,7 @@
             jnp.concatenate([nothing, proj_act], axis=1),
         ]
     )
-    summed = lax.dot_general(
-        jnp.concatenate(left, axis=1), right, NT, preferred_element_type=jnp.float32
-    )
+    summed = jnp.dot(left, right, preferred_element_type=jnp.float32)
     summed = summed * (1.0 / math.sqrt(length))
     lanes = 2 * rank
     tiles = block // lanes
@@ -118,13 +120,22 @@
     )(activations.reshape(rows, width), out_grads.reshape(rows, width), w_in, w_out)
 
 
-def precond_kernel(block, weights, got, own, other, out):
+def precond_kernel(block, weights, got, own, other, out, other_v, sem):
+    step = block // PARTS
+    copies = []
+    for i in range(PARTS):
+        part = pl.ds(i * step, step)
+        copies.append(pltpu.make_async_copy(other.at[part], other_v.at[part], sem.at[i]))
+        copies[-1].start()
     left = got[:, :block].astype(jnp.float32)
     right = got[:, block:].astype(jnp.float32)
     for_own = (left * weights[0] + right * weights[1]).astype(got.dtype)
     for_other = (left * weights[2] + right * weights[3]).astype(got.dtype)
     total = jnp.dot(for_own, own[...], preferred_element_type=jnp.float32)
-    total += jnp.dot(for_other, other[...], preferred_element_type=jnp.float32)
+    for i in range(PARTS):
+        copies[i].wait()
+        part = slice(i * step, (i + 1) * step)
+        total += jnp.dot(for_other[:, part], other_v[part, :], preferred_element_type=jnp.float32)
     out[...] = total.astype(out.dtype)
 
 
@@ -134,8 +145,9 @@
     return pl.pallas_call(
         functools.partial(precond_kernel, block),
         out_shape=jax.ShapeDtypeStruct((rows, width), got.dtype),
-        in_specs=[pl.BlockSpec(memory_space=pltpu.SMEM)] + [VMEM] * 3,
+        in_specs=[pl.BlockSpec(memory_space=pltpu.SMEM), VMEM, VMEM, HBM],
         out_specs=VMEM,
+        scratch_shapes=[pltpu.VMEM(other.shape, other.dtype), pltpu.SemaphoreType.DMA((PARTS,))],
         compiler_params=pltpu.CompilerParams(vmem_limit_bytes=16 * 2**20),
         cost_estimate=pl.CostEstimate(
             flops=4 * rows * block * width, bytes_accessed=4 * block * width, transcendentals=0

time: 36.3 us -> 36.5 us (level)
  no operation moved by 1% of the time
where the time goes in v7:
time: 36.5 us; the launch traced here: 36.3 us
  waiting for transfers between devices  10.4 us (28%)
  blocking collectives  9.19 us (25%)
  Pallas kernels  8.41 us (23%)
  starting transfers between devices  7.34 us (20%)
  other arithmetic  0.74 us (2%)
    all_to_all x1, waiting for transfers between devices, per_device(): lax.all_to_all(pieces, PLANE, 0, 0, tiled=True).reshape(half, 2 * block)  10.4 us
    all_to_all x1, blocking collectives, per_device(): lax.all_to_all(terms, ('chip', 'core', 'gc'), 0, 0, tiled=True)  9.19 us
    all_to_all x1, starting transfers between devices, per_device(): lax.all_to_all(pieces, PLANE, 0, 0, tiled=True).reshape(half, 2 * block)  6.82 us
    pallas_call x1, Pallas kernels, gradient_pieces(): pl.pallas_call(functools.partial(rows_kernel, length, block, cols), out_s...  5.36 us
    pallas_call x1, Pallas kernels, precondition(): pl.pallas_call(functools.partial(precond_kernel, block), out_shape=jax.Sh...  2.65 us
  transfers between devices with their start and end apart: 3, of which 1 were waited for; matrix products, arithmetic and copies ran while one was open for 0% of the time, Pallas kernels for 22%

profile of v7, /device:TPU:0, one launch (start us, length us, event | category | flops | bytes accessed | tf_op | source)
XLA Modules:
  0.0 36.3 jit_solution(6100377568835136219)
XLA Ops:
  0.0 0.5 %collective-permute-start.1 = (bf16[1024,1024]{1,0:T(8,128)(2,1)}, bf16[1024,1024]{1,0:T(8,128)(2,1)}, u32[]{:S(2)}, u32[]{:S(2)}) collective-permute-start(bf16[1024,1024]{1,0:T(8,128)(2,1)} %own.1), channel_id=1, source_target_pairs={{0,4},{4,0},{1,5},{5,1},{2,6},{6,2},{3,7},{7,3},{8,12},{12,8},{9,1... | collective-permute-start | bytes 6291464 | tf_op jit(solution)/shard_map/ppermute | solution.py:21
  0.5 0.0 copy-start
  0.5 5.4 %gradient_pieces.1 = bf16[8,8,2048]{2,1,0:T(8,128)(2,1)} custom-call(bf16[256,4096]{1,0:T(8,128)(2,1)} %bitcast.20, bf16[256,4096]{1,0:T(8,128)(2,1)} %bitcast.21, bf16[64,4096]{1,0:T(8,128)(2,1)} %bitcast.23, bf16[64,4096]{1,0:T(8,128)(2,1)} %bitcast.24), custom_call_target="tpu_custom_call" | custom-call | flops 268435456 | bytes 5242880 | tf_op jit(solution)/shard_map/gradient_pieces/pallas_call | solution.py:102
  5.8 6.8 %all-to-all-start = ((bf16[8,8,2048]{2,1,0:T(8,128)(2,1)}), bf16[8,8,2048]{2,1,0:T(8,128)(2,1)S(1)}, u32[]{:S(2)}, u32[]{:S(2)}) async-start(bf16[8,8,2048]{2,1,0:T(8,128)(2,1)} %gradient_pieces.1), calls=%async_computation | async-start | bytes 524288 | tf_op jit(solution)/shard_map/all_to_all | solution.py:217
  12.6 10.4 %all-to-all-done = bf16[8,8,2048]{2,1,0:T(8,128)(2,1)S(1)} async-done(((bf16[8,8,2048]{2,1,0:T(8,128)(2,1)}), bf16[8,8,2048]{2,1,0:T(8,128)(2,1)S(1)}, u32[]{:S(2)}, u32[]{:S(2)}) %all-to-all-start) | async-done | bytes 262176 | tf_op jit(solution)/shard_map/all_to_all | solution.py:217
  23.1 0.1 collective-permute-start
  23.2 0.1 pad_maximum_fusion.1.weights
  23.3 0.0 collective-permute-done.1.other
  23.3 0.0 copy-done
  23.3 2.6 %precondition.1.precond = bf16[64,1024]{1,0:T(8,128)(2,1)S(1)} custom-call(f32[4]{0:T(128)S(1)} %pad_maximum_fusion.1.weights, bf16[64,2048]{1,0:T(8,128)(2,1)S(1)} %bitcast.18, bf16[1024,1024]{1,0:T(8,128)(2,1)S(1)} %copy-done, bf16[1024,1024]{1,0:T(8,128)(2,1)} %collective-permute-done.1.other), custom_call_target="tpu_custom_call" | custom-call | flops 268435456 | bytes 4194304 | tf_op jit(solution)/shard_map/precondition/pallas_call | solution.py:145
  25.9 0.0 collective-permute-done
  26.0 0.4 %kernel_terms.1 = f32[16,8,128]{2,1,0:T(8,128)S(1)} custom-call(s32[1]{0:T(128)} %bitcast.core, bf16[64,1024]{1,0:T(8,128)(2,1)S(1)} %precondition.1.precond, bf16[128,1024]{1,0:T(8,128)(2,1)S(1)} %bitcast.19), custom_call_target="tpu_custom_call" | custom-call | flops 33554432 | bytes 65536 | tf_op jit(solution)/shard_map/kernel_terms/pallas_call | solution.py:189
  26.4 9.2 %all_to_all.10 = f32[16,8,128]{2,1,0:T(8,128)S(1)} all-to-all(f32[16,8,128]{2,1,0:T(8,128)S(1)} %kernel_terms.1), channel_id=1, replica_groups=mesh['grp'=2,'chip'=2,'core'=2,'gc'=4] {'chip','core','gc'}, dimensions={0} | all-to-all | bytes 131072 | tf_op jit(solution)/shard_map/all_to_all | solution.py:246
  35.6 0.1 fusion
  35.7 0.6 %pad_maximum_fusion = f32[32,32]{1,0:T(8,128)} fusion(f32[8,32]{1,0:T(8,128)S(1)} %get-tuple-element.10, f32[8,32]{1,0:T(8,128)S(1)} %get-tuple-element.11, f32[8,32]{1,0:T(8,128)S(1)} %get-tuple-element.12, f32[8,32]{1,0:T(8,128)S(1)} %get-tuple-element.9), kind=kLoop, calls=%fused_computation.1 | loop fusion | flops 3072 | bytes 8192 | tf_op jit(solution)/shard_map/concatenate | solution.py:247
  (3 shorter events, 0.1 us)
Async XLA Ops:
  0.0 23.3 %collective-permute-start.1 = (bf16[1024,1024]{1,0:T(8,128)(2,1)}, bf16[1024,1024]{1,0:T(8,128)(2,1)}, u32[]{:S(2)}, u32[]{:S(2)}) collective-permute-start(bf16[1024,1024]{1,0:T(8,128)(2,1)} %own.1), channel_id=1, source_target_pairs={{0,4},{4,0},{1,5},{5,1},{2,6},{6,2},{3,7},{7,3},{8,12},{12,8},{9,1... | collective-permute-start | bytes 6291464 | tf_op jit(solution)/shard_map/ppermute | solution.py:21
  0.5 22.8 %copy-start = (bf16[1024,1024]{1,0:T(8,128)(2,1)S(1)}, bf16[1024,1024]{1,0:T(8,128)(2,1)}, u32[]{:S(2)}) copy-start(bf16[1024,1024]{1,0:T(8,128)(2,1)} %own.1) | copy-start | bytes 6291460
  5.8 17.3 %all-to-all-start = ((bf16[8,8,2048]{2,1,0:T(8,128)(2,1)}), bf16[8,8,2048]{2,1,0:T(8,128)(2,1)S(1)}, u32[]{:S(2)}, u32[]{:S(2)}) async-start(bf16[8,8,2048]{2,1,0:T(8,128)(2,1)} %gradient_pieces.1), calls=%async_computation | async-start | bytes 524288 | tf_op jit(solution)/shard_map/all_to_all | solution.py:217
  23.1 2.8 %collective-permute-start = (bf16[64,1024]{1,0:T(8,128)(2,1)S(1)}, bf16[64,1024]{1,0:T(8,128)(2,1)S(1)}, u32[]{:S(2)}, u32[]{:S(2)}) collective-permute-start(bf16[64,1024]{1,0:T(8,128)(2,1)S(1)} %slice.20), channel_id=1, source_target_pairs={{0,4},{4,0},{1,5},{5,1},{2,6},{6,2},{3,7},{7,3},{8,12},{12,8},{9,1... | collective-permute-start | bytes 393224 | tf_op jit(solution)/shard_map/ppermute | solution.py:21

commit v8 on v5

--- a/solution.py
+++ b/solution.py
@@ -25,37 +25,39 @@
     return jnp.where(chip < home, col % 2, 1 - col % 2)
 
 
-def rows_kernel(length, block, cols, act, grad, w_in, w_out, out, act_v, grad_v, in_v, out_v, w_sem, x_sem):
+def rows_kernel(length, block, cols, act, grad, w_in, w_out, out, x_v, w_v, w_sem, x_sem):
     seqs = out.shape[1]
     rank = w_in.shape[0]
     rows, width = act.shape
-    steps = width // CHUNK
-    sides = ((act, w_in, act_v, in_v), (grad, w_out, grad_v, out_v))
+    weights = [
+        pltpu.make_async_copy(w, w_v.at[pl.ds(side * rank, rank)], w_sem.at[side])
+        for side, w in enumerate((w_in, w_out))
+    ]
     copies = []
-    for side, (x, w, x_v, w_v) in enumerate(sides):
-        for step in range(steps):
-            part = pl.ds(step * CHUNK, CHUNK)
-            slot = side * steps + step
-            pair = (
-                pltpu.make_async_copy(w.at[:, part], w_v.at[:, part], w_sem.at[slot]),
-                pltpu.make_async_copy(x.at[:, part], x_v.at[:, part], x_sem.at[slot]),
-            )
-            for copy in pair:
-                copy.start()
-            copies.append(pair)
-    projected = []
-    for side, (x, w, x_v, w_v) in enumerate(sides):
-        total = jnp.zeros((rows, rank), jnp.float32)
-        for step in range(steps):
-            for copy in copies[side * steps + step]:
-                copy.wait()
-            part = pl.ds(step * CHUNK, CHUNK)
-            total += lax.dot_general(
-                x_v[:, part], w_v[:, part], NT, preferred_element_type=jnp.float32
-            )
-        projected.append(total)
-    both = jnp.concatenate(projected, axis=1).T.astype(out.dtype)
-    proj_act, proj_grad = both[:rank], both[rank:]
+    for step in range(width // CHUNK):
+        part = pl.ds(step * CHUNK, CHUNK)
+        copies.append(
+            [
+                pltpu.make_async_copy(
+                    x.at[:, part], x_v.at[pl.ds(side * rows, rows), part], x_sem.at[step, side]
+                )
+                for side, x in enumerate((act, grad))
+            ]
+        )
+    for copy in weights + sum(copies, []):
+        copy.start()
+    total = jnp.zeros((2 * rank, 2 * rows), jnp.float32)
+    for copy in weights:
+        copy.wait()
+    for step, pair in enumerate(copies):
+        for copy in pair:
+            copy.wait()
+        part = pl.ds(step * CHUNK, CHUNK)
+        total += lax.dot_general(
+            w_v[:, part], x_v[:, part], NT, preferred_element_type=jnp.float32
+        )
+    proj_act = total[:rank, :rows].astype(out.dtype)
+    proj_grad = total[rank:, rows:].astype(out.dtype)
     many = rank // 2 * seqs
     row = lax.broadcasted_iota(jnp.int32, (many, rank), 0)
     column = lax.broadcasted_iota(jnp.int32, (many, rank), 1)
@@ -96,23 +98,20 @@
     rank = w_in.shape[0]
     rows = seqs * length
     kind = activations.dtype
-    steps = 2 * width // CHUNK
     return pl.pallas_call(
         functools.partial(rows_kernel, length, block, cols),
         out_shape=jax.ShapeDtypeStruct((plane, seqs, 2 * block), kind),
         in_specs=[HBM] * 4,
         out_specs=VMEM,
         scratch_shapes=[
-            pltpu.VMEM((rows, width), kind),
-            pltpu.VMEM((rows, width), kind),
-            pltpu.VMEM((rank, width), kind),
-            pltpu.VMEM((rank, width), kind),
-            pltpu.SemaphoreType.DMA((steps,)),
-            pltpu.SemaphoreType.DMA((steps,)),
+            pltpu.VMEM((2 * rows, width), kind),
+            pltpu.VMEM((2 * rank, width), kind),
+            pltpu.SemaphoreType.DMA((2,)),
+            pltpu.SemaphoreType.DMA((width // CHUNK, 2)),
         ],
         compiler_params=pltpu.CompilerParams(vmem_limit_bytes=LIMIT),
         cost_estimate=pl.CostEstimate(
-            flops=4 * rows * width * rank, bytes_accessed=4 * (rows + rank) * width, transcendentals=0
+            flops=8 * rows * width * rank, bytes_accessed=4 * (rows + rank) * width, transcendentals=0
         ),
         name="gradient_pieces",
     )(activations.reshape(rows, width), out_grads.reshape(rows, width), w_in, w_out)

time: 36.3 us -> 36.5 us (level)
  no operation moved by 1% of the time
where the time goes in v8:
time: 36.5 us; the launch traced here: 36.2 us
  waiting for transfers between devices  10.4 us (28%)
  blocking collectives  9.19 us (25%)
  Pallas kernels  8.35 us (23%)
  starting transfers between devices  7.34 us (20%)
  other arithmetic  0.74 us (2%)
    all_to_all x1, waiting for transfers between devices, per_device(): lax.all_to_all(pieces, PLANE, 0, 0, tiled=True).reshape(half, 2 * block)  10.4 us
    all_to_all x1, blocking collectives, per_device(): lax.all_to_all(terms, ('chip', 'core', 'gc'), 0, 0, tiled=True)  9.19 us
    all_to_all x1, starting transfers between devices, per_device(): lax.all_to_all(pieces, PLANE, 0, 0, tiled=True).reshape(half, 2 * block)  6.82 us
    pallas_call x1, Pallas kernels, gradient_pieces(): pl.pallas_call(functools.partial(rows_kernel, length, block, cols), out_s...  5.5 us
    pallas_call x1, Pallas kernels, precondition(): pl.pallas_call(functools.partial(precond_kernel, block), out_shape=jax.Sh...  2.44 us
  transfers between devices with their start and end apart: 3, of which 1 were waited for; matrix products, arithmetic and copies ran while one was open for 0% of the time, Pallas kernels for 22%

profile of v8, /device:TPU:0, one launch (start us, length us, event | category | flops | bytes accessed | tf_op | source)
XLA Modules:
  0.0 36.2 jit_solution(18143520806138804512)
XLA Ops:
  0.0 0.5 %collective-permute-start.1 = (bf16[1024,1024]{1,0:T(8,128)(2,1)}, bf16[1024,1024]{1,0:T(8,128)(2,1)}, u32[]{:S(2)}, u32[]{:S(2)}) collective-permute-start(bf16[1024,1024]{1,0:T(8,128)(2,1)} %own.1), channel_id=1, source_target_pairs={{0,4},{4,0},{1,5},{5,1},{2,6},{6,2},{3,7},{7,3},{8,12},{12,8},{9,1... | collective-permute-start | bytes 6291464 | tf_op jit(solution)/shard_map/ppermute | solution.py:20
  0.5 0.0 copy-start
  0.5 5.5 %gradient_pieces.1 = bf16[8,8,2048]{2,1,0:T(8,128)(2,1)} custom-call(bf16[256,4096]{1,0:T(8,128)(2,1)} %bitcast.20, bf16[256,4096]{1,0:T(8,128)(2,1)} %bitcast.21, bf16[64,4096]{1,0:T(8,128)(2,1)} %bitcast.23, bf16[64,4096]{1,0:T(8,128)(2,1)} %bitcast.24), custom_call_target="tpu_custom_call" | custom-call | flops 536870912 | bytes 5242880 | tf_op jit(solution)/shard_map/gradient_pieces/pallas_call | solution.py:101
  6.0 6.8 %all-to-all-start = ((bf16[8,8,2048]{2,1,0:T(8,128)(2,1)}), bf16[8,8,2048]{2,1,0:T(8,128)(2,1)S(1)}, u32[]{:S(2)}, u32[]{:S(2)}) async-start(bf16[8,8,2048]{2,1,0:T(8,128)(2,1)} %gradient_pieces.1), calls=%async_computation | async-start | bytes 524288 | tf_op jit(solution)/shard_map/all_to_all | solution.py:204
  12.8 10.4 %all-to-all-done = bf16[8,8,2048]{2,1,0:T(8,128)(2,1)S(1)} async-done(((bf16[8,8,2048]{2,1,0:T(8,128)(2,1)}), bf16[8,8,2048]{2,1,0:T(8,128)(2,1)S(1)}, u32[]{:S(2)}, u32[]{:S(2)}) %all-to-all-start) | async-done | bytes 262176 | tf_op jit(solution)/shard_map/all_to_all | solution.py:204
  23.2 0.1 collective-permute-start
  23.3 0.1 pad_maximum_fusion.1.weights
  23.4 0.0 collective-permute-done.1.other
  23.4 0.0 copy-done
  23.4 2.4 %precondition.1.precond = bf16[64,1024]{1,0:T(8,128)(2,1)S(1)} custom-call(f32[4]{0:T(128)S(1)} %pad_maximum_fusion.1.weights, bf16[64,2048]{1,0:T(8,128)(2,1)S(1)} %bitcast.18, bf16[1024,1024]{1,0:T(8,128)(2,1)S(1)} %copy-done, bf16[1024,1024]{1,0:T(8,128)(2,1)} %collective-permute-done.1.other), custom_call_target="tpu_custom_call" | custom-call | flops 268435456 | bytes 4194304 | tf_op jit(solution)/shard_map/precondition/pallas_call | solution.py:133
  25.9 0.0 collective-permute-done
  25.9 0.4 %kernel_terms.1 = f32[16,8,128]{2,1,0:T(8,128)S(1)} custom-call(s32[1]{0:T(128)} %bitcast.core, bf16[64,1024]{1,0:T(8,128)(2,1)S(1)} %precondition.1.precond, bf16[128,1024]{1,0:T(8,128)(2,1)S(1)} %bitcast.19), custom_call_target="tpu_custom_call" | custom-call | flops 33554432 | bytes 65536 | tf_op jit(solution)/shard_map/kernel_terms/pallas_call | solution.py:176
  26.3 9.2 %all_to_all.10 = f32[16,8,128]{2,1,0:T(8,128)S(1)} all-to-all(f32[16,8,128]{2,1,0:T(8,128)S(1)} %kernel_terms.1), channel_id=1, replica_groups=mesh['grp'=2,'chip'=2,'core'=2,'gc'=4] {'chip','core','gc'}, dimensions={0} | all-to-all | bytes 131072 | tf_op jit(solution)/shard_map/all_to_all | solution.py:233
  35.5 0.1 fusion
  35.6 0.6 %pad_maximum_fusion = f32[32,32]{1,0:T(8,128)} fusion(f32[8,32]{1,0:T(8,128)S(1)} %get-tuple-element.10, f32[8,32]{1,0:T(8,128)S(1)} %get-tuple-element.11, f32[8,32]{1,0:T(8,128)S(1)} %get-tuple-element.12, f32[8,32]{1,0:T(8,128)S(1)} %get-tuple-element.9), kind=kLoop, calls=%fused_computation.1 | loop fusion | flops 3072 | bytes 8192 | tf_op jit(solution)/shard_map/concatenate | solution.py:234
  (3 shorter events, 0.1 us)
Async XLA Ops:
  0.0 23.4 %collective-permute-start.1 = (bf16[1024,1024]{1,0:T(8,128)(2,1)}, bf16[1024,1024]{1,0:T(8,128)(2,1)}, u32[]{:S(2)}, u32[]{:S(2)}) collective-permute-start(bf16[1024,1024]{1,0:T(8,128)(2,1)} %own.1), channel_id=1, source_target_pairs={{0,4},{4,0},{1,5},{5,1},{2,6},{6,2},{3,7},{7,3},{8,12},{12,8},{9,1... | collective-permute-start | bytes 6291464 | tf_op jit(solution)/shard_map/ppermute | solution.py:20
  0.5 22.9 %copy-start = (bf16[1024,1024]{1,0:T(8,128)(2,1)S(1)}, bf16[1024,1024]{1,0:T(8,128)(2,1)}, u32[]{:S(2)}) copy-start(bf16[1024,1024]{1,0:T(8,128)(2,1)} %own.1) | copy-start | bytes 6291460
  6.0 17.3 %all-to-all-start = ((bf16[8,8,2048]{2,1,0:T(8,128)(2,1)}), bf16[8,8,2048]{2,1,0:T(8,128)(2,1)S(1)}, u32[]{:S(2)}, u32[]{:S(2)}) async-start(bf16[8,8,2048]{2,1,0:T(8,128)(2,1)} %gradient_pieces.1), calls=%async_computation | async-start | bytes 524288 | tf_op jit(solution)/shard_map/all_to_all | solution.py:204
  23.2 2.6 %collective-permute-start = (bf16[64,1024]{1,0:T(8,128)(2,1)S(1)}, bf16[64,1024]{1,0:T(8,128)(2,1)S(1)}, u32[]{:S(2)}, u32[]{:S(2)}) collective-permute-start(bf16[64,1024]{1,0:T(8,128)(2,1)S(1)} %slice.20), channel_id=1, source_target_pairs={{0,4},{4,0},{1,5},{5,1},{2,6},{6,2},{3,7},{7,3},{8,12},{12,8},{9,1... | collective-permute-start | bytes 393224 | tf_op jit(solution)/shard_map/ppermute | solution.py:20

commit v9 on v5

--- a/solution.py
+++ b/solution.py
@@ -118,30 +118,60 @@
     )(activations.reshape(rows, width), out_grads.reshape(rows, width), w_in, w_out)
 
 
-def precond_kernel(block, weights, got, own, other, out):
-    left = got[:, :block].astype(jnp.float32)
-    right = got[:, block:].astype(jnp.float32)
-    for_own = (left * weights[0] + right * weights[1]).astype(got.dtype)
-    for_other = (left * weights[2] + right * weights[3]).astype(got.dtype)
-    total = jnp.dot(for_own, own[...], preferred_element_type=jnp.float32)
-    total += jnp.dot(for_other, other[...], preferred_element_type=jnp.float32)
-    out[...] = total.astype(out.dtype)
-
-
-def precondition(weights, got, own, other):
+def precond_kernel(case, got, own, other, out):
+    block = own.shape[0]
+    tile = min(256, block)
+    half = block // 2
+    left, right = got.at[:, :block], got.at[:, block:]
+
+    def product(lhs, rhs):
+        return jnp.dot(lhs, rhs, preferred_element_type=jnp.float32)
+
+    def whole(pair):
+        out[...] = product(left[...], pair[...]).astype(out.dtype)
+
+    def at_home(odd, diagonal, pair):
+        for start in range(0, block, tile):
+            lanes = slice(start, start + tile)
+            total = product(right[:, lanes] * 0.5, diagonal[lanes, lanes])
+            if start > 0:
+                total += product(right[:, :start], diagonal[:start, lanes])
+            if not odd:
+                total += product(left[:, :half], pair[:half, lanes])
+            elif start + tile > half:
+                skip = max(half - start, 0)
+                more = product(left[...], pair[:, start + skip : start + tile])
+                if skip > 0:
+                    more = jnp.concatenate([jnp.zeros((left.shape[0], skip), jnp.float32), more], axis=1)
+                total += more
+            out[:, lanes] = total.astype(out.dtype)
+
+    branches = [
+        functools.partial(whole, own),
+        functools.partial(whole, other),
+        functools.partial(at_home, False, own, other),
+        functools.partial(at_home, False, other, own),
+        functools.partial(at_home, True, own, other),
+        functools.partial(at_home, True, other, own),
+    ]
+    for i, branch in enumerate(branches):
+        pl.when(case[0] == i)(branch)
+
+
+def precondition(case, got, own, other):
     rows = got.shape[0]
     block, width = own.shape
     return pl.pallas_call(
-        functools.partial(precond_kernel, block),
+        precond_kernel,
         out_shape=jax.ShapeDtypeStruct((rows, width), got.dtype),
         in_specs=[pl.BlockSpec(memory_space=pltpu.SMEM)] + [VMEM] * 3,
         out_specs=VMEM,
         compiler_params=pltpu.CompilerParams(vmem_limit_bytes=16 * 2**20),
         cost_estimate=pl.CostEstimate(
-            flops=4 * rows * block * width, bytes_accessed=4 * block * width, transcendentals=0
+            flops=2 * rows * block * width, bytes_accessed=4 * block * width, transcendentals=0
         ),
         name="precondition",
-    )(weights, got, own, other)
+    )(case, got, own, other)
 
 
 def terms_kernel(n, fold, scale, core, precond, right, out):
@@ -207,19 +237,11 @@
     mine = got[:, block:]
     theirs = other_core(mine)
     home = col // 2 == chip
-    once = jnp.where(home & (col % 2 == 1), 0.0, 1.0)
-    again = jnp.where(home, 0.5, 0.0)
-    own_left = left_parity(chip, col) == core
-    weights = jnp.stack(
-        [
-            jnp.where(own_left, once, 0.0),
-            jnp.where(own_left, 0.0, again),
-            jnp.where(own_left, 0.0, once),
-            jnp.where(own_left, again, 0.0),
-        ]
-    ).astype(jnp.float32)
+    left_other = (left_parity(chip, col) != core).astype(jnp.int32)
+    diagonal_other = (col % 2 != core).astype(jnp.int32)
+    case = jnp.where(home, 2 + 2 * (col % 2) + diagonal_other, left_other).astype(jnp.int32)
     theirs, precond = lax.optimization_barrier(
-        (theirs, precondition(weights, got, inv_gram, inv_other))
+        (theirs, precondition(case.reshape(1), got, inv_gram, inv_other))
     )
     mine = mine.reshape(chips, 1, tall, block)
     theirs = theirs.reshape(chips, 1, tall, block)

time: 36.3 us -> 35 us (0.964)
  blocking collectives: 9.19 us -> 26.2 us
  waiting for transfers between devices: 10.4 us -> 0.01 us
  starting transfers between devices: 7.34 us -> 0.52 us
  Pallas kernels: 8.17 us -> 7.15 us
    all_to_all x0 -> x1, blocking collectives: none -> 17 us  [per_device(): lax.all_to_all(pieces, PLANE, 0, 0, tiled=True).reshape(half, 2 * block)]
    all_to_all x1 -> x0, waiting for transfers between devices: 10.4 us -> none  [per_device(): lax.all_to_all(pieces, PLANE, 0, 0, tiled=True).reshape(half, 2 * block)]
    all_to_all x1 -> x0, starting transfers between devices: 6.82 us -> none  [per_device(): lax.all_to_all(pieces, PLANE, 0, 0, tiled=True).reshape(half, 2 * block)]
    pallas_call x1, Pallas kernels: 5.32 us -> 4.61 us  [gradient_pieces(): pl.pallas_call(functools.partial(rows_kernel, length, block, cols), out_s...]
  transfers between devices with their start and end apart: 3 -> 2, of which waited for: 1 -> 0; matrix products, arithmetic and copies ran while one was open for 0% -> 0% of each run, Pallas kernels for 22% -> 19%
where the time goes in v9:
time: 35 us; the launch traced here: 34.8 us
  blocking collectives  26.2 us (75%)
  Pallas kernels  7.15 us (20%)
  other arithmetic  0.66 us (2%)
  starting transfers between devices  0.52 us (1%)
    all_to_all x1, blocking collectives, per_device(): lax.all_to_all(pieces, PLANE, 0, 0, tiled=True).reshape(half, 2 * block)  17 us
    all_to_all x1, blocking collectives, per_device(): lax.all_to_all(terms, ('chip', 'core', 'gc'), 0, 0, tiled=True)  9.19 us
    pallas_call x1, Pallas kernels, gradient_pieces(): pl.pallas_call(functools.partial(rows_kernel, length, block, cols), out_s...  4.61 us
    pallas_call x1, Pallas kernels, precondition(): pl.pallas_call(precond_kernel, out_shape=jax.ShapeDtypeStruct((rows, widt...  2.14 us
  transfers between devices with their start and end apart: 2, of which 0 were waited for; matrix products, arithmetic and copies ran while one was open for 0% of the time, Pallas kernels for 19%

profile of v9, /device:TPU:0, one launch (start us, length us, event | category | flops | bytes accessed | tf_op | source)
XLA Modules:
  0.0 34.8 jit_solution(15696229931649616345)
XLA Ops:
  0.0 0.5 %collective-permute-start.1 = (bf16[1024,1024]{1,0:T(8,128)(2,1)}, bf16[1024,1024]{1,0:T(8,128)(2,1)}, u32[]{:S(2)}, u32[]{:S(2)}) collective-permute-start(bf16[1024,1024]{1,0:T(8,128)(2,1)} %own.1), channel_id=1, source_target_pairs={{0,4},{4,0},{1,5},{5,1},{2,6},{6,2},{3,7},{7,3},{8,12},{12,8},{9,1... | collective-permute-start | bytes 6291464 | tf_op jit(solution)/shard_map/ppermute | solution.py:20
  0.5 0.0 copy-start
  0.5 4.6 %gradient_pieces.1 = bf16[8,8,2048]{2,1,0:T(8,128)(2,1)S(1)} custom-call(bf16[256,4096]{1,0:T(8,128)(2,1)} %bitcast.17, bf16[256,4096]{1,0:T(8,128)(2,1)} %bitcast.18, bf16[64,4096]{1,0:T(8,128)(2,1)} %bitcast.20, bf16[64,4096]{1,0:T(8,128)(2,1)} %bitcast.21), custom_call_target="tpu_custom_call" | custom-call | flops 268435456 | bytes 5242880 | tf_op jit(solution)/shard_map/gradient_pieces/pallas_call | solution.py:100
  5.1 17.0 %all_to_all.10 = bf16[8,8,2048]{2,1,0:T(8,128)(2,1)S(1)} all-to-all(bf16[8,8,2048]{2,1,0:T(8,128)(2,1)S(1)} %gradient_pieces.1), channel_id=1, replica_groups=mesh['grp'=2,'chip'=2,'core'=2,'gc'=4] {'chip','gc'}, dimensions={0} | all-to-all | bytes 524288 | tf_op jit(solution)/shard_map/all_to_all | solution.py:235
  22.1 0.1 collective-permute-start
  22.2 0.0 collective-permute-done.1.other
  22.3 0.0 copy-done
  22.3 2.1 %precondition.1.precond = bf16[64,1024]{1,0:T(8,128)(2,1)S(1)} custom-call(s32[1]{0:T(128)} %bitcast.6.case, bf16[64,2048]{1,0:T(8,128)(2,1)S(1)} %bitcast.15, bf16[1024,1024]{1,0:T(8,128)(2,1)S(1)} %copy-done, bf16[1024,1024]{1,0:T(8,128)(2,1)} %collective-permute-done.1.other), custom_call_target="tpu_custom_call" | custom-call | flops 134217728 | bytes 4194304 | tf_op jit(solution)/shard_map/precondition/pallas_call | solution.py:164
  24.4 0.0 collective-permute-done
  24.5 0.4 %kernel_terms.1 = f32[16,8,128]{2,1,0:T(8,128)S(1)} custom-call(s32[1]{0:T(128)} %bitcast.core, bf16[64,1024]{1,0:T(8,128)(2,1)S(1)} %precondition.1.precond, bf16[128,1024]{1,0:T(8,128)(2,1)S(1)} %bitcast.16), custom_call_target="tpu_custom_call" | custom-call | flops 33554432 | bytes 65536 | tf_op jit(solution)/shard_map/kernel_terms/pallas_call | solution.py:207
  24.9 9.2 %all_to_all.11 = f32[16,8,128]{2,1,0:T(8,128)S(1)} all-to-all(f32[16,8,128]{2,1,0:T(8,128)S(1)} %kernel_terms.1), channel_id=1, replica_groups=mesh['grp'=2,'chip'=2,'core'=2,'gc'=4] {'chip','core','gc'}, dimensions={0} | all-to-all | bytes 131072 | tf_op jit(solution)/shard_map/all_to_all | solution.py:256
  34.1 0.1 fusion
  34.2 0.6 %pad_maximum_fusion = f32[32,32]{1,0:T(8,128)} fusion(f32[8,32]{1,0:T(8,128)S(1)} %get-tuple-element.10, f32[8,32]{1,0:T(8,128)S(1)} %get-tuple-element.11, f32[8,32]{1,0:T(8,128)S(1)} %get-tuple-element.12, f32[8,32]{1,0:T(8,128)S(1)} %get-tuple-element.9), kind=kLoop, calls=%fused_computation.1 | loop fusion | flops 3072 | bytes 8192 | tf_op jit(solution)/shard_map/concatenate | solution.py:257
  (3 shorter events, 0.1 us)
Async XLA Ops:
  0.0 22.2 %collective-permute-start.1 = (bf16[1024,1024]{1,0:T(8,128)(2,1)}, bf16[1024,1024]{1,0:T(8,128)(2,1)}, u32[]{:S(2)}, u32[]{:S(2)}) collective-permute-start(bf16[1024,1024]{1,0:T(8,128)(2,1)} %own.1), channel_id=1, source_target_pairs={{0,4},{4,0},{1,5},{5,1},{2,6},{6,2},{3,7},{7,3},{8,12},{12,8},{9,1... | collective-permute-start | bytes 6291464 | tf_op jit(solution)/shard_map/ppermute | solution.py:20
  0.5 21.8 %copy-start = (bf16[1024,1024]{1,0:T(8,128)(2,1)S(1)}, bf16[1024,1024]{1,0:T(8,128)(2,1)}, u32[]{:S(2)}) copy-start(bf16[1024,1024]{1,0:T(8,128)(2,1)} %own.1) | copy-start | bytes 6291460
  22.1 2.3 %collective-permute-start = (bf16[64,1024]{1,0:T(8,128)(2,1)S(1)}, bf16[64,1024]{1,0:T(8,128)(2,1)S(1)}, u32[]{:S(2)}, u32[]{:S(2)}) collective-permute-start(bf16[64,1024]{1,0:T(8,128)(2,1)S(1)} %slice.20), channel_id=1, source_target_pairs={{0,4},{4,0},{1,5},{5,1},{2,6},{6,2},{3,7},{7,3},{8,12},{12,8},{9,1... | collective-permute-start | bytes 393224 | tf_op jit(solution)/shard_map/ppermute | solution.py:20

commit v10 on v9

--- a/solution.py
+++ b/solution.py
@@ -14,6 +14,11 @@
 VMEM = pl.BlockSpec(memory_space=pltpu.VMEM)
 HBM = pl.BlockSpec(memory_space=pl.ANY)
 NT = (((1,), (1,)), ((), ()))
+
+
+def exchange(value, axes, members):
+    order = [i ^ 1 for i in range(members)]
+    return lax.all_to_all(value, axes, 0, 0, axis_index_groups=[order], tiled=True)
 
 
 def other_core(value):
@@ -83,7 +88,7 @@
         summed[i * seqs : (i + 1) * seqs].astype(out.dtype) for i in range(many // seqs)
     ]
     for place in range(out.shape[0]):
-        chip, col = place // cols, place % cols
+        chip, col = (place ^ 1) // cols, (place ^ 1) % cols
         odd = col % 2 if chip < col // 2 else 1 - col % 2
         for slot, source in enumerate((2 * chip + odd, col)):
             for i in range(tiles):
@@ -188,10 +193,10 @@
         once = lax.dot_general(held, right[...], NT, preferred_element_type=jnp.float32) * scale
         turned = lax.dot_general(right[...], held, NT, preferred_element_type=jnp.float32) * scale
         for chip in range(count):
-            mine = 2 * (first + chip) + core[0]
+            mine, next_to = 2 * (first + chip) + core[0], 2 * (first + chip) + 1 - core[0]
             for place in range(n):
-                out[mine * n + place] += packed(once, chip, place)
-                out[place * n + mine] += packed(turned, place, chip)
+                out[mine * n + (place ^ 1)] += packed(once, chip, place)
+                out[place * n + next_to] += packed(turned, place, chip)
 
     out[...] = jnp.zeros_like(out)
     if chips <= 2:
@@ -232,7 +237,8 @@
     inv_other = other_core(inv_gram)
 
     pieces = gradient_pieces(plane, cols, block, activations, out_grads, proj_in.T, proj_out.T)
-    got = lax.all_to_all(pieces, PLANE, 0, 0, tiled=True).reshape(half, 2 * block)
+    got = exchange(pieces, PLANE, plane).reshape(plane // 2, 2, seqs, 2 * block)
+    got = jnp.concatenate([got[:, 1:], got[:, :1]], axis=1).reshape(half, 2 * block)
 
     mine = got[:, block:]
     theirs = other_core(mine)
@@ -253,7 +259,7 @@
 
     fold = max(1, 128 // tall)
     terms = kernel_terms(cols, fold, 8.0 / feat, core.reshape(1).astype(jnp.int32), precond, right)
-    total = jnp.sum(lax.all_to_all(terms, ("chip", "core", "gc"), 0, 0, tiled=True), axis=0)
+    total = jnp.sum(exchange(terms, ("chip", "core", "gc"), cols * cols), axis=0)
     return jnp.concatenate([total[:, i * tall : (i + 1) * tall] for i in range(fold)])
 
 

time: 35 us -> 33.4 us (0.954)
  blocking collectives: 26.2 us -> 24.6 us
    all_to_all x2, blocking collectives: 26.2 us -> 24.6 us  [exchange(): lax.all_to_all(value, axes, 0, 0, axis_index_groups=[order], tiled=True)]
  transfers between devices with their start and end apart: 2 -> 2, of which waited for: 0 -> 0; matrix products, arithmetic and copies ran while one was open for 0% -> 0% of each run, Pallas kernels for 19% -> 20%
where the time goes in v10:
time: 33.4 us; the launch traced here: 33.2 us
  blocking collectives  24.6 us (74%)
  Pallas kernels  7.15 us (21%)
  other arithmetic  0.69 us (2%)
  starting transfers between devices  0.52 us (2%)
    all_to_all x2, blocking collectives, exchange(): lax.all_to_all(value, axes, 0, 0, axis_index_groups=[order], tiled=True)  24.6 us
    pallas_call x1, Pallas kernels, gradient_pieces(): pl.pallas_call(functools.partial(rows_kernel, length, block, cols), out_s...  4.61 us
    pallas_call x1, Pallas kernels, precondition(): pl.pallas_call(precond_kernel, out_shape=jax.ShapeDtypeStruct((rows, widt...  2.14 us
  transfers between devices with their start and end apart: 2, of which 0 were waited for; matrix products, arithmetic and copies ran while one was open for 0% of the time, Pallas kernels for 20%

profile of v10, /device:TPU:0, one launch (start us, length us, event | category | flops | bytes accessed | tf_op | source)
XLA Modules:
  0.0 33.2 jit_solution(13171931412162910800)
XLA Ops:
  0.0 0.5 %collective-permute-start.1 = (bf16[1024,1024]{1,0:T(8,128)(2,1)}, bf16[1024,1024]{1,0:T(8,128)(2,1)}, u32[]{:S(2)}, u32[]{:S(2)}) collective-permute-start(bf16[1024,1024]{1,0:T(8,128)(2,1)} %own.1), channel_id=1, source_target_pairs={{0,4},{4,0},{1,5},{5,1},{2,6},{6,2},{3,7},{7,3},{8,12},{12,8},{9,1... | collective-permute-start | bytes 6291464 | tf_op jit(solution)/shard_map/ppermute | solution.py:25
  0.5 0.0 copy-start
  0.5 4.6 %gradient_pieces.1 = bf16[8,8,2048]{2,1,0:T(8,128)(2,1)S(1)} custom-call(bf16[256,4096]{1,0:T(8,128)(2,1)} %bitcast.18, bf16[256,4096]{1,0:T(8,128)(2,1)} %bitcast.19, bf16[64,4096]{1,0:T(8,128)(2,1)} %bitcast.22, bf16[64,4096]{1,0:T(8,128)(2,1)} %bitcast.23), custom_call_target="tpu_custom_call" | custom-call | flops 268435456 | bytes 5242880 | tf_op jit(solution)/shard_map/gradient_pieces/pallas_call | solution.py:105
  5.1 15.4 %all_to_all.10 = bf16[8,8,2048]{2,1,0:T(8,128)(2,1)S(1)} all-to-all(bf16[8,8,2048]{2,1,0:T(8,128)(2,1)S(1)} %gradient_pieces.1), channel_id=1, replica_groups={{1,0,3,2,9,8,11,10},{5,4,7,6,13,12,15,14},{17,16,19,18,25,24,27,26},{21..., dimensions={0} | all-to-all | bytes 524288 | tf_op jit(solution)/shard_map/all_to_all | solution.py:21
  20.6 0.1 collective-permute-start
  20.7 0.0 collective-permute-done.1.other
  20.7 0.0 copy-done
  20.7 2.1 %precondition.1.precond = bf16[64,1024]{1,0:T(8,128)(2,1)S(1)} custom-call(s32[1]{0:T(128)} %bitcast.7.case, bf16[64,2048]{1,0:T(8,128)(2,1)S(1)} %bitcast.16, bf16[1024,1024]{1,0:T(8,128)(2,1)S(1)} %copy-done, bf16[1024,1024]{1,0:T(8,128)(2,1)} %collective-permute-done.1.other), custom_call_target="tpu_custom_call" | custom-call | flops 134217728 | bytes 4194304 | tf_op jit(solution)/shard_map/precondition/pallas_call | solution.py:169
  22.9 0.0 collective-permute-done
  22.9 0.4 %kernel_terms.1 = f32[16,8,128]{2,1,0:T(8,128)S(1)} custom-call(s32[1]{0:T(128)} %bitcast.core, bf16[64,1024]{1,0:T(8,128)(2,1)S(1)} %precondition.1.precond, bf16[128,1024]{1,0:T(8,128)(2,1)S(1)} %bitcast.17), custom_call_target="tpu_custom_call" | custom-call | flops 33554432 | bytes 65536 | tf_op jit(solution)/shard_map/kernel_terms/pallas_call | solution.py:212
  23.3 9.2 %all_to_all.11 = f32[16,8,128]{2,1,0:T(8,128)S(1)} all-to-all(f32[16,8,128]{2,1,0:T(8,128)S(1)} %kernel_terms.1), channel_id=1, replica_groups={{1,0,3,2,5,4,7,6,9,8,11,10,13,12,15,14},{17,16,19,18,21,20,23,22,25,24,..., dimensions={0} | all-to-all | bytes 131072 | tf_op jit(solution)/shard_map/all_to_all | solution.py:21
  32.5 0.1 fusion.1
  32.6 0.6 %pad_maximum_fusion.1 = f32[32,32]{1,0:T(8,128)} fusion(f32[8,32]{1,0:T(8,128)S(1)} %get-tuple-element.12, f32[8,32]{1,0:T(8,128)S(1)} %get-tuple-element.13, f32[8,32]{1,0:T(8,128)S(1)} %get-tuple-element.14, f32[8,32]{1,0:T(8,128)S(1)} %get-tuple-element.11), kind=kLoop, calls=%fused_computation.2 | loop fusion | flops 3072 | bytes 8192 | tf_op jit(solution)/shard_map/concatenate | solution.py:263
  (5 shorter events, 0.1 us)
Async XLA Ops:
  0.0 20.7 %collective-permute-start.1 = (bf16[1024,1024]{1,0:T(8,128)(2,1)}, bf16[1024,1024]{1,0:T(8,128)(2,1)}, u32[]{:S(2)}, u32[]{:S(2)}) collective-permute-start(bf16[1024,1024]{1,0:T(8,128)(2,1)} %own.1), channel_id=1, source_target_pairs={{0,4},{4,0},{1,5},{5,1},{2,6},{6,2},{3,7},{7,3},{8,12},{12,8},{9,1... | collective-permute-start | bytes 6291464 | tf_op jit(solution)/shard_map/ppermute | solution.py:25
  0.5 20.3 %copy-start = (bf16[1024,1024]{1,0:T(8,128)(2,1)S(1)}, bf16[1024,1024]{1,0:T(8,128)(2,1)}, u32[]{:S(2)}) copy-start(bf16[1024,1024]{1,0:T(8,128)(2,1)} %own.1) | copy-start | bytes 6291460
  20.6 2.3 %collective-permute-start = (bf16[64,1024]{1,0:T(8,128)(2,1)S(1)}, bf16[64,1024]{1,0:T(8,128)(2,1)S(1)}, u32[]{:S(2)}, u32[]{:S(2)}) collective-permute-start(bf16[64,1024]{1,0:T(8,128)(2,1)S(1)} %slice.30), channel_id=1, source_target_pairs={{0,4},{4,0},{1,5},{5,1},{2,6},{6,2},{3,7},{7,3},{8,12},{12,8},{9,1... | collective-permute-start | bytes 393224 | tf_op jit(solution)/shard_map/ppermute | solution.py:25

commit v11 on v10

--- a/solution.py
+++ b/solution.py
@@ -16,9 +16,13 @@
 NT = (((1,), (1,)), ((), ()))
 
 
-def exchange(value, axes, members):
-    order = [i ^ 1 for i in range(members)]
+def exchange(value, axes, members, first):
+    order = [i ^ first for i in range(members)]
     return lax.all_to_all(value, axes, 0, 0, axis_index_groups=[order], tiled=True)
+
+
+def leader(chips, cols):
+    return chips // 2 * cols + cols // 2
 
 
 def other_core(value):
@@ -88,7 +92,8 @@
         summed[i * seqs : (i + 1) * seqs].astype(out.dtype) for i in range(many // seqs)
     ]
     for place in range(out.shape[0]):
-        chip, col = (place ^ 1) // cols, (place ^ 1) % cols
+        member = place ^ leader(out.shape[0] // cols, cols)
+        chip, col = member // cols, member % cols
         odd = col % 2 if chip < col // 2 else 1 - col % 2
         for slot, source in enumerate((2 * chip + odd, col)):
             for i in range(tiles):
@@ -237,8 +242,9 @@
     inv_other = other_core(inv_gram)
 
     pieces = gradient_pieces(plane, cols, block, activations, out_grads, proj_in.T, proj_out.T)
-    got = exchange(pieces, PLANE, plane).reshape(plane // 2, 2, seqs, 2 * block)
-    got = jnp.concatenate([got[:, 1:], got[:, :1]], axis=1).reshape(half, 2 * block)
+    first = leader(chips, cols)
+    got = exchange(pieces, PLANE, plane, first)
+    got = jnp.concatenate([got[i ^ first] for i in range(plane)])
 
     mine = got[:, block:]
     theirs = other_core(mine)
@@ -259,7 +265,7 @@
 
     fold = max(1, 128 // tall)
     terms = kernel_terms(cols, fold, 8.0 / feat, core.reshape(1).astype(jnp.int32), precond, right)
-    total = jnp.sum(exchange(terms, ("chip", "core", "gc"), cols * cols), axis=0)
+    total = jnp.sum(exchange(terms, ("chip", "core", "gc"), cols * cols, 1), axis=0)
     return jnp.concatenate([total[:, i * tall : (i + 1) * tall] for i in range(fold)])
 
 

time: 33.4 us -> 33.8 us (1.012)
  blocking collectives: 24.6 us -> 9.57 us
  starting transfers between devices: 0.52 us -> 8.39 us
  waiting for transfers between devices: 0.01 us -> 6.78 us
  Pallas kernels: 7.15 us -> 7.87 us
    all_to_all x2 -> x1, blocking collectives: 24.6 us -> 9.57 us  [exchange(): lax.all_to_all(value, axes, 0, 0, axis_index_groups=[order], tiled=True)]
    all_to_all x0 -> x1, starting transfers between devices: none -> 8.32 us  [exchange(): lax.all_to_all(value, axes, 0, 0, axis_index_groups=[order], tiled=True)]
    all_to_all x0 -> x1, waiting for transfers between devices: none -> 6.77 us  [exchange(): lax.all_to_all(value, axes, 0, 0, axis_index_groups=[order], tiled=True)]
    pallas_call x1, Pallas kernels: 4.61 us -> 5.33 us  [gradient_pieces(): pl.pallas_call(functools.partial(rows_kernel, length, block, cols), out_s...]
    ppermute x2, starting transfers between devices: 0.52 us -> 0.07 us  [other_core(): return lax.ppermute(value, 'core', [(0, 1), (1, 0)])]
  transfers between devices with their start and end apart: 2 -> 3, of which waited for: 0 -> 1; matrix products, arithmetic and copies ran while one was open for 0% -> 0% of each run, Pallas kernels for 20% -> 6%
where the time goes in v11:
time: 33.8 us; the launch traced here: 33.5 us
  blocking collectives  9.57 us (28%)
  starting transfers between devices  8.39 us (25%)
  Pallas kernels  7.87 us (23%)
  waiting for transfers between devices  6.78 us (20%)
  other arithmetic  0.66 us (2%)
    all_to_all x1, blocking collectives, exchange(): lax.all_to_all(value, axes, 0, 0, axis_index_groups=[order], tiled=True)  9.57 us
    all_to_all x1, starting transfers between devices, exchange(): lax.all_to_all(value, axes, 0, 0, axis_index_groups=[order], tiled=True)  8.32 us
    all_to_all x1, waiting for transfers between devices, exchange(): lax.all_to_all(value, axes, 0, 0, axis_index_groups=[order], tiled=True)  6.77 us
    pallas_call x1, Pallas kernels, gradient_pieces(): pl.pallas_call(functools.partial(rows_kernel, length, block, cols), out_s...  5.33 us
    pallas_call x1, Pallas kernels, precondition(): pl.pallas_call(precond_kernel, out_shape=jax.ShapeDtypeStruct((rows, widt...  2.14 us
  transfers between devices with their start and end apart: 3, of which 1 were waited for; matrix products, arithmetic and copies ran while one was open for 0% of the time, Pallas kernels for 6%

profile of v11, /device:TPU:0, one launch (start us, length us, event | category | flops | bytes accessed | tf_op | source)
XLA Modules:
  0.0 33.5 jit_solution(3083350466026843143)
XLA Ops:
  0.0 0.0 copy-start
  0.0 5.3 %gradient_pieces.1 = bf16[8,8,2048]{2,1,0:T(8,128)(2,1)} custom-call(bf16[256,4096]{1,0:T(8,128)(2,1)} %bitcast.46, bf16[256,4096]{1,0:T(8,128)(2,1)} %bitcast.47, bf16[64,4096]{1,0:T(8,128)(2,1)} %bitcast.49, bf16[64,4096]{1,0:T(8,128)(2,1)} %bitcast.50), custom_call_target="tpu_custom_call" | custom-call | flops 268435456 | bytes 5242880 | tf_op jit(solution)/shard_map/gradient_pieces/pallas_call | solution.py:110
  5.3 8.3 %all-to-all-start = ((bf16[8,8,2048]{2,1,0:T(8,128)(2,1)}), bf16[8,8,2048]{2,1,0:T(8,128)(2,1)S(1)}, u32[]{:S(2)}, u32[]{:S(2)}) async-start(bf16[8,8,2048]{2,1,0:T(8,128)(2,1)} %gradient_pieces.1), calls=%async_computation | async-start | bytes 524288 | tf_op jit(solution)/shard_map/all_to_all | solution.py:21
  13.7 0.0 copy-done
  13.7 0.0 collective-permute-start.1
  13.7 6.8 %all-to-all-done = bf16[8,8,2048]{2,1,0:T(8,128)(2,1)S(1)} async-done(((bf16[8,8,2048]{2,1,0:T(8,128)(2,1)}), bf16[8,8,2048]{2,1,0:T(8,128)(2,1)S(1)}, u32[]{:S(2)}, u32[]{:S(2)}) %all-to-all-start) | async-done | bytes 262176 | tf_op jit(solution)/shard_map/all_to_all | solution.py:21
  20.5 0.1 collective-permute-start
  20.7 0.0 collective-permute-done.1.other
  20.7 2.1 %precondition.1.precond = bf16[64,1024]{1,0:T(8,128)(2,1)S(1)} custom-call(s32[1]{0:T(128)} %bitcast.13.case, bf16[64,2048]{1,0:T(8,128)(2,1)S(1)} %fusion.got, bf16[1024,1024]{1,0:T(8,128)(2,1)S(1)} %copy-done, bf16[1024,1024]{1,0:T(8,128)(2,1)} %collective-permute-done.1.other), custom_call_target="tpu_custom_call" | custom-call | flops 134217728 | bytes 4194304 | tf_op jit(solution)/shard_map/precondition/pallas_call | solution.py:174
  22.8 0.0 collective-permute-done
  22.9 0.4 %kernel_terms.1 = f32[16,8,128]{2,1,0:T(8,128)S(1)} custom-call(s32[1]{0:T(128)} %bitcast.core, bf16[64,1024]{1,0:T(8,128)(2,1)S(1)} %precondition.1.precond, bf16[128,1024]{1,0:T(8,128)(2,1)S(1)} %bitcast.45), custom_call_target="tpu_custom_call" | custom-call | flops 33554432 | bytes 65536 | tf_op jit(solution)/shard_map/kernel_terms/pallas_call | solution.py:217
  23.3 9.6 %all_to_all.10 = f32[16,8,128]{2,1,0:T(8,128)S(1)} all-to-all(f32[16,8,128]{2,1,0:T(8,128)S(1)} %kernel_terms.1), channel_id=1, replica_groups={{1,0,3,2,5,4,7,6,9,8,11,10,13,12,15,14},{17,16,19,18,21,20,23,22,25,24,..., dimensions={0} | all-to-all | bytes 131072 | tf_op jit(solution)/shard_map/all_to_all | solution.py:21
  32.9 0.1 fusion.8
  32.9 0.6 %pad_maximum_fusion = f32[32,32]{1,0:T(8,128)} fusion(f32[8,32]{1,0:T(8,128)S(1)} %get-tuple-element.10, f32[8,32]{1,0:T(8,128)S(1)} %get-tuple-element.11, f32[8,32]{1,0:T(8,128)S(1)} %get-tuple-element.12, f32[8,32]{1,0:T(8,128)S(1)} %get-tuple-element.9), kind=kLoop, calls=%fused_computation.17 | loop fusion | flops 3072 | bytes 8192 | tf_op jit(solution)/shard_map/concatenate | solution.py:269
  (11 shorter events, 0.1 us)
Async XLA Ops:
  0.0 13.7 %copy-start = (bf16[1024,1024]{1,0:T(8,128)(2,1)S(1)}, bf16[1024,1024]{1,0:T(8,128)(2,1)}, u32[]{:S(2)}) copy-start(bf16[1024,1024]{1,0:T(8,128)(2,1)} %own.1) | copy-start | bytes 6291460
  5.3 15.1 %all-to-all-start = ((bf16[8,8,2048]{2,1,0:T(8,128)(2,1)}), bf16[8,8,2048]{2,1,0:T(8,128)(2,1)S(1)}, u32[]{:S(2)}, u32[]{:S(2)}) async-start(bf16[8,8,2048]{2,1,0:T(8,128)(2,1)} %gradient_pieces.1), calls=%async_computation | async-start | bytes 524288 | tf_op jit(solution)/shard_map/all_to_all | solution.py:21
  13.7 7.0 %collective-permute-start.1 = (bf16[1024,1024]{1,0:T(8,128)(2,1)S(1)}, bf16[1024,1024]{1,0:T(8,128)(2,1)}, u32[]{:S(2)}, u32[]{:S(2)}) collective-permute-start(bf16[1024,1024]{1,0:T(8,128)(2,1)S(1)} %copy-done), channel_id=1, source_target_pairs={{0,4},{4,0},{1,5},{5,1},{2,6},{6,2},{3,7},{7,3},{8,12},{12,8},{9,1... | collective-permute-start | bytes 6291464 | tf_op jit(solution)/shard_map/ppermute | solution.py:29
  20.5 2.3 %collective-permute-start = (bf16[64,1024]{1,0:T(8,128)(2,1)S(1)}, bf16[64,1024]{1,0:T(8,128)(2,1)S(1)}, u32[]{:S(2)}, u32[]{:S(2)}) collective-permute-start(bf16[64,1024]{1,0:T(8,128)(2,1)S(1)} %slice.60), channel_id=1, source_target_pairs={{0,4},{4,0},{1,5},{5,1},{2,6},{6,2},{3,7},{7,3},{8,12},{12,8},{9,1... | collective-permute-start | bytes 393224 | tf_op jit(solution)/shard_map/ppermute | solution.py:29

commit v12 on v11

--- a/solution.py
+++ b/solution.py
@@ -242,6 +242,7 @@
     inv_other = other_core(inv_gram)
 
     pieces = gradient_pieces(plane, cols, block, activations, out_grads, proj_in.T, proj_out.T)
+    pieces, inv_other = lax.optimization_barrier((pieces, inv_other))
     first = leader(chips, cols)
     got = exchange(pieces, PLANE, plane, first)
     got = jnp.concatenate([got[i ^ first] for i in range(plane)])

time: 33.8 us -> 34 us (level)
  blocking collectives: 9.57 us -> 23.9 us
  starting transfers between devices: 8.39 us -> 0.52 us
  waiting for transfers between devices: 6.78 us -> 0.01 us
  local copies, waits for them, and re-layouts: 0.12 us -> 3.03 us
  Pallas kernels: 7.87 us -> 5.58 us
    all_to_all x1 -> x2, blocking collectives: 9.57 us -> 23.9 us  [exchange(): lax.all_to_all(value, axes, 0, 0, axis_index_groups=[order], tiled=True)]
    all_to_all x1 -> x0, starting transfers between devices: 8.32 us -> none  [exchange(): lax.all_to_all(value, axes, 0, 0, axis_index_groups=[order], tiled=True)]
    all_to_all x1 -> x0, waiting for transfers between devices: 6.77 us -> none  [exchange(): lax.all_to_all(value, axes, 0, 0, axis_index_groups=[order], tiled=True)]
    unnamed x9 -> x13, local copies, waits for them, and re-layouts: 0.03 us -> 2.94 us
    pallas_call x1, Pallas kernels: 2.14 us -> 0.57 us  [precondition(): pl.pallas_call(precond_kernel, out_shape=jax.ShapeDtypeStruct((rows, widt...]
    pallas_call x1, Pallas kernels: 5.33 us -> 4.61 us  [gradient_pieces(): pl.pallas_call(functools.partial(rows_kernel, length, block, cols), out_s...]
    ppermute x2, starting transfers between devices: 0.07 us -> 0.52 us  [other_core(): return lax.ppermute(value, 'core', [(0, 1), (1, 0)])]
  transfers between devices with their start and end apart: 3 -> 2, of which waited for: 1 -> 0; matrix products, arithmetic and copies ran while one was open for 0% -> 0% of each run, Pallas kernels for 6% -> 15%
where the time goes in v12:
time: 34 us; the launch traced here: 33.8 us
  blocking collectives  23.9 us (70%)
  Pallas kernels  5.58 us (16%)
  local copies, waits for them, and re-layouts  3.03 us (9%)
  other arithmetic  0.66 us (2%)
  starting transfers between devices  0.52 us (2%)
    all_to_all x2, blocking collectives, exchange(): lax.all_to_all(value, axes, 0, 0, axis_index_groups=[order], tiled=True)  23.9 us
    pallas_call x1, Pallas kernels, gradient_pieces(): pl.pallas_call(functools.partial(rows_kernel, length, block, cols), out_s...  4.61 us
    unnamed x13, local copies, waits for them, and re-layouts  2.94 us
  transfers between devices with their start and end apart: 2, of which 0 were waited for; matrix products, arithmetic and copies ran while one was open for 0% of the time, Pallas kernels for 15%

profile of v12, /device:TPU:0, one launch (start us, length us, event | category | flops | bytes accessed | tf_op | source)
XLA Modules:
  0.0 33.8 jit_solution(9782303921439979133)
XLA Ops:
  0.0 0.5 %collective-permute-start = (bf16[1024,1024]{1,0:T(8,128)(2,1)}, bf16[1024,1024]{1,0:T(8,128)(2,1)S(1)}, u32[]{:S(2)}, u32[]{:S(2)}) collective-permute-start(bf16[1024,1024]{1,0:T(8,128)(2,1)} %own.1), channel_id=1, source_target_pairs={{0,4},{4,0},{1,5},{5,1},{2,6},{6,2},{3,7},{7,3},{8,12},{12,8},{9,1... | collective-permute-start | bytes 6291464 | tf_op jit(solution)/shard_map/ppermute | solution.py:29
  0.5 0.0 copy-start
  0.5 4.6 %gradient_pieces.1 = bf16[8,8,2048]{2,1,0:T(8,128)(2,1)S(1)} custom-call(bf16[256,4096]{1,0:T(8,128)(2,1)} %bitcast.46, bf16[256,4096]{1,0:T(8,128)(2,1)} %bitcast.47, bf16[64,4096]{1,0:T(8,128)(2,1)} %bitcast.49, bf16[64,4096]{1,0:T(8,128)(2,1)} %bitcast.50), custom_call_target="tpu_custom_call" | custom-call | flops 268435456 | bytes 5242880 | tf_op jit(solution)/shard_map/gradient_pieces/pallas_call | solution.py:110
  5.1 0.0 collective-permute-done.other
  5.1 0.0 copy-start.1
  5.1 1.3 %copy-done.1 = bf16[1024,1024]{1,0:T(8,128)(2,1)} copy-done((bf16[1024,1024]{1,0:T(8,128)(2,1)}, bf16[1024,1024]{1,0:T(8,128)(2,1)S(1)}, u32[]{:S(2)}) %copy-start.1) | copy-done | bytes 2097176
  6.4 14.4 %all_to_all.10 = bf16[8,8,2048]{2,1,0:T(8,128)(2,1)S(1)} all-to-all(bf16[8,8,2048]{2,1,0:T(8,128)(2,1)S(1)} %gradient_pieces.1), channel_id=1, replica_groups={{10,11,8,9,2,3,0,1},{14,15,12,13,6,7,4,5},{26,27,24,25,18,19,16,17},{30..., dimensions={0} | all-to-all | bytes 524288 | tf_op jit(solution)/shard_map/all_to_all | solution.py:21
  20.9 0.1 collective-permute-start.1
  21.0 0.0 copy-done
  21.0 0.0 copy-start.2
  21.0 1.6 %copy-done.2 = bf16[1024,1024]{1,0:T(8,128)(2,1)S(1)} copy-done((bf16[1024,1024]{1,0:T(8,128)(2,1)S(1)}, bf16[1024,1024]{1,0:T(8,128)(2,1)}, u32[]{:S(2)}) %copy-start.2) | copy-done | bytes 2097176
  22.6 0.6 %precondition.1.precond = bf16[64,1024]{1,0:T(8,128)(2,1)S(1)} custom-call(s32[1]{0:T(128)} %bitcast.13.case, bf16[64,2048]{1,0:T(8,128)(2,1)S(1)} %fusion.got, bf16[1024,1024]{1,0:T(8,128)(2,1)S(1)} %copy-done, bf16[1024,1024]{1,0:T(8,128)(2,1)S(1)} %copy-done.2), custom_call_target="tpu_custom_call" | custom-call | flops 134217728 | bytes 4194304 | tf_op jit(solution)/shard_map/precondition/pallas_call | solution.py:174
  23.2 0.0 collective-permute-done.1
  23.2 0.4 %kernel_terms.1 = f32[16,8,128]{2,1,0:T(8,128)S(1)} custom-call(s32[1]{0:T(128)} %bitcast.core, bf16[64,1024]{1,0:T(8,128)(2,1)S(1)} %precondition.1.precond, bf16[128,1024]{1,0:T(8,128)(2,1)S(1)} %bitcast.45), custom_call_target="tpu_custom_call" | custom-call | flops 33554432 | bytes 65536 | tf_op jit(solution)/shard_map/kernel_terms/pallas_call | solution.py:217
  23.6 9.5 %all_to_all.11 = f32[16,8,128]{2,1,0:T(8,128)S(1)} all-to-all(f32[16,8,128]{2,1,0:T(8,128)S(1)} %kernel_terms.1), channel_id=1, replica_groups={{1,0,3,2,5,4,7,6,9,8,11,10,13,12,15,14},{17,16,19,18,21,20,23,22,25,24,..., dimensions={0} | all-to-all | bytes 131072 | tf_op jit(solution)/shard_map/all_to_all | solution.py:21
  33.1 0.1 fusion.8
  33.2 0.6 %pad_maximum_fusion = f32[32,32]{1,0:T(8,128)} fusion(f32[8,32]{1,0:T(8,128)S(1)} %get-tuple-element.14, f32[8,32]{1,0:T(8,128)S(1)} %get-tuple-element.15, f32[8,32]{1,0:T(8,128)S(1)} %get-tuple-element.16, f32[8,32]{1,0:T(8,128)S(1)} %get-tuple-element.13), kind=kLoop, calls=%fused_computation.17 | loop fusion | flops 3072 | bytes 8192 | tf_op jit(solution)/shard_map/concatenate | solution.py:270
  (11 shorter events, 0.1 us)
Async XLA Ops:
  0.0 5.1 %collective-permute-start = (bf16[1024,1024]{1,0:T(8,128)(2,1)}, bf16[1024,1024]{1,0:T(8,128)(2,1)S(1)}, u32[]{:S(2)}, u32[]{:S(2)}) collective-permute-start(bf16[1024,1024]{1,0:T(8,128)(2,1)} %own.1), channel_id=1, source_target_pairs={{0,4},{4,0},{1,5},{5,1},{2,6},{6,2},{3,7},{7,3},{8,12},{12,8},{9,1... | collective-permute-start | bytes 6291464 | tf_op jit(solution)/shard_map/ppermute | solution.py:29
  0.5 20.5 %copy-start = (bf16[1024,1024]{1,0:T(8,128)(2,1)S(1)}, bf16[1024,1024]{1,0:T(8,128)(2,1)}, u32[]{:S(2)}) copy-start(bf16[1024,1024]{1,0:T(8,128)(2,1)} %own.1) | copy-start | bytes 6291460
  5.1 1.3 %copy-start.1 = (bf16[1024,1024]{1,0:T(8,128)(2,1)}, bf16[1024,1024]{1,0:T(8,128)(2,1)S(1)}, u32[]{:S(2)}) copy-start(bf16[1024,1024]{1,0:T(8,128)(2,1)S(1)} %collective-permute-done.other) | copy-start | bytes 6291460
  20.9 2.3 %collective-permute-start.1 = (bf16[64,1024]{1,0:T(8,128)(2,1)S(1)}, bf16[64,1024]{1,0:T(8,128)(2,1)S(1)}, u32[]{:S(2)}, u32[]{:S(2)}) collective-permute-start(bf16[64,1024]{1,0:T(8,128)(2,1)S(1)} %slice.60), channel_id=1, source_target_pairs={{0,4},{4,0},{1,5},{5,1},{2,6},{6,2},{3,7},{7,3},{8,12},{12,8},{9,1... | collective-permute-start | bytes 393224 | tf_op jit(solution)/shard_map/ppermute | solution.py:29
  21.0 1.6 %copy-start.2 = (bf16[1024,1024]{1,0:T(8,128)(2,1)S(1)}, bf16[1024,1024]{1,0:T(8,128)(2,1)}, u32[]{:S(2)}) copy-start(bf16[1024,1024]{1,0:T(8,128)(2,1)} %copy-done.1) | copy-start | bytes 6291460

commit v13 on v12

--- a/solution.py
+++ b/solution.py
@@ -10,6 +10,7 @@
 
 PLANE = ("chip", "gc")
 CHUNK = 1024
+FETCH_LIMIT = 16 * 2**20
 LIMIT = 107 * 2**19
 VMEM = pl.BlockSpec(memory_space=pltpu.VMEM)
 HBM = pl.BlockSpec(memory_space=pl.ANY)
@@ -128,6 +129,27 @@
     )(activations.reshape(rows, width), out_grads.reshape(rows, width), w_in, w_out)
 
 
+def fetch_kernel(block, out, sem):
+    copy = pltpu.make_async_copy(block, out, sem)
+    copy.start()
+    copy.wait()
+
+
+def fetch(block):
+    return pl.pallas_call(
+        fetch_kernel,
+        out_shape=jax.ShapeDtypeStruct(block.shape, block.dtype),
+        in_specs=[HBM],
+        out_specs=VMEM,
+        scratch_shapes=[pltpu.SemaphoreType.DMA],
+        compiler_params=pltpu.CompilerParams(vmem_limit_bytes=FETCH_LIMIT),
+        cost_estimate=pl.CostEstimate(
+            flops=0, bytes_accessed=2 * block.size * block.dtype.itemsize, transcendentals=0
+        ),
+        name="fetch",
+    )(block)
+
+
 def precond_kernel(case, got, own, other, out):
     block = own.shape[0]
     tile = min(256, block)
@@ -243,6 +265,7 @@
 
     pieces = gradient_pieces(plane, cols, block, activations, out_grads, proj_in.T, proj_out.T)
     pieces, inv_other = lax.optimization_barrier((pieces, inv_other))
+    inv_other = fetch(inv_other)
     first = leader(chips, cols)
     got = exchange(pieces, PLANE, plane, first)
     got = jnp.concatenate([got[i ^ first] for i in range(plane)])

time: 34 us -> 32.6 us (0.959)
  local copies, waits for them, and re-layouts: 3.03 us -> 1.55 us
    unnamed x13 -> x9, local copies, waits for them, and re-layouts: 2.94 us -> 1.45 us
  transfers between devices with their start and end apart: 2 -> 2, of which waited for: 0 -> 0; matrix products, arithmetic and copies ran while one was open for 0% -> 0% of each run, Pallas kernels for 15% -> 16%
where the time goes in v13:
time: 32.6 us; the launch traced here: 32.4 us
  blocking collectives  23.9 us (73%)
  Pallas kernels  5.58 us (17%)
  local copies, waits for them, and re-layouts  1.55 us (5%)
  other arithmetic  0.66 us (2%)
  starting transfers between devices  0.52 us (2%)
    all_to_all x2, blocking collectives, exchange(): lax.all_to_all(value, axes, 0, 0, axis_index_groups=[order], tiled=True)  23.9 us
    pallas_call x1, Pallas kernels, gradient_pieces(): pl.pallas_call(functools.partial(rows_kernel, length, block, cols), out_s...  4.47 us
    unnamed x9, local copies, waits for them, and re-layouts  1.45 us
  transfers between devices with their start and end apart: 2, of which 0 were waited for; matrix products, arithmetic and copies ran while one was open for 0% of the time, Pallas kernels for 16%

profile of v13, /device:TPU:0, one launch (start us, length us, event | category | flops | bytes accessed | tf_op | source)
XLA Modules:
  0.0 32.4 jit_solution(16411835188470357642)
XLA Ops:
  0.0 0.5 %collective-permute-start = (bf16[1024,1024]{1,0:T(8,128)(2,1)}, bf16[1024,1024]{1,0:T(8,128)(2,1)S(1)}, u32[]{:S(2)}, u32[]{:S(2)}) collective-permute-start(bf16[1024,1024]{1,0:T(8,128)(2,1)} %own.1), channel_id=1, source_target_pairs={{0,4},{4,0},{1,5},{5,1},{2,6},{6,2},{3,7},{7,3},{8,12},{12,8},{9,1... | collective-permute-start | bytes 6291464 | tf_op jit(solution)/shard_map/ppermute | solution.py:30
  0.5 4.5 %gradient_pieces.1 = bf16[8,8,2048]{2,1,0:T(8,128)(2,1)S(1)} custom-call(bf16[256,4096]{1,0:T(8,128)(2,1)} %bitcast.46, bf16[256,4096]{1,0:T(8,128)(2,1)} %bitcast.47, bf16[64,4096]{1,0:T(8,128)(2,1)} %bitcast.49, bf16[64,4096]{1,0:T(8,128)(2,1)} %bitcast.50), custom_call_target="tpu_custom_call" | custom-call | flops 268435456 | bytes 5242880 | tf_op jit(solution)/shard_map/gradient_pieces/pallas_call | solution.py:111
  4.9 0.0 collective-permute-done.block
  4.9 14.4 %all_to_all.10 = bf16[8,8,2048]{2,1,0:T(8,128)(2,1)S(1)} all-to-all(bf16[8,8,2048]{2,1,0:T(8,128)(2,1)S(1)} %gradient_pieces.1), channel_id=1, replica_groups={{10,11,8,9,2,3,0,1},{14,15,12,13,6,7,4,5},{26,27,24,25,18,19,16,17},{30..., dimensions={0} | all-to-all | bytes 524288 | tf_op jit(solution)/shard_map/all_to_all | solution.py:22
  19.4 0.1 collective-permute-start.1
  19.5 0.0 copy-start
  19.5 0.2 fetch.1.other
  19.7 1.4 %copy-done = bf16[1024,1024]{1,0:T(8,128)(2,1)S(1)} copy-done((bf16[1024,1024]{1,0:T(8,128)(2,1)S(1)}, bf16[1024,1024]{1,0:T(8,128)(2,1)}, u32[]{:S(2)}) %copy-start) | copy-done | bytes 2097176
  21.1 0.6 %precondition.1.precond = bf16[64,1024]{1,0:T(8,128)(2,1)S(1)} custom-call(s32[1]{0:T(128)} %bitcast.13.case, bf16[64,2048]{1,0:T(8,128)(2,1)S(1)} %fusion.got, bf16[1024,1024]{1,0:T(8,128)(2,1)S(1)} %copy-done, bf16[1024,1024]{1,0:T(8,128)(2,1)S(1)} %fetch.1.other), custom_call_target="tpu_custom_call" | custom-call | flops 134217728 | bytes 4194304 | tf_op jit(solution)/shard_map/precondition/pallas_call | solution.py:196
  21.7 0.0 collective-permute-done.1
  21.7 0.4 %kernel_terms.1 = f32[16,8,128]{2,1,0:T(8,128)S(1)} custom-call(s32[1]{0:T(128)} %bitcast.core, bf16[64,1024]{1,0:T(8,128)(2,1)S(1)} %precondition.1.precond, bf16[128,1024]{1,0:T(8,128)(2,1)S(1)} %bitcast.45), custom_call_target="tpu_custom_call" | custom-call | flops 33554432 | bytes 65536 | tf_op jit(solution)/shard_map/kernel_terms/pallas_call | solution.py:239
  22.1 9.5 %all_to_all.11 = f32[16,8,128]{2,1,0:T(8,128)S(1)} all-to-all(f32[16,8,128]{2,1,0:T(8,128)S(1)} %kernel_terms.1), channel_id=1, replica_groups={{1,0,3,2,5,4,7,6,9,8,11,10,13,12,15,14},{17,16,19,18,21,20,23,22,25,24,..., dimensions={0} | all-to-all | bytes 131072 | tf_op jit(solution)/shard_map/all_to_all | solution.py:22
  31.7 0.1 fusion.8
  31.8 0.6 %pad_maximum_fusion = f32[32,32]{1,0:T(8,128)} fusion(f32[8,32]{1,0:T(8,128)S(1)} %get-tuple-element.14, f32[8,32]{1,0:T(8,128)S(1)} %get-tuple-element.15, f32[8,32]{1,0:T(8,128)S(1)} %get-tuple-element.16, f32[8,32]{1,0:T(8,128)S(1)} %get-tuple-element.13), kind=kLoop, calls=%fused_computation.17 | loop fusion | flops 3072 | bytes 8192 | tf_op jit(solution)/shard_map/concatenate | solution.py:293
  (11 shorter events, 0.1 us)
Async XLA Ops:
  0.0 4.9 %collective-permute-start = (bf16[1024,1024]{1,0:T(8,128)(2,1)}, bf16[1024,1024]{1,0:T(8,128)(2,1)S(1)}, u32[]{:S(2)}, u32[]{:S(2)}) collective-permute-start(bf16[1024,1024]{1,0:T(8,128)(2,1)} %own.1), channel_id=1, source_target_pairs={{0,4},{4,0},{1,5},{5,1},{2,6},{6,2},{3,7},{7,3},{8,12},{12,8},{9,1... | collective-permute-start | bytes 6291464 | tf_op jit(solution)/shard_map/ppermute | solution.py:30
  19.4 2.3 %collective-permute-start.1 = (bf16[64,1024]{1,0:T(8,128)(2,1)S(1)}, bf16[64,1024]{1,0:T(8,128)(2,1)S(1)}, u32[]{:S(2)}, u32[]{:S(2)}) collective-permute-start(bf16[64,1024]{1,0:T(8,128)(2,1)S(1)} %slice.60), channel_id=1, source_target_pairs={{0,4},{4,0},{1,5},{5,1},{2,6},{6,2},{3,7},{7,3},{8,12},{12,8},{9,1... | collective-permute-start | bytes 393224 | tf_op jit(solution)/shard_map/ppermute | solution.py:30
  19.5 1.6 %copy-start = (bf16[1024,1024]{1,0:T(8,128)(2,1)S(1)}, bf16[1024,1024]{1,0:T(8,128)(2,1)}, u32[]{:S(2)}) copy-start(bf16[1024,1024]{1,0:T(8,128)(2,1)} %own.1) | copy-start | bytes 6291460

commit v14 on v12

--- a/solution.py
+++ b/solution.py
@@ -10,6 +10,7 @@
 
 PLANE = ("chip", "gc")
 CHUNK = 1024
+FETCH_LIMIT = 16 * 2**20
 LIMIT = 107 * 2**19
 VMEM = pl.BlockSpec(memory_space=pltpu.VMEM)
 HBM = pl.BlockSpec(memory_space=pl.ANY)
@@ -128,6 +129,32 @@
     )(activations.reshape(rows, width), out_grads.reshape(rows, width), w_in, w_out)
 
 
+def fetch_kernel(own, other, own_v, other_v, sem):
+    copies = [
+        pltpu.make_async_copy(own, own_v, sem.at[0]),
+        pltpu.make_async_copy(other, other_v, sem.at[1]),
+    ]
+    for copy in copies:
+        copy.start()
+    for copy in copies:
+        copy.wait()
+
+
+def fetch(own, other):
+    return pl.pallas_call(
+        fetch_kernel,
+        out_shape=[jax.ShapeDtypeStruct(own.shape, own.dtype)] * 2,
+        in_specs=[HBM] * 2,
+        out_specs=[VMEM] * 2,
+        scratch_shapes=[pltpu.SemaphoreType.DMA((2,))],
+        compiler_params=pltpu.CompilerParams(vmem_limit_bytes=FETCH_LIMIT),
+        cost_estimate=pl.CostEstimate(
+            flops=0, bytes_accessed=4 * own.size * own.dtype.itemsize, transcendentals=0
+        ),
+        name="fetch",
+    )(own, other)
+
+
 def precond_kernel(case, got, own, other, out):
     block = own.shape[0]
     tile = min(256, block)
@@ -243,6 +270,7 @@
 
     pieces = gradient_pieces(plane, cols, block, activations, out_grads, proj_in.T, proj_out.T)
     pieces, inv_other = lax.optimization_barrier((pieces, inv_other))
+    inv_own, inv_other = fetch(inv_gram, inv_other)
     first = leader(chips, cols)
     got = exchange(pieces, PLANE, plane, first)
     got = jnp.concatenate([got[i ^ first] for i in range(plane)])
@@ -254,7 +282,7 @@
     diagonal_other = (col % 2 != core).astype(jnp.int32)
     case = jnp.where(home, 2 + 2 * (col % 2) + diagonal_other, left_other).astype(jnp.int32)
     theirs, precond = lax.optimization_barrier(
-        (theirs, precondition(case.reshape(1), got, inv_gram, inv_other))
+        (theirs, precondition(case.reshape(1), got, inv_own, inv_other))
     )
     mine = mine.reshape(chips, 1, tall, block)
     theirs = theirs.reshape(chips, 1, tall, block)

time: 34 us -> 34.4 us (1.012)
  transfers between devices with their start and end apart: 2 -> 2, of which waited for: 0 -> 0; matrix products, arithmetic and copies ran while one was open for 0% -> 0% of each run, Pallas kernels for 15% -> 16%
where the time goes in v14:
time: 34.4 us; the launch traced here: 34.2 us
  blocking collectives  23.9 us (69%)
  Pallas kernels  5.91 us (17%)
  local copies, waits for them, and re-layouts  3.03 us (9%)
  other arithmetic  0.66 us (2%)
  starting transfers between devices  0.52 us (2%)
    all_to_all x2, blocking collectives, exchange(): lax.all_to_all(value, axes, 0, 0, axis_index_groups=[order], tiled=True)  23.9 us
    pallas_call x1, Pallas kernels, gradient_pieces(): pl.pallas_call(functools.partial(rows_kernel, length, block, cols), out_s...  4.61 us
    unnamed x13, local copies, waits for them, and re-layouts  2.94 us
  transfers between devices with their start and end apart: 2, of which 0 were waited for; matrix products, arithmetic and copies ran while one was open for 0% of the time, Pallas kernels for 16%

profile of v14, /device:TPU:0, one launch (start us, length us, event | category | flops | bytes accessed | tf_op | source)
XLA Modules:
  0.0 34.2 jit_solution(17037475751945827579)
XLA Ops:
  0.0 0.5 %collective-permute-start = (bf16[1024,1024]{1,0:T(8,128)(2,1)}, bf16[1024,1024]{1,0:T(8,128)(2,1)S(1)}, u32[]{:S(2)}, u32[]{:S(2)}) collective-permute-start(bf16[1024,1024]{1,0:T(8,128)(2,1)} %own.1), channel_id=1, source_target_pairs={{0,4},{4,0},{1,5},{5,1},{2,6},{6,2},{3,7},{7,3},{8,12},{12,8},{9,1... | collective-permute-start | bytes 6291464 | tf_op jit(solution)/shard_map/ppermute | solution.py:30
  0.5 0.0 copy-start
  0.5 4.6 %gradient_pieces.1 = bf16[8,8,2048]{2,1,0:T(8,128)(2,1)S(1)} custom-call(bf16[256,4096]{1,0:T(8,128)(2,1)} %bitcast.46, bf16[256,4096]{1,0:T(8,128)(2,1)} %bitcast.47, bf16[64,4096]{1,0:T(8,128)(2,1)} %bitcast.49, bf16[64,4096]{1,0:T(8,128)(2,1)} %bitcast.50), custom_call_target="tpu_custom_call" | custom-call | flops 268435456 | bytes 5242880 | tf_op jit(solution)/shard_map/gradient_pieces/pallas_call | solution.py:111
  5.1 0.0 collective-permute-done.other
  5.1 0.0 copy-start.1
  5.1 1.3 %copy-done.1 = bf16[1024,1024]{1,0:T(8,128)(2,1)} copy-done((bf16[1024,1024]{1,0:T(8,128)(2,1)}, bf16[1024,1024]{1,0:T(8,128)(2,1)S(1)}, u32[]{:S(2)}) %copy-start.1) | copy-done | bytes 2097176
  6.4 14.4 %all_to_all.10 = bf16[8,8,2048]{2,1,0:T(8,128)(2,1)S(1)} all-to-all(bf16[8,8,2048]{2,1,0:T(8,128)(2,1)S(1)} %gradient_pieces.1), channel_id=1, replica_groups={{10,11,8,9,2,3,0,1},{14,15,12,13,6,7,4,5},{26,27,24,25,18,19,16,17},{30..., dimensions={0} | all-to-all | bytes 524288 | tf_op jit(solution)/shard_map/all_to_all | solution.py:22
  20.9 0.1 collective-permute-start.1
  21.0 0.0 copy-done
  21.0 0.0 copy-start.2
  21.0 1.6 %copy-done.2 = bf16[1024,1024]{1,0:T(8,128)(2,1)S(1)} copy-done((bf16[1024,1024]{1,0:T(8,128)(2,1)S(1)}, bf16[1024,1024]{1,0:T(8,128)(2,1)}, u32[]{:S(2)}) %copy-start.2) | copy-done | bytes 2097176
  22.6 0.3 fetch.1
  22.9 0.6 %precondition.1.precond = bf16[64,1024]{1,0:T(8,128)(2,1)S(1)} custom-call(s32[1]{0:T(128)} %bitcast.13.case, bf16[64,2048]{1,0:T(8,128)(2,1)S(1)} %fusion.got, bf16[1024,1024]{1,0:T(8,128)(2,1)S(1)} %get-tuple-element.13.own, bf16[1024,1024]{1,0:T(8,128)(2,1)S(1)} %get-tuple-element.14.other), custom_call_target="tpu_custom_call" | custom-call | flops 134217728 | bytes 4194304 | tf_op jit(solution)/shard_map/precondition/pallas_call | solution.py:201
  23.5 0.0 collective-permute-done.1
  23.5 0.4 %kernel_terms.1 = f32[16,8,128]{2,1,0:T(8,128)S(1)} custom-call(s32[1]{0:T(128)} %bitcast.core, bf16[64,1024]{1,0:T(8,128)(2,1)S(1)} %precondition.1.precond, bf16[128,1024]{1,0:T(8,128)(2,1)S(1)} %bitcast.45), custom_call_target="tpu_custom_call" | custom-call | flops 33554432 | bytes 65536 | tf_op jit(solution)/shard_map/kernel_terms/pallas_call | solution.py:244
  24.0 9.5 %all_to_all.11 = f32[16,8,128]{2,1,0:T(8,128)S(1)} all-to-all(f32[16,8,128]{2,1,0:T(8,128)S(1)} %kernel_terms.1), channel_id=1, replica_groups={{1,0,3,2,5,4,7,6,9,8,11,10,13,12,15,14},{17,16,19,18,21,20,23,22,25,24,..., dimensions={0} | all-to-all | bytes 131072 | tf_op jit(solution)/shard_map/all_to_all | solution.py:22
  33.5 0.1 fusion.8
  33.6 0.6 %pad_maximum_fusion = f32[32,32]{1,0:T(8,128)} fusion(f32[8,32]{1,0:T(8,128)S(1)} %get-tuple-element.18, f32[8,32]{1,0:T(8,128)S(1)} %get-tuple-element.19, f32[8,32]{1,0:T(8,128)S(1)} %get-tuple-element.20, f32[8,32]{1,0:T(8,128)S(1)} %get-tuple-element.17), kind=kLoop, calls=%fused_computation.17 | loop fusion | flops 3072 | bytes 8192 | tf_op jit(solution)/shard_map/concatenate | solution.py:298
  (11 shorter events, 0.1 us)
Async XLA Ops:
  0.0 5.1 %collective-permute-start = (bf16[1024,1024]{1,0:T(8,128)(2,1)}, bf16[1024,1024]{1,0:T(8,128)(2,1)S(1)}, u32[]{:S(2)}, u32[]{:S(2)}) collective-permute-start(bf16[1024,1024]{1,0:T(8,128)(2,1)} %own.1), channel_id=1, source_target_pairs={{0,4},{4,0},{1,5},{5,1},{2,6},{6,2},{3,7},{7,3},{8,12},{12,8},{9,1... | collective-permute-start | bytes 6291464 | tf_op jit(solution)/shard_map/ppermute | solution.py:30
  0.5 20.5 %copy-start = (bf16[1024,1024]{1,0:T(8,128)(2,1)S(1)}, bf16[1024,1024]{1,0:T(8,128)(2,1)}, u32[]{:S(2)}) copy-start(bf16[1024,1024]{1,0:T(8,128)(2,1)} %own.1) | copy-start | bytes 6291460
  5.1 1.3 %copy-start.1 = (bf16[1024,1024]{1,0:T(8,128)(2,1)}, bf16[1024,1024]{1,0:T(8,128)(2,1)S(1)}, u32[]{:S(2)}) copy-start(bf16[1024,1024]{1,0:T(8,128)(2,1)S(1)} %collective-permute-done.other) | copy-start | bytes 6291460
  20.9 2.6 %collective-permute-start.1 = (bf16[64,1024]{1,0:T(8,128)(2,1)S(1)}, bf16[64,1024]{1,0:T(8,128)(2,1)S(1)}, u32[]{:S(2)}, u32[]{:S(2)}) collective-permute-start(bf16[64,1024]{1,0:T(8,128)(2,1)S(1)} %slice.60), channel_id=1, source_target_pairs={{0,4},{4,0},{1,5},{5,1},{2,6},{6,2},{3,7},{7,3},{8,12},{12,8},{9,1... | collective-permute-start | bytes 393224 | tf_op jit(solution)/shard_map/ppermute | solution.py:30
  21.0 1.6 %copy-start.2 = (bf16[1024,1024]{1,0:T(8,128)(2,1)S(1)}, bf16[1024,1024]{1,0:T(8,128)(2,1)}, u32[]{:S(2)}) copy-start(bf16[1024,1024]{1,0:T(8,128)(2,1)} %copy-done.1) | copy-start | bytes 6291460

commit v15 on v13

--- a/solution.py
+++ b/solution.py
@@ -220,10 +220,11 @@
         once = lax.dot_general(held, right[...], NT, preferred_element_type=jnp.float32) * scale
         turned = lax.dot_general(right[...], held, NT, preferred_element_type=jnp.float32) * scale
         for chip in range(count):
-            mine, next_to = 2 * (first + chip) + core[0], 2 * (first + chip) + 1 - core[0]
+            mine = 2 * (first + chip) + core[0]
+            across = ((2 * (first + chip)) ^ (n // 2)) + core[0]
             for place in range(n):
-                out[mine * n + (place ^ 1)] += packed(once, chip, place)
-                out[place * n + next_to] += packed(turned, place, chip)
+                out[mine * n + (place ^ (n // 2))] += packed(once, chip, place)
+                out[place * n + across] += packed(turned, place, chip)
 
     out[...] = jnp.zeros_like(out)
     if chips <= 2:
@@ -289,7 +290,7 @@
 
     fold = max(1, 128 // tall)
     terms = kernel_terms(cols, fold, 8.0 / feat, core.reshape(1).astype(jnp.int32), precond, right)
-    total = jnp.sum(exchange(terms, ("chip", "core", "gc"), cols * cols, 1), axis=0)
+    total = jnp.sum(exchange(terms, ("chip", "core", "gc"), cols * cols, cols // 2), axis=0)
     return jnp.concatenate([total[:, i * tall : (i + 1) * tall] for i in range(fold)])
 
 

time: 32.6 us -> 32.1 us (0.985)
  blocking collectives: 23.9 us -> 23.4 us
    all_to_all x2, blocking collectives: 23.9 us -> 23.4 us  [exchange(): lax.all_to_all(value, axes, 0, 0, axis_index_groups=[order], tiled=True)]
where the time goes in v15:
time: 32.1 us; the launch traced here: 31.9 us
  blocking collectives  23.4 us (73%)
  Pallas kernels  5.58 us (17%)
  local copies, waits for them, and re-layouts  1.55 us (5%)
  other arithmetic  0.66 us (2%)
  starting transfers between devices  0.52 us (2%)
    all_to_all x2, blocking collectives, exchange(): lax.all_to_all(value, axes, 0, 0, axis_index_groups=[order], tiled=True)  23.4 us
    pallas_call x1, Pallas kernels, gradient_pieces(): pl.pallas_call(functools.partial(rows_kernel, length, block, cols), out_s...  4.47 us
    unnamed x9, local copies, waits for them, and re-layouts  1.45 us
  transfers between devices with their start and end apart: 2, of which 0 were waited for; matrix products, arithmetic and copies ran while one was open for 0% of the time, Pallas kernels for 16%

profile of v15, /device:TPU:0, one launch (start us, length us, event | category | flops | bytes accessed | tf_op | source)
XLA Modules:
  0.0 31.9 jit_solution(200151416469732470)
XLA Ops:
  0.0 0.5 %collective-permute-start = (bf16[1024,1024]{1,0:T(8,128)(2,1)}, bf16[1024,1024]{1,0:T(8,128)(2,1)S(1)}, u32[]{:S(2)}, u32[]{:S(2)}) collective-permute-start(bf16[1024,1024]{1,0:T(8,128)(2,1)} %own.1), channel_id=1, source_target_pairs={{0,4},{4,0},{1,5},{5,1},{2,6},{6,2},{3,7},{7,3},{8,12},{12,8},{9,1... | collective-permute-start | bytes 6291464 | tf_op jit(solution)/shard_map/ppermute | solution.py:30
  0.5 4.5 %gradient_pieces.1 = bf16[8,8,2048]{2,1,0:T(8,128)(2,1)S(1)} custom-call(bf16[256,4096]{1,0:T(8,128)(2,1)} %bitcast.46, bf16[256,4096]{1,0:T(8,128)(2,1)} %bitcast.47, bf16[64,4096]{1,0:T(8,128)(2,1)} %bitcast.49, bf16[64,4096]{1,0:T(8,128)(2,1)} %bitcast.50), custom_call_target="tpu_custom_call" | custom-call | flops 268435456 | bytes 5242880 | tf_op jit(solution)/shard_map/gradient_pieces/pallas_call | solution.py:111
  4.9 0.0 collective-permute-done.block
  4.9 14.4 %all_to_all.10 = bf16[8,8,2048]{2,1,0:T(8,128)(2,1)S(1)} all-to-all(bf16[8,8,2048]{2,1,0:T(8,128)(2,1)S(1)} %gradient_pieces.1), channel_id=1, replica_groups={{10,11,8,9,2,3,0,1},{14,15,12,13,6,7,4,5},{26,27,24,25,18,19,16,17},{30..., dimensions={0} | all-to-all | bytes 524288 | tf_op jit(solution)/shard_map/all_to_all | solution.py:22
  19.4 0.1 collective-permute-start.1
  19.5 0.0 copy-start
  19.5 0.2 fetch.1.other
  19.7 1.4 %copy-done = bf16[1024,1024]{1,0:T(8,128)(2,1)S(1)} copy-done((bf16[1024,1024]{1,0:T(8,128)(2,1)S(1)}, bf16[1024,1024]{1,0:T(8,128)(2,1)}, u32[]{:S(2)}) %copy-start) | copy-done | bytes 2097176
  21.1 0.6 %precondition.1.precond = bf16[64,1024]{1,0:T(8,128)(2,1)S(1)} custom-call(s32[1]{0:T(128)} %bitcast.13.case, bf16[64,2048]{1,0:T(8,128)(2,1)S(1)} %fusion.got, bf16[1024,1024]{1,0:T(8,128)(2,1)S(1)} %copy-done, bf16[1024,1024]{1,0:T(8,128)(2,1)S(1)} %fetch.1.other), custom_call_target="tpu_custom_call" | custom-call | flops 134217728 | bytes 4194304 | tf_op jit(solution)/shard_map/precondition/pallas_call | solution.py:196
  21.7 0.0 collective-permute-done.1
  21.7 0.4 %kernel_terms.1 = f32[16,8,128]{2,1,0:T(8,128)S(1)} custom-call(s32[1]{0:T(128)} %bitcast.core, bf16[64,1024]{1,0:T(8,128)(2,1)S(1)} %precondition.1.precond, bf16[128,1024]{1,0:T(8,128)(2,1)S(1)} %bitcast.45), custom_call_target="tpu_custom_call" | custom-call | flops 33554432 | bytes 65536 | tf_op jit(solution)/shard_map/kernel_terms/pallas_call | solution.py:240
  22.1 9.0 %all_to_all.11 = f32[16,8,128]{2,1,0:T(8,128)S(1)} all-to-all(f32[16,8,128]{2,1,0:T(8,128)S(1)} %kernel_terms.1), channel_id=1, replica_groups={{2,3,0,1,6,7,4,5,10,11,8,9,14,15,12,13},{18,19,16,17,22,23,20,21,26,27,..., dimensions={0} | all-to-all | bytes 131072 | tf_op jit(solution)/shard_map/all_to_all | solution.py:22
  31.2 0.1 fusion.8
  31.3 0.6 %pad_maximum_fusion = f32[32,32]{1,0:T(8,128)} fusion(f32[8,32]{1,0:T(8,128)S(1)} %get-tuple-element.14, f32[8,32]{1,0:T(8,128)S(1)} %get-tuple-element.15, f32[8,32]{1,0:T(8,128)S(1)} %get-tuple-element.16, f32[8,32]{1,0:T(8,128)S(1)} %get-tuple-element.13), kind=kLoop, calls=%fused_computation.17 | loop fusion | flops 3072 | bytes 8192 | tf_op jit(solution)/shard_map/concatenate | solution.py:294
  (11 shorter events, 0.1 us)
Async XLA Ops:
  0.0 4.9 %collective-permute-start = (bf16[1024,1024]{1,0:T(8,128)(2,1)}, bf16[1024,1024]{1,0:T(8,128)(2,1)S(1)}, u32[]{:S(2)}, u32[]{:S(2)}) collective-permute-start(bf16[1024,1024]{1,0:T(8,128)(2,1)} %own.1), channel_id=1, source_target_pairs={{0,4},{4,0},{1,5},{5,1},{2,6},{6,2},{3,7},{7,3},{8,12},{12,8},{9,1... | collective-permute-start | bytes 6291464 | tf_op jit(solution)/shard_map/ppermute | solution.py:30
  19.4 2.3 %collective-permute-start.1 = (bf16[64,1024]{1,0:T(8,128)(2,1)S(1)}, bf16[64,1024]{1,0:T(8,128)(2,1)S(1)}, u32[]{:S(2)}, u32[]{:S(2)}) collective-permute-start(bf16[64,1024]{1,0:T(8,128)(2,1)S(1)} %slice.60), channel_id=1, source_target_pairs={{0,4},{4,0},{1,5},{5,1},{2,6},{6,2},{3,7},{7,3},{8,12},{12,8},{9,1... | collective-permute-start | bytes 393224 | tf_op jit(solution)/shard_map/ppermute | solution.py:30
  19.5 1.6 %copy-start = (bf16[1024,1024]{1,0:T(8,128)(2,1)S(1)}, bf16[1024,1024]{1,0:T(8,128)(2,1)}, u32[]{:S(2)}) copy-start(bf16[1024,1024]{1,0:T(8,128)(2,1)} %own.1) | copy-start | bytes 6291460

commit v16 on v15

--- a/solution.py
+++ b/solution.py
@@ -22,8 +22,8 @@
     return lax.all_to_all(value, axes, 0, 0, axis_index_groups=[order], tiled=True)
 
 
-def leader(chips, cols):
-    return chips // 2 * cols + cols // 2
+def leader(cols):
+    return cols // 2
 
 
 def other_core(value):
@@ -93,7 +93,7 @@
         summed[i * seqs : (i + 1) * seqs].astype(out.dtype) for i in range(many // seqs)
     ]
     for place in range(out.shape[0]):
-        member = place ^ leader(out.shape[0] // cols, cols)
+        member = place ^ leader(cols)
         chip, col = member // cols, member % cols
         odd = col % 2 if chip < col // 2 else 1 - col % 2
         for slot, source in enumerate((2 * chip + odd, col)):
@@ -267,7 +267,7 @@
     pieces = gradient_pieces(plane, cols, block, activations, out_grads, proj_in.T, proj_out.T)
     pieces, inv_other = lax.optimization_barrier((pieces, inv_other))
     inv_other = fetch(inv_other)
-    first = leader(chips, cols)
+    first = leader(cols)
     got = exchange(pieces, PLANE, plane, first)
     got = jnp.concatenate([got[i ^ first] for i in range(plane)])
 

time: 32.1 us -> 32.4 us (level)
  no operation moved by 1% of the time
where the time goes in v16:
time: 32.4 us; the launch traced here: 32.2 us
  blocking collectives  23.7 us (73%)
  Pallas kernels  5.58 us (17%)
  local copies, waits for them, and re-layouts  1.55 us (5%)
  other arithmetic  0.66 us (2%)
  starting transfers between devices  0.52 us (2%)
    all_to_all x2, blocking collectives, exchange(): lax.all_to_all(value, axes, 0, 0, axis_index_groups=[order], tiled=True)  23.7 us
    pallas_call x1, Pallas kernels, gradient_pieces(): pl.pallas_call(functools.partial(rows_kernel, length, block, cols), out_s...  4.47 us
    unnamed x9, local copies, waits for them, and re-layouts  1.45 us
  transfers between devices with their start and end apart: 2, of which 0 were waited for; matrix products, arithmetic and copies ran while one was open for 0% of the time, Pallas kernels for 16%

profile of v16, /device:TPU:0, one launch (start us, length us, event | category | flops | bytes accessed | tf_op | source)
XLA Modules:
  0.0 32.2 jit_solution(16156318405882291757)
XLA Ops:
  0.0 0.5 %collective-permute-start = (bf16[1024,1024]{1,0:T(8,128)(2,1)}, bf16[1024,1024]{1,0:T(8,128)(2,1)S(1)}, u32[]{:S(2)}, u32[]{:S(2)}) collective-permute-start(bf16[1024,1024]{1,0:T(8,128)(2,1)} %own.1), channel_id=1, source_target_pairs={{0,4},{4,0},{1,5},{5,1},{2,6},{6,2},{3,7},{7,3},{8,12},{12,8},{9,1... | collective-permute-start | bytes 6291464 | tf_op jit(solution)/shard_map/ppermute | solution.py:30
  0.5 4.5 %gradient_pieces.1 = bf16[8,8,2048]{2,1,0:T(8,128)(2,1)S(1)} custom-call(bf16[256,4096]{1,0:T(8,128)(2,1)} %bitcast.46, bf16[256,4096]{1,0:T(8,128)(2,1)} %bitcast.47, bf16[64,4096]{1,0:T(8,128)(2,1)} %bitcast.49, bf16[64,4096]{1,0:T(8,128)(2,1)} %bitcast.50), custom_call_target="tpu_custom_call" | custom-call | flops 268435456 | bytes 5242880 | tf_op jit(solution)/shard_map/gradient_pieces/pallas_call | solution.py:111
  4.9 0.0 collective-permute-done.block
  4.9 14.9 %all_to_all.10 = bf16[8,8,2048]{2,1,0:T(8,128)(2,1)S(1)} all-to-all(bf16[8,8,2048]{2,1,0:T(8,128)(2,1)S(1)} %gradient_pieces.1), channel_id=1, replica_groups={{2,3,0,1,10,11,8,9},{6,7,4,5,14,15,12,13},{18,19,16,17,26,27,24,25},{22..., dimensions={0} | all-to-all | bytes 524288 | tf_op jit(solution)/shard_map/all_to_all | solution.py:22
  19.9 0.1 collective-permute-start.1
  20.0 0.0 copy-start
  20.1 0.2 fetch.1.other
  20.2 1.4 %copy-done = bf16[1024,1024]{1,0:T(8,128)(2,1)S(1)} copy-done((bf16[1024,1024]{1,0:T(8,128)(2,1)S(1)}, bf16[1024,1024]{1,0:T(8,128)(2,1)}, u32[]{:S(2)}) %copy-start) | copy-done | bytes 2097176
  21.6 0.6 %precondition.1.precond = bf16[64,1024]{1,0:T(8,128)(2,1)S(1)} custom-call(s32[1]{0:T(128)} %bitcast.13.case, bf16[64,2048]{1,0:T(8,128)(2,1)S(1)} %fusion.got, bf16[1024,1024]{1,0:T(8,128)(2,1)S(1)} %copy-done, bf16[1024,1024]{1,0:T(8,128)(2,1)S(1)} %fetch.1.other), custom_call_target="tpu_custom_call" | custom-call | flops 134217728 | bytes 4194304 | tf_op jit(solution)/shard_map/precondition/pallas_call | solution.py:196
  22.2 0.0 collective-permute-done.1
  22.3 0.4 %kernel_terms.1 = f32[16,8,128]{2,1,0:T(8,128)S(1)} custom-call(s32[1]{0:T(128)} %bitcast.core, bf16[64,1024]{1,0:T(8,128)(2,1)S(1)} %precondition.1.precond, bf16[128,1024]{1,0:T(8,128)(2,1)S(1)} %bitcast.45), custom_call_target="tpu_custom_call" | custom-call | flops 33554432 | bytes 65536 | tf_op jit(solution)/shard_map/kernel_terms/pallas_call | solution.py:240
  22.7 8.8 %all_to_all.11 = f32[16,8,128]{2,1,0:T(8,128)S(1)} all-to-all(f32[16,8,128]{2,1,0:T(8,128)S(1)} %kernel_terms.1), channel_id=1, replica_groups={{2,3,0,1,6,7,4,5,10,11,8,9,14,15,12,13},{18,19,16,17,22,23,20,21,26,27,..., dimensions={0} | all-to-all | bytes 131072 | tf_op jit(solution)/shard_map/all_to_all | solution.py:22
  31.5 0.1 fusion.8
  31.6 0.6 %pad_maximum_fusion = f32[32,32]{1,0:T(8,128)} fusion(f32[8,32]{1,0:T(8,128)S(1)} %get-tuple-element.14, f32[8,32]{1,0:T(8,128)S(1)} %get-tuple-element.15, f32[8,32]{1,0:T(8,128)S(1)} %get-tuple-element.16, f32[8,32]{1,0:T(8,128)S(1)} %get-tuple-element.13), kind=kLoop, calls=%fused_computation.17 | loop fusion | flops 3072 | bytes 8192 | tf_op jit(solution)/shard_map/concatenate | solution.py:294
  (11 shorter events, 0.1 us)
Async XLA Ops:
  0.0 4.9 %collective-permute-start = (bf16[1024,1024]{1,0:T(8,128)(2,1)}, bf16[1024,1024]{1,0:T(8,128)(2,1)S(1)}, u32[]{:S(2)}, u32[]{:S(2)}) collective-permute-start(bf16[1024,1024]{1,0:T(8,128)(2,1)} %own.1), channel_id=1, source_target_pairs={{0,4},{4,0},{1,5},{5,1},{2,6},{6,2},{3,7},{7,3},{8,12},{12,8},{9,1... | collective-permute-start | bytes 6291464 | tf_op jit(solution)/shard_map/ppermute | solution.py:30
  19.9 2.3 %collective-permute-start.1 = (bf16[64,1024]{1,0:T(8,128)(2,1)S(1)}, bf16[64,1024]{1,0:T(8,128)(2,1)S(1)}, u32[]{:S(2)}, u32[]{:S(2)}) collective-permute-start(bf16[64,1024]{1,0:T(8,128)(2,1)S(1)} %slice.60), channel_id=1, source_target_pairs={{0,4},{4,0},{1,5},{5,1},{2,6},{6,2},{3,7},{7,3},{8,12},{12,8},{9,1... | collective-permute-start | bytes 393224 | tf_op jit(solution)/shard_map/ppermute | solution.py:30
  20.0 1.6 %copy-start = (bf16[1024,1024]{1,0:T(8,128)(2,1)S(1)}, bf16[1024,1024]{1,0:T(8,128)(2,1)}, u32[]{:S(2)}) copy-start(bf16[1024,1024]{1,0:T(8,128)(2,1)} %own.1) | copy-start | bytes 6291460

commit v17 on v15

--- a/solution.py
+++ b/solution.py
@@ -9,7 +9,7 @@
 from jax.sharding import Mesh, PartitionSpec as P
 
 PLANE = ("chip", "gc")
-CHUNK = 1024
+CHUNK = 512
 FETCH_LIMIT = 16 * 2**20
 LIMIT = 107 * 2**19
 VMEM = pl.BlockSpec(memory_space=pltpu.VMEM)

time: 32.1 us -> 32.2 us (level)
  no operation moved by 1% of the time
where the time goes in v17:
time: 32.2 us; the launch traced here: 32 us
  blocking collectives  23.4 us (73%)
  Pallas kernels  5.66 us (18%)
  local copies, waits for them, and re-layouts  1.55 us (5%)
  other arithmetic  0.66 us (2%)
  starting transfers between devices  0.52 us (2%)
    all_to_all x2, blocking collectives, exchange(): lax.all_to_all(value, axes, 0, 0, axis_index_groups=[order], tiled=True)  23.4 us
    pallas_call x1, Pallas kernels, gradient_pieces(): pl.pallas_call(functools.partial(rows_kernel, length, block, cols), out_s...  4.55 us
    unnamed x9, local copies, waits for them, and re-layouts  1.45 us
  transfers between devices with their start and end apart: 2, of which 0 were waited for; matrix products, arithmetic and copies ran while one was open for 0% of the time, Pallas kernels for 16%

profile of v17, /device:TPU:0, one launch (start us, length us, event | category | flops | bytes accessed | tf_op | source)
XLA Modules:
  0.0 32.0 jit_solution(5839169666157445577)
XLA Ops:
  0.0 0.5 %collective-permute-start = (bf16[1024,1024]{1,0:T(8,128)(2,1)}, bf16[1024,1024]{1,0:T(8,128)(2,1)S(1)}, u32[]{:S(2)}, u32[]{:S(2)}) collective-permute-start(bf16[1024,1024]{1,0:T(8,128)(2,1)} %own.1), channel_id=1, source_target_pairs={{0,4},{4,0},{1,5},{5,1},{2,6},{6,2},{3,7},{7,3},{8,12},{12,8},{9,1... | collective-permute-start | bytes 6291464 | tf_op jit(solution)/shard_map/ppermute | solution.py:30
  0.5 4.5 %gradient_pieces.1 = bf16[8,8,2048]{2,1,0:T(8,128)(2,1)S(1)} custom-call(bf16[256,4096]{1,0:T(8,128)(2,1)} %bitcast.46, bf16[256,4096]{1,0:T(8,128)(2,1)} %bitcast.47, bf16[64,4096]{1,0:T(8,128)(2,1)} %bitcast.49, bf16[64,4096]{1,0:T(8,128)(2,1)} %bitcast.50), custom_call_target="tpu_custom_call" | custom-call | flops 268435456 | bytes 5242880 | tf_op jit(solution)/shard_map/gradient_pieces/pallas_call | solution.py:111
  5.0 0.0 collective-permute-done.block
  5.0 14.4 %all_to_all.10 = bf16[8,8,2048]{2,1,0:T(8,128)(2,1)S(1)} all-to-all(bf16[8,8,2048]{2,1,0:T(8,128)(2,1)S(1)} %gradient_pieces.1), channel_id=1, replica_groups={{10,11,8,9,2,3,0,1},{14,15,12,13,6,7,4,5},{26,27,24,25,18,19,16,17},{30..., dimensions={0} | all-to-all | bytes 524288 | tf_op jit(solution)/shard_map/all_to_all | solution.py:22
  19.5 0.1 collective-permute-start.1
  19.6 0.0 copy-start
  19.6 0.2 fetch.1.other
  19.8 1.4 %copy-done = bf16[1024,1024]{1,0:T(8,128)(2,1)S(1)} copy-done((bf16[1024,1024]{1,0:T(8,128)(2,1)S(1)}, bf16[1024,1024]{1,0:T(8,128)(2,1)}, u32[]{:S(2)}) %copy-start) | copy-done | bytes 2097176
  21.2 0.6 %precondition.1.precond = bf16[64,1024]{1,0:T(8,128)(2,1)S(1)} custom-call(s32[1]{0:T(128)} %bitcast.13.case, bf16[64,2048]{1,0:T(8,128)(2,1)S(1)} %fusion.got, bf16[1024,1024]{1,0:T(8,128)(2,1)S(1)} %copy-done, bf16[1024,1024]{1,0:T(8,128)(2,1)S(1)} %fetch.1.other), custom_call_target="tpu_custom_call" | custom-call | flops 134217728 | bytes 4194304 | tf_op jit(solution)/shard_map/precondition/pallas_call | solution.py:196
  21.8 0.0 collective-permute-done.1
  21.8 0.4 %kernel_terms.1 = f32[16,8,128]{2,1,0:T(8,128)S(1)} custom-call(s32[1]{0:T(128)} %bitcast.core, bf16[64,1024]{1,0:T(8,128)(2,1)S(1)} %precondition.1.precond, bf16[128,1024]{1,0:T(8,128)(2,1)S(1)} %bitcast.45), custom_call_target="tpu_custom_call" | custom-call | flops 33554432 | bytes 65536 | tf_op jit(solution)/shard_map/kernel_terms/pallas_call | solution.py:240
  22.2 9.0 %all_to_all.11 = f32[16,8,128]{2,1,0:T(8,128)S(1)} all-to-all(f32[16,8,128]{2,1,0:T(8,128)S(1)} %kernel_terms.1), channel_id=1, replica_groups={{2,3,0,1,6,7,4,5,10,11,8,9,14,15,12,13},{18,19,16,17,22,23,20,21,26,27,..., dimensions={0} | all-to-all | bytes 131072 | tf_op jit(solution)/shard_map/all_to_all | solution.py:22
  31.3 0.1 fusion.8
  31.4 0.6 %pad_maximum_fusion = f32[32,32]{1,0:T(8,128)} fusion(f32[8,32]{1,0:T(8,128)S(1)} %get-tuple-element.14, f32[8,32]{1,0:T(8,128)S(1)} %get-tuple-element.15, f32[8,32]{1,0:T(8,128)S(1)} %get-tuple-element.16, f32[8,32]{1,0:T(8,128)S(1)} %get-tuple-element.13), kind=kLoop, calls=%fused_computation.17 | loop fusion | flops 3072 | bytes 8192 | tf_op jit(solution)/shard_map/concatenate | solution.py:294
  (11 shorter events, 0.1 us)
Async XLA Ops:
  0.0 5.0 %collective-permute-start = (bf16[1024,1024]{1,0:T(8,128)(2,1)}, bf16[1024,1024]{1,0:T(8,128)(2,1)S(1)}, u32[]{:S(2)}, u32[]{:S(2)}) collective-permute-start(bf16[1024,1024]{1,0:T(8,128)(2,1)} %own.1), channel_id=1, source_target_pairs={{0,4},{4,0},{1,5},{5,1},{2,6},{6,2},{3,7},{7,3},{8,12},{12,8},{9,1... | collective-permute-start | bytes 6291464 | tf_op jit(solution)/shard_map/ppermute | solution.py:30
  19.5 2.3 %collective-permute-start.1 = (bf16[64,1024]{1,0:T(8,128)(2,1)S(1)}, bf16[64,1024]{1,0:T(8,128)(2,1)S(1)}, u32[]{:S(2)}, u32[]{:S(2)}) collective-permute-start(bf16[64,1024]{1,0:T(8,128)(2,1)S(1)} %slice.60), channel_id=1, source_target_pairs={{0,4},{4,0},{1,5},{5,1},{2,6},{6,2},{3,7},{7,3},{8,12},{12,8},{9,1... | collective-permute-start | bytes 393224 | tf_op jit(solution)/shard_map/ppermute | solution.py:30
  19.6 1.6 %copy-start = (bf16[1024,1024]{1,0:T(8,128)(2,1)S(1)}, bf16[1024,1024]{1,0:T(8,128)(2,1)}, u32[]{:S(2)}) copy-start(bf16[1024,1024]{1,0:T(8,128)(2,1)} %own.1) | copy-start | bytes 6291460
